TPU v7x, 128 devices: a whole 4x4x4 slice. The times are simulated.
128 devices in a mesh: dp: 32 (over y, z, core), tensor: 4 (over x).
Axes of the slice: x: 4, y: 4, z: 4, core: 2. Of those that a mesh axis runs over, the one named last changes fastest.
Arguments:
- tokens: bfloat16 [32768, 1536], P(('dp', 'tensor')), may hold values from -6 to 6
- norm_gains: float32 [2, 1536], replicated, may hold values from 0.5 to 1.5
- query_matrix: bfloat16 [1536, 1536], P(None, 'tensor'), may hold values from -0.15625 to 0.15625
- key_value_weight: bfloat16 [1536, 2, 512], P(None, None, 'tensor'), may hold values from -0.15625 to 0.15625
- output_weight: bfloat16 [1536, 1536], P('tensor'), may hold values from -0.625 to 0.625
- router: bfloat16 [32, 1536], replicated, may hold values from -0.078125 to 0.078125
- expert_up: bfloat16 [32, 1536, 1024], P('dp'), may hold values from -0.15625 to 0.15625
- expert_down: bfloat16 [32, 512, 1536], P('dp'), may hold values from -1 to 1
- routes: int32 [32768, 8], P(('dp', 'tensor')), may hold values from 0 to 31, all different within a row; in each aligned block of 256 rows (0 to 255, 256 to 511, ...) at most 68 rows name the same one
- cotangent: bfloat16 [32768, 1536], P(('dp', 'tensor')), may hold values from -6 to 6
Outputs:
- layer_out: bfloat16 [32768, 1536], P(('dp', 'tensor'))
- tokens_grad: float32 [32768, 1536], P(('dp', 'tensor'))
- gains_grad: float32 [2, 1536], P(None, ('dp', 'tensor'))
- query_weight_grad: float32 [1536, 1536], P('dp', 'tensor')
- keyval_weight_grad: float32 [1536, 2, 512], P('dp', None, 'tensor')
- output_weight_grad: float32 [1536, 1536], P('tensor', 'dp')
- router_grad: float32 [32, 1536], P(None, ('dp', 'tensor'))
- expert_up_grad: float32 [32, 1536, 1024], P('dp', 'tensor')
- expert_down_grad: float32 [32, 512, 1536], P('dp', None, 'tensor')
Inputs may be any that keep to these rules, and one draw needn't show every extreme that they name: `routes`: each row names 8 different experts; in each aligned block of 256 rows (one device's tokens) no expert is named by more than 68 rows, a bound that some block reaches.
All inputs are finite; a program needn't handle non-finite values.
Results may differ from a plain program's by a relative error of at most 0.025.
Values may be sent and summed in bfloat16 or wider, within the bound.
No kernel may reach another device: no remote copies, remote signals or barrier semaphores. Data moves between devices by JAX's collectives and lax.ppermute only.
A program may use at most 192 MiB of HBM per device.

v0:
```python
import jax
import jax.numpy as jnp
from jax import lax
from jax.sharding import PartitionSpec as P

QUERY_HEADS = 24
KEY_VALUE_HEADS = 8
HEAD_DIM = 64
FF = 512
CAP = 68


epsilon = 1e-06
theta = 10000.0
highest = lax.Precision.HIGHEST


def norm_rows(values, gain_row):
    inv_rms = lax.rsqrt(jnp.mean(values * values, axis=-1, keepdims=True) + epsilon)
    return (values * inv_rms * gain_row, inv_rms)


def norm_back(values, inv_rms, gain_row, upstream):
    scaled = upstream * gain_row
    inner_sum = jnp.mean(scaled * values, axis=-1, keepdims=True)
    values_grad = inv_rms * scaled - values * (inv_rms * inv_rms * inv_rms) * inner_sum
    return (values_grad, jnp.sum(upstream * values * inv_rms, axis=0))


def rotary_tables(sequence_length, head_width):
    half_width = head_width // 2
    freqs = theta ** (-(jnp.arange(half_width).astype(jnp.float32) * 2.0 / head_width))
    angles = jnp.arange(sequence_length).astype(jnp.float32)[:, None] * freqs[None, :]
    return (jnp.cos(angles), jnp.sin(angles))


def apply_rotary(values, cosine_table, sine_table, direction):
    half_width = values.shape[-1] // 2
    first_half = values[..., :half_width]
    second_half = values[..., half_width:]
    cos_rows = cosine_table[:, None, :]
    sin_rows = sine_table[:, None, :] * direction
    return jnp.concatenate(
        [
            first_half * cos_rows - second_half * sin_rows,
            second_half * cos_rows + first_half * sin_rows,
        ],
        axis=-1,
    )


def per_device(
    tokens,
    norm_gains,
    query_matrix,
    key_value_weight,
    output_weight,
    router,
    expert_up,
    expert_down,
    routes,
    cotangent,
):
    local_rows, model_width = tokens.shape
    query_width = query_matrix.shape[1]
    keyval_width = key_value_weight.shape[2]
    head_width = HEAD_DIM
    group_width = QUERY_HEADS // KEY_VALUE_HEADS
    kv_heads = keyval_width // head_width
    local_heads = query_width // head_width
    experts_all = router.shape[0]
    top_count = routes.shape[1]
    inputs = tokens.astype(jnp.float32)
    normed, inv_rms_one = norm_rows(inputs, norm_gains[0])
    sequence = lax.all_gather(normed.astype(jnp.bfloat16), "tensor", axis=0, tiled=True)
    sequence_length = sequence.shape[0]
    joined_weight = jnp.concatenate(
        [query_matrix, key_value_weight.reshape(model_width, 2 * keyval_width)], axis=1
    )
    projected_rows = jnp.dot(sequence, joined_weight, preferred_element_type=jnp.float32)
    cosine_table, sine_table = rotary_tables(sequence_length, head_width)
    query_rows = apply_rotary(
        projected_rows[:, :query_width].reshape(sequence_length, local_heads, head_width),
        cosine_table,
        sine_table,
        1.0,
    ).astype(jnp.bfloat16)
    keys_low = apply_rotary(
        projected_rows[:, query_width : query_width + keyval_width].reshape(
            sequence_length, kv_heads, head_width
        ),
        cosine_table,
        sine_table,
        1.0,
    ).astype(jnp.bfloat16)
    values_low = (
        projected_rows[:, query_width + keyval_width :]
        .reshape(sequence_length, kv_heads, head_width)
        .astype(jnp.bfloat16)
    )
    rows_per_block = min(512, sequence_length)
    block_count = sequence_length // rows_per_block
    query_block_list = query_rows.reshape(
        block_count, rows_per_block, kv_heads, group_width, head_width
    )
    block_starts = jnp.arange(block_count, dtype=jnp.int32) * rows_per_block
    key_index = jnp.arange(sequence_length, dtype=jnp.int32)
    factor = head_width ** (-0.5)

    def masked_scores(query_piece, row_start):
        raw_scores = (
            jnp.einsum("qhgd,shd->hgqs", query_piece, keys_low, preferred_element_type=jnp.float32)
            * factor
        )
        row_index = row_start + jnp.arange(rows_per_block, dtype=jnp.int32)
        return jnp.where(row_index[:, None] >= key_index[None, :], raw_scores, -1e30)

    def forward_block(operands):
        query_piece, row_start = operands
        scores = masked_scores(query_piece, row_start)
        row_max = jnp.max(scores, axis=-1, keepdims=True)
        exp_scores = jnp.exp(scores - row_max)
        row_total = jnp.sum(exp_scores, axis=-1, keepdims=True)
        attn_probs = (exp_scores / row_total).astype(jnp.bfloat16)
        attended_piece = jnp.einsum(
            "hgqs,shd->qhgd", attn_probs, values_low, preferred_element_type=jnp.float32
        )
        return (attended_piece.astype(jnp.bfloat16), row_max + jnp.log(row_total))

    attended_blocks, log_totals = lax.map(forward_block, (query_block_list, block_starts))
    attended = attended_blocks.reshape(sequence_length, query_width)
    attn_sum = lax.psum_scatter(
        jnp.dot(attended, output_weight, preferred_element_type=jnp.float32).astype(jnp.bfloat16),
        "tensor",
        scatter_dimension=0,
        tiled=True,
    ).astype(jnp.float32)
    middle = inputs + attn_sum
    mixed_norm, inv_rms_two = norm_rows(middle, norm_gains[1])
    mixed_low = mixed_norm.astype(jnp.bfloat16)
    logits = jnp.einsum("td,ed->te", mixed_low, router, preferred_element_type=jnp.float32)
    expert_index = jnp.arange(experts_all, dtype=jnp.int32)
    pick_table = routes[:, :, None] == expert_index[None, None, :]
    chosen = jnp.sum(jnp.where(pick_table, logits[:, None, :], 0.0), axis=2)
    chosen_exp = jnp.exp(chosen - jnp.max(chosen, axis=1, keepdims=True))
    gate_weights = chosen_exp / jnp.sum(chosen_exp, axis=1, keepdims=True)
    flat_routes = routes.reshape(-1)
    flat_picks = pick_table.reshape(-1, experts_all)
    pick_counts = jnp.cumsum(flat_picks.astype(jnp.int32), axis=0)
    slot_index = jnp.sum(jnp.where(flat_picks, pick_counts - 1, 0), axis=1)
    token_index = jnp.arange(local_rows * top_count, dtype=jnp.int32) // top_count
    send_rows = (
        jnp.zeros((CAP, experts_all, model_width), jnp.bfloat16)
        .at[slot_index, flat_routes]
        .set(mixed_low[token_index])
    )
    received = lax.all_to_all(send_rows, "dp", split_axis=1, concat_axis=0, tiled=True)
    gate_up = jnp.einsum("rld,ldf->rlf", received, expert_up, preferred_element_type=jnp.float32)
    gate_part = gate_up[..., :FF]
    up_part = gate_up[..., FF:]
    sigmoid_gate = jax.nn.sigmoid(gate_part)
    hidden = (gate_part * sigmoid_gate * up_part).astype(jnp.bfloat16)
    expert_result = jnp.einsum(
        "rlf,lfd->rld", hidden, expert_down, preferred_element_type=jnp.float32
    ).astype(jnp.bfloat16)
    returned = lax.all_to_all(expert_result, "dp", split_axis=0, concat_axis=1, tiled=True)
    pair_result = (
        returned[slot_index, flat_routes]
        .reshape(local_rows, top_count, model_width)
        .astype(jnp.float32)
    )
    moe_sum = jnp.sum(gate_weights[:, :, None] * pair_result, axis=1)
    layer_out = (middle + moe_sum).astype(jnp.bfloat16)
    grad_out = cotangent.astype(jnp.float32)
    grad_gate = jnp.sum(grad_out[:, None, :] * pair_result, axis=2)
    grad_chosen = gate_weights * (
        grad_gate - jnp.sum(gate_weights * grad_gate, axis=1, keepdims=True)
    )
    grad_logits = jnp.sum(jnp.where(pick_table, grad_chosen[:, :, None], 0.0), axis=1)
    grad_pairs = (
        (gate_weights[:, :, None] * grad_out[:, None, :])
        .astype(jnp.bfloat16)
        .reshape(-1, model_width)
    )
    grad_send = jnp.zeros_like(send_rows).at[slot_index, flat_routes].set(grad_pairs)
    grad_received, rows_again = (
        lax.all_to_all(grad_send, "dp", split_axis=1, concat_axis=0, tiled=True),
        lax.all_to_all(send_rows, "dp", split_axis=1, concat_axis=0, tiled=True),
    )
    down_grad = jnp.einsum(
        "rld,rlf->ldf", grad_received, hidden, preferred_element_type=jnp.float32
    )
    grad_hidden = jnp.einsum(
        "rld,lfd->rlf", grad_received, expert_down, preferred_element_type=jnp.float32
    )
    grad_gate_part = grad_hidden * up_part * sigmoid_gate * (1.0 + gate_part * (1.0 - sigmoid_gate))
    grad_up_part = grad_hidden * gate_part * sigmoid_gate
    grad_gate_up = jnp.concatenate([grad_gate_part, grad_up_part], axis=-1).astype(jnp.bfloat16)
    up_grad = jnp.einsum(
        "rld,rlf->ldf", rows_again, grad_gate_up, preferred_element_type=jnp.float32
    )
    grad_rows = jnp.einsum(
        "rlf,ldf->rld", grad_gate_up, expert_up, preferred_element_type=jnp.float32
    ).astype(jnp.bfloat16)
    grad_returned = lax.all_to_all(grad_rows, "dp", split_axis=0, concat_axis=1, tiled=True)
    grad_mixed = jnp.sum(
        grad_returned[slot_index, flat_routes]
        .reshape(local_rows, top_count, model_width)
        .astype(jnp.float32),
        axis=1,
    )
    grad_mixed = grad_mixed + jnp.dot(grad_logits, router.astype(jnp.float32), precision=highest)
    router_part = jnp.einsum(
        "te,td->ed", grad_logits, mixed_low.astype(jnp.float32), precision=highest
    )
    grad_norm_two, gain_two_grad = norm_back(middle, inv_rms_two, norm_gains[1], grad_mixed)
    grad_middle = grad_out + grad_norm_two
    grad_attn_seq = lax.all_gather(grad_middle.astype(jnp.bfloat16), "tensor", axis=0, tiled=True)
    output_grad_turned = jnp.einsum(
        "sd,sq->dq", grad_attn_seq, attended, preferred_element_type=jnp.float32
    )
    grad_attended = jnp.einsum(
        "sd,qd->sq", grad_attn_seq, output_weight, preferred_element_type=jnp.float32
    ).astype(jnp.bfloat16)
    grad_blocks = grad_attended.reshape(
        block_count, rows_per_block, kv_heads, group_width, head_width
    )

    def backward_block(totals, operands):
        key_total, value_total = totals
        query_piece, grad_piece, row_start, log_total = operands
        attn_probs = jnp.exp(masked_scores(query_piece, row_start) - log_total)
        value_total = value_total + jnp.einsum(
            "hgqs,qhgd->shd",
            attn_probs.astype(jnp.bfloat16),
            grad_piece,
            preferred_element_type=jnp.float32,
        )
        grad_probs = jnp.einsum(
            "qhgd,shd->hgqs", grad_piece, values_low, preferred_element_type=jnp.float32
        )
        row_inner = jnp.sum(attn_probs * grad_probs, axis=-1, keepdims=True)
        grad_scores = (attn_probs * (grad_probs - row_inner)).astype(jnp.bfloat16)
        query_grad = (
            jnp.einsum("hgqs,shd->qhgd", grad_scores, keys_low, preferred_element_type=jnp.float32)
            * factor
        )
        key_total = (
            key_total
            + jnp.einsum(
                "hgqs,qhgd->shd", grad_scores, query_piece, preferred_element_type=jnp.float32
            )
            * factor
        )
        return ((key_total, value_total), query_grad)

    zero_keys = jnp.zeros((sequence_length, kv_heads, head_width), jnp.float32)
    (key_grad, value_grad), query_grads = lax.scan(
        backward_block,
        (zero_keys, zero_keys),
        (query_block_list, grad_blocks, block_starts, log_totals),
    )
    query_grad_back = apply_rotary(
        query_grads.reshape(sequence_length, local_heads, head_width),
        cosine_table,
        sine_table,
        -1.0,
    )
    key_grad_back = apply_rotary(key_grad, cosine_table, sine_table, -1.0)
    grad_projected = jnp.concatenate(
        [
            query_grad_back.reshape(sequence_length, query_width),
            key_grad_back.reshape(sequence_length, keyval_width),
            value_grad.reshape(sequence_length, keyval_width),
        ],
        axis=1,
    ).astype(jnp.bfloat16)
    joined_grad = jnp.einsum(
        "sd,sf->df", sequence, grad_projected, preferred_element_type=jnp.float32
    )
    grad_normed = lax.psum_scatter(
        jnp.einsum(
            "sf,df->sd", grad_projected, joined_weight, preferred_element_type=jnp.float32
        ).astype(jnp.bfloat16),
        "tensor",
        scatter_dimension=0,
        tiled=True,
    ).astype(jnp.float32)
    grad_norm_one, gain_one_grad = norm_back(inputs, inv_rms_one, norm_gains[0], grad_normed)
    tokens_grad = grad_middle + grad_norm_one
    joined_part, output_part = (
        lax.psum_scatter(
            joined_grad.astype(jnp.bfloat16), "dp", scatter_dimension=0, tiled=True
        ).astype(jnp.float32),
        lax.psum_scatter(
            output_grad_turned.astype(jnp.bfloat16), "dp", scatter_dimension=0, tiled=True
        ).astype(jnp.float32),
    )
    query_weight_grad = joined_part[:, :query_width]
    keyval_weight_grad = joined_part[:, query_width:].reshape(-1, 2, keyval_width)
    output_weight_grad = output_part.T
    expert_up_grad, down_part = (
        lax.psum_scatter(
            up_grad.astype(jnp.bfloat16), "tensor", scatter_dimension=1, tiled=True
        ).astype(jnp.float32),
        lax.psum_scatter(
            down_grad.astype(jnp.bfloat16), "tensor", scatter_dimension=1, tiled=True
        ).astype(jnp.float32),
    )
    expert_down_grad = jnp.swapaxes(down_part, 1, 2)
    router_grad, gains_grad = (
        lax.psum_scatter(router_part, ("dp", "tensor"), scatter_dimension=1, tiled=True),
        lax.psum_scatter(
            jnp.stack([gain_one_grad, gain_two_grad]),
            ("dp", "tensor"),
            scatter_dimension=1,
            tiled=True,
        ),
    )
    return (
        layer_out,
        tokens_grad,
        gains_grad,
        query_weight_grad,
        keyval_weight_grad,
        output_weight_grad,
        router_grad,
        expert_up_grad,
        expert_down_grad,
    )


def solution(mesh):
    placed = (
        P(("dp", "tensor"), None),
        P(),
        P(None, "tensor"),
        P(None, None, "tensor"),
        P("tensor", None),
        P(),
        P("dp", None, None),
        P("dp", None, None),
        P(("dp", "tensor"), None),
        P(("dp", "tensor"), None),
    )
    return jax.shard_map(
        per_device,
        mesh=mesh,
        in_specs=placed,
        out_specs=(
            P(("dp", "tensor"), None),
            P(("dp", "tensor"), None),
            P(None, ("dp", "tensor")),
            P("dp", "tensor"),
            P("dp", None, "tensor"),
            P("tensor", "dp"),
            P(None, ("dp", "tensor")),
            P("dp", "tensor", None),
            P("dp", None, "tensor"),
        ),
        check_vma=False,
    )
```

profile of v0, /device:TPU:1, one launch (start us, length us, event | category | flops | bytes accessed | tf_op | source)
XLA Modules:
  0.0 1701.3 jit_solution(5919732856706622959)
XLA Ops:
  18.0 38.0 %all-gather.3.cloned.1.call-done = bf16[1024,1536]{1,0:T(8,128)(2,1)} async-done(((bf16[256,1536]{1,0:T(8,128)(2,1)}), bf16[1024,1536]{1,0:T(8,128)(2,1)}) %all-gather.3.cloned.1.call-update) | async-done | bytes 3145744 | tf_op jit(solution)/shard_map/all_gather | solution.py:75
  71.7 29.4 %while.28 = (s32[]{:T(128)}, bf16[2,512,2,3,64]{1,4,3,2,0:T(8,128)(2,1)}, f32[2,2,3,512,1]{3,2,1,4,0:T(4,128)}, s32[2]{0:T(128)S(1)}, bf16[2,512,2,3,64]{1,4,3,2...) while((s32[]{:T(128)}, ...), condition=%wide.region_4.5_spmd.clone, body=%wide.region_1.4_spmd.clone.sunk | while | flops 843773440 | bytes 48816388 | solution.py:130
  109.6 15.9 reduce-window.6
  132.1 14.3 reduce-scatter.10.cloned.1.call-done
  153.1 15.0 scatter_custom_fusion.1
  185.6 37.5 %scatter_custom_fusion = bf16[2176,1536]{1,0:T(8,128)(2,1)} fusion(s32[2048]{0:T(1024)S(1)} %get-tuple-element.387, bf16[256,1536]{1,0:T(8,128)(2,1)} %copy-done.12, s32[2048]{0:T(1024)S(1)} %get-tuple-element.386, bf16[]{:T(256)} %constant.52.clone.1), kind=kCustom, calls=%fused_computation.83 | custom fusion | bytes 6685184
  232.7 40.5 %all-to-all-done.2 = bf16[68,32,1536]{2,0,1:T(8,128)(2,1)} async-done(((bf16[68,32,1536]{2,0,1:T(8,128)(2,1)}), bf16[68,32,1536]{2,0,1:T(8,128)(2,1)}, u32[]{:S(2)}, u32[]{:S(2)}) %all-to-all-start.2) | async-done | bytes 6684704 | tf_op jit(solution)/shard_map/all_to_all | solution.py:187
  273.2 24.2 %all-to-all-start = ((bf16[68,32,1536]{2,0,1:T(8,128)(2,1)}), bf16[68,32,1536]{2,0,1:T(8,128)(2,1)}, u32[]{:S(2)}, u32[]{:S(2)}) async-start(bf16[68,32,1536]{2,0,1:T(8,128)(2,1)} %copy.107), calls=%async_computation.1 | async-start | bytes 14155776 | tf_op jit(solution)/shard_map/all_to_all | solution.py:157
  305.8 79.1 %all-to-all-done = bf16[68,32,1536]{2,0,1:T(8,128)(2,1)} async-done(((bf16[68,32,1536]{2,0,1:T(8,128)(2,1)}), bf16[68,32,1536]{2,0,1:T(8,128)(2,1)}, u32[]{:S(2)}, u32[]{:S(2)}) %all-to-all-start) | async-done | bytes 6684704 | tf_op jit(solution)/shard_map/all_to_all | solution.py:157
  442.8 24.1 %all-to-all-start.3 = ((bf16[32,2,52224]{2,1,0:T(2,128)(2,1)}), bf16[32,2,52224]{2,1,0:T(2,128)(2,1)}, u32[]{:S(2)}, u32[]{:S(2)}) async-start(bf16[32,2,52224]{2,1,0:T(2,128)(2,1)} %reshape.560), calls=%async_computation.4 | async-start | bytes 13369344 | tf_op jit(solution)/shard_map/all_to_all | solution.py:205
  495.6 54.0 %all-to-all-done.3 = bf16[32,2,52224]{2,1,0:T(2,128)(2,1)} async-done(((bf16[32,2,52224]{2,1,0:T(2,128)(2,1)}), bf16[32,2,52224]{2,1,0:T(2,128)(2,1)}, u32[]{:S(2)}, u32[]{:S(2)}) %all-to-all-start.3) | async-done | bytes 6684704 | tf_op jit(solution)/shard_map/all_to_all | solution.py:205
  549.6 22.1 %all-to-all-start.1 = ((bf16[32,2,52224]{2,1,0:T(2,128)(2,1)}), bf16[32,2,52224]{2,1,0:T(2,128)(2,1)}, u32[]{:S(2)}, u32[]{:S(2)}) async-start(bf16[32,2,52224]{2,1,0:T(2,128)(2,1)} %reshape.562), calls=%async_computation.2 | async-start | bytes 13369344 | tf_op jit(solution)/shard_map/all_to_all | solution.py:166
  571.8 21.5 %reshape.561 = bf16[2176,1,1536]{2,1,0:T(2,128)(2,1)} reshape(bf16[32,2,52224]{2,1,0:T(2,128)(2,1)} %all-to-all-done.3) | data formatting | bytes 13369344
  593.3 141.9 %reduce.11 = bf16[2176,1536]{1,0:T(8,128)(2,1)} reduce(bf16[2176,1,1536]{2,1,0:T(2,128)(2,1)} %reshape.561, bf16[]{:T(256)} %constant.151), dimensions={1}, to_apply=%all_to_all.63.reduce_sub_computation | reduce | bytes 13369346 | tf_op jit(solution)/shard_map/all_to_all | solution.py:205
  751.6 46.4 %gather_fusion.1 = bf16[2048,1536]{1,0:T(8,128)(2,1)} fusion(bf16[68,32,1536]{2,1,0:T(8,128)(2,1)} %bitcast.335, s32[2048]{0:T(1024)S(1)} %bitcast.333), kind=kCustom, calls=%fused_computation.2 | custom fusion | bytes 12599296 | tf_op jit(solution)/shard_map/gather | solution.py:207
  806.1 21.5 %reshape.563 = bf16[2176,1,1536]{2,1,0:T(2,128)(2,1)} reshape(bf16[32,2,52224]{2,1,0:T(2,128)(2,1)} %all-to-all-done.1) | data formatting | bytes 13369344
  827.6 141.7 %reduce.10 = bf16[2176,1536]{1,0:T(8,128)(2,1)} reduce(bf16[2176,1,1536]{2,1,0:T(2,128)(2,1)} %reshape.563, bf16[]{:T(256)} %constant.151), dimensions={1}, to_apply=%all_to_all.56.reduce_sub_computation | reduce | bytes 13369346 | tf_op jit(solution)/shard_map/all_to_all | solution.py:166
  985.9 46.0 %gather_fusion = bf16[2048,1536]{1,0:T(8,128)(2,1)} fusion(bf16[68,32,1536]{2,1,0:T(8,128)(2,1)} %bitcast.336, s32[2048]{0:T(1024)S(1)} %bitcast.334), kind=kCustom, calls=%fused_computation.1 | custom fusion | bytes 12599296 | tf_op jit(solution)/shard_map/gather | solution.py:168
  1070.1 17.4 %all-gather.5.cloned.1.call-done = bf16[1024,1536]{1,0:T(8,128)(2,1)} async-done(((bf16[256,1536]{1,0:T(8,128)(2,1)}), bf16[1024,1536]{1,0:T(8,128)(2,1)}) %all-gather.5.cloned.1.call-update) | async-done | bytes 3145744 | tf_op jit(solution)/shard_map/all_gather | solution.py:218
  1098.6 85.3 %while.29 = (s32[]{:T(128)}, f32[1024,2,64]{0,2,1:T(8,128)S(1)}, f32[1024,2,64]{0,2,1:T(8,128)}, f32[2,512,2,3,64]{1,0,4,3,2:T(2,128)}, bf16[2,512,2,3,64]{1,4,3...) while((s32[]{:T(128)}, f32[1024,2,64]{0,2,1:T(8,128)S(1)}, ...), condition=%wide.region_23.24_spmd.clone, body=%wide.region_21.23_spmd.clone.sunk | while | flops 2061825536 | bytes 104947896 | solution.py:258
  1126.3 15.0 dynamic_update_slice.22
  1168.9 15.0 dynamic_update_slice.22
  1200.5 316.8 %fusion.4 = f32[32,16]{0,1:T(8,128)S(1)} fusion(f32[32,1536]{0,1:T(8,128)S(1)} %fusion.103), kind=kCustom, calls=%all-reduce-scatter | all-reduce-scatter fusion | flops 65537 | bytes 198656
  1623.5 64.7 %all-reduce = f32[2,1536]{1,0:T(2,128)S(1)} all-reduce(f32[2,1536]{1,0:T(2,128)S(1)} %pad_maximum_fusion.10), channel_id=4, replica_groups=mesh['dp'=32,'tensor'=4] {'dp','tensor'}, use_global_device_ids=true, to_apply=%region_28.29.clone | all-reduce | flops 3072 | bytes 24576
  (377 shorter events, 471.8 us)
Async XLA Ops:
  7.2 48.8 %all-gather.3.cloned.1.call-start = ((), (), s32[]{:S(2)}) async-start(), calls=%async_computation.10 | async-start | bytes 3932160 | tf_op jit(solution)/shard_map/all_gather | solution.py:75
  13.1 133.4 %reduce-scatter.10.cloned.1.call-start = ((), (), s32[]{:S(2)}) async-start(), calls=%async_computation.11 | async-start | bytes 3932160 | tf_op jit(solution)/shard_map/reduce_scatter | solution.py:132
  177.5 95.6 %all-to-all-start.2 = ((bf16[68,32,1536]{2,0,1:T(8,128)(2,1)}), bf16[68,32,1536]{2,0,1:T(8,128)(2,1)}, u32[]{:S(2)}, u32[]{:S(2)}) async-start(bf16[68,32,1536]{2,0,1:T(8,128)(2,1)} %copy.111), calls=%async_computation.3 | async-start | bytes 14155776 | tf_op jit(solution)/shard_map/all_to_all | solution.py:187
  273.2 111.8 %all-to-all-start = ((bf16[68,32,1536]{2,0,1:T(8,128)(2,1)}), bf16[68,32,1536]{2,0,1:T(8,128)(2,1)}, u32[]{:S(2)}, u32[]{:S(2)}) async-start(bf16[68,32,1536]{2,0,1:T(8,128)(2,1)} %copy.107), calls=%async_computation.1 | async-start | bytes 14155776 | tf_op jit(solution)/shard_map/all_to_all | solution.py:157
  442.8 106.8 %all-to-all-start.3 = ((bf16[32,2,52224]{2,1,0:T(2,128)(2,1)}), bf16[32,2,52224]{2,1,0:T(2,128)(2,1)}, u32[]{:S(2)}, u32[]{:S(2)}) async-start(bf16[32,2,52224]{2,1,0:T(2,128)(2,1)} %reshape.560), calls=%async_computation.4 | async-start | bytes 13369344 | tf_op jit(solution)/shard_map/all_to_all | solution.py:205
  549.6 256.5 %all-to-all-start.1 = ((bf16[32,2,52224]{2,1,0:T(2,128)(2,1)}), bf16[32,2,52224]{2,1,0:T(2,128)(2,1)}, u32[]{:S(2)}, u32[]{:S(2)}) async-start(bf16[32,2,52224]{2,1,0:T(2,128)(2,1)} %reshape.562), calls=%async_computation.2 | async-start | bytes 13369344 | tf_op jit(solution)/shard_map/all_to_all | solution.py:166
  571.7 515.8 %all-gather.5.cloned.1.call-start = ((), (), s32[]{:S(2)}) async-start(), calls=%async_computation.12 | async-start | bytes 3932160 | tf_op jit(solution)/shard_map/all_gather | solution.py:218
  1048.4 560.3 %reduce-scatter.20.cloned.1.call-start = ((), (), s32[]{:S(2)}) async-start(), calls=%async_computation.17 | async-start | bytes 1966080 | tf_op jit(solution)/shard_map/reduce_scatter | solution.py:306
  1057.0 553.9 %reduce-scatter.18.cloned.1.call-start = ((), (), s32[]{:S(2)}) async-start(), calls=%async_computation.16 | async-start | bytes 3932160 | tf_op jit(solution)/shard_map/reduce_scatter | solution.py:303
  1070.0 547.6 %reduce-scatter.16.cloned.1.call-start = ((), (), s32[]{:S(2)}) async-start(), calls=%async_computation.15 | async-start | bytes 1216512 | tf_op jit(solution)/shard_map/reduce_scatter | solution.py:295
  1098.5 520.6 %reduce-scatter.14.cloned.1.call-start = ((), (), s32[]{:S(2)}) async-start(), calls=%async_computation.14 | async-start | bytes 2027520 | tf_op jit(solution)/shard_map/reduce_scatter | solution.py:292
  1192.7 429.2 %reduce-scatter.12.cloned.1.call-start = ((), (), s32[]{:S(2)}) async-start(), calls=%async_computation.13 | async-start | bytes 3932160 | tf_op jit(solution)/shard_map/reduce_scatter | solution.py:281
  1517.3 15.9 collective-permute-start.30
  1520.0 14.5 collective-permute-start.29
  1521.3 14.5 collective-permute-start.28
  1533.2 18.3 %collective-permute-start.25 = (f32[32,16]{0,1:T(8,128)S(1)}, f32[32,16]{0,1:T(8,128)S(1)}, u32[]{:S(2)}, u32[]{:S(2)}) collective-permute-start(f32[32,16]{0,1:T(8,128)S(1)} %fusion.4), channel_id=1, source_target_pairs={{0,26},{1,27},{2,28},{3,29},{4,30},{5,31},{6,32},{7,33},{8,34},{9,... | collective-permute-start | bytes 6152
  1534.5 21.1 %collective-permute-start.24 = (f32[32,16]{0,1:T(8,128)S(1)}, f32[32,16]{0,1:T(8,128)S(1)}, u32[]{:S(2)}, u32[]{:S(2)}) collective-permute-start(f32[32,16]{0,1:T(8,128)S(1)} %fusion.4), channel_id=1, source_target_pairs={{0,25},{1,26},{2,27},{3,28},{4,29},{5,30},{6,31},{7,32},{8,33},{9,... | collective-permute-start | bytes 6152
  1535.8 21.7 %collective-permute-start.23 = (f32[32,16]{0,1:T(8,128)S(1)}, f32[32,16]{0,1:T(8,128)S(1)}, u32[]{:S(2)}, u32[]{:S(2)}) collective-permute-start(f32[32,16]{0,1:T(8,128)S(1)} %fusion.4), channel_id=1, source_target_pairs={{0,24},{1,25},{2,26},{3,27},{4,28},{5,29},{6,30},{7,31},{8,32},{9,... | collective-permute-start | bytes 6152
  1537.1 23.6 %collective-permute-start.22 = (f32[32,16]{0,1:T(8,128)S(1)}, f32[32,16]{0,1:T(8,128)S(1)}, u32[]{:S(2)}, u32[]{:S(2)}) collective-permute-start(f32[32,16]{0,1:T(8,128)S(1)} %fusion.4), channel_id=1, source_target_pairs={{0,23},{1,24},{2,25},{3,26},{4,27},{5,28},{6,29},{7,30},{8,31},{9,... | collective-permute-start | bytes 6152
  1538.5 24.2 %collective-permute-start.21 = (f32[32,16]{0,1:T(8,128)S(1)}, f32[32,16]{0,1:T(8,128)S(1)}, u32[]{:S(2)}, u32[]{:S(2)}) collective-permute-start(f32[32,16]{0,1:T(8,128)S(1)} %fusion.4), channel_id=1, source_target_pairs={{0,22},{1,23},{2,24},{3,25},{4,26},{5,27},{6,28},{7,29},{8,30},{9,... | collective-permute-start | bytes 6152
  1567.4 14.7 collective-permute-start.14
  1588.0 15.5 collective-permute-start.6
  1594.9 18.6 %collective-permute-start.4 = (f32[32,16]{0,1:T(8,128)S(1)}, f32[32,16]{0,1:T(8,128)S(1)}, u32[]{:S(2)}, u32[]{:S(2)}) collective-permute-start(f32[32,16]{0,1:T(8,128)S(1)} %fusion.4), channel_id=1, source_target_pairs={{0,5},{1,6},{2,7},{3,8},{4,9},{5,10},{6,11},{7,12},{8,13},{9,14},{... | collective-permute-start | bytes 6152
  1596.7 16.7 collective-permute-start.3
  (90 other events, 2356.1 us)
Sparse Core Ops, SparseCore 0:
  13.2 42.7 all-gather.2
  107.9 38.5 reduce-scatter.9
  1048.5 38.9 all-gather.4
  1089.7 24.8 reduce-scatter.19
  1116.9 39.0 reduce-scatter.17
  1159.4 74.3 reduce-scatter.15
  1237.3 76.4 reduce-scatter.13
  1316.4 39.9 reduce-scatter.11
where the time goes:
time: 1720 us; the launch traced here: 1700 us
  other arithmetic  412 us (24%)
  blocking collectives  381 us (22%)
  local copies, waits for them, and re-layouts  340 us (20%)
  waiting for transfers between devices  243 us (14%)
  starting transfers between devices  170 us (10%)
  matrix products  137 us (8%)
    unnamed x2, blocking collectives  381 us
    all_to_all x1, other arithmetic, per_device(): lax.all_to_all(grad_rows, 'dp', split_axis=0, concat_axis=1, tiled=True)  142 us
    all_to_all x1, other arithmetic, per_device(): lax.all_to_all(expert_result, 'dp', split_axis=0, concat_axis=1, tiled=True)  142 us
    unnamed x135, local copies, waits for them, and re-layouts  124 us
    unnamed x32, starting transfers between devices  90.8 us
    all_to_all x1, waiting for transfers between devices, per_device(): lax.all_to_all(send_rows, 'dp', split_axis=1, concat_axis=0, tiled=True)  79.1 us
    all_to_all x1, waiting for transfers between devices, per_device(): lax.all_to_all(grad_rows, 'dp', split_axis=0, concat_axis=1, tiled=True)  54 us
    gather x1, local copies, waits for them, and re-layouts, per_device(): grad_returned[slot_index, flat_routes]  46.4 us
  transfers between devices with their start and end apart: 44, of which 6 were waited for; matrix products, arithmetic and copies ran while one was open for 47% of the time, Pallas kernels for 0%

commit v1 on v0

v1 whole, which is shorter than its diff:
```python
import jax
import jax.numpy as jnp
from jax import lax
from jax.sharding import PartitionSpec as P

QUERY_HEADS = 24
KEY_VALUE_HEADS = 8
HEAD_DIM = 64
FF = 512
CAP = 68
ROWS = 72


epsilon = 1e-06
theta = 10000.0
highest = lax.Precision.HIGHEST
f32 = jnp.float32
bf16 = jnp.bfloat16


def dot(a, b, ca, cb, precision=None):
    return lax.dot_general(
        a, b, (((ca,), (cb,)), ((), ())), preferred_element_type=f32, precision=precision
    )


def norm_rows(values, gain_row):
    inv_rms = lax.rsqrt(jnp.mean(values * values, axis=-1, keepdims=True) + epsilon)
    return (values * inv_rms * gain_row, inv_rms)


def norm_back(values, inv_rms, gain_row, upstream):
    scaled = upstream * gain_row
    inner_sum = jnp.mean(scaled * values, axis=-1, keepdims=True)
    return inv_rms * scaled - values * (inv_rms * inv_rms * inv_rms) * inner_sum


def rotary_tables(sequence_length, head_width):
    half_width = head_width // 2
    freqs = theta ** (-(jnp.arange(half_width).astype(jnp.float32) * 2.0 / head_width))
    angles = jnp.arange(sequence_length).astype(jnp.float32)[:, None] * freqs[None, :]
    return (jnp.cos(angles), jnp.sin(angles))


def apply_rotary(values, cosine_table, sine_table, direction):
    half_width = values.shape[-1] // 2
    first_half = values[..., :half_width]
    second_half = values[..., half_width:]
    cos_rows = cosine_table[:, None, :]
    sin_rows = sine_table[:, None, :] * direction
    return jnp.concatenate(
        [
            first_half * cos_rows - second_half * sin_rows,
            second_half * cos_rows + first_half * sin_rows,
        ],
        axis=-1,
    )


def split_two(values):
    high = lax.reduce_precision(values, 8, 7)
    return high, values - high


def shift_tensor(values, step):
    return lax.ppermute(values, "tensor", [(i, (i + step) % 4) for i in range(4)])


def gather_tensor(mine, place):
    rows, width = mine.shape
    half = rows // 2
    left = shift_tensor(mine, 1)
    right = shift_tensor(mine, -1)
    far_top = shift_tensor(left[:half], 1)
    far_low = shift_tensor(right[half:], -1)
    whole = jnp.zeros((4 * rows, width), mine.dtype)
    for piece, owner, offset in (
        (mine, 0, 0),
        (left, 3, 0),
        (right, 1, 0),
        (far_top, 2, 0),
        (far_low, 2, half),
    ):
        start = lax.rem(place + owner, 4) * rows + offset
        whole = lax.dynamic_update_slice(whole, piece, (start, jnp.int32(0)))
    return whole


def scatter_tensor(chunk):
    far = chunk(2).astype(bf16)
    half = far.shape[0] // 2
    from_left = shift_tensor(far[:half], 1)
    from_right = shift_tensor(far[half:], -1)
    near_right = chunk(1)
    near_left = chunk(3)
    near_right = jnp.concatenate([near_right[:half] + from_left, near_right[half:]], axis=0)
    near_left = jnp.concatenate([near_left[:half], near_left[half:] + from_right], axis=0)
    one = shift_tensor(near_right.astype(bf16), 1)
    two = shift_tensor(near_left.astype(bf16), -1)
    return chunk(0) + one + two


def exchange(values):
    return lax.all_to_all(values, "dp", split_axis=0, concat_axis=0, tiled=True)


def per_device(
    tokens,
    norm_gains,
    query_matrix,
    key_value_weight,
    output_weight,
    router,
    expert_up,
    expert_down,
    routes,
    cotangent,
):
    local_rows, model_width = tokens.shape
    query_width = query_matrix.shape[1]
    keyval_width = key_value_weight.shape[2]
    head_width = HEAD_DIM
    group_width = QUERY_HEADS // KEY_VALUE_HEADS
    kv_heads = keyval_width // head_width
    local_heads = query_width // head_width
    experts_all = router.shape[0]
    place = lax.axis_index("tensor")
    group = lax.axis_index("dp")

    expert_index = jnp.arange(experts_all, dtype=jnp.int32)
    picked = jnp.any(routes[:, :, None] == expert_index[None, None, :], axis=1)
    token_index = jnp.arange(local_rows, dtype=jnp.int32)
    before = (token_index[:, None] > token_index[None, :]).astype(bf16)
    rank = dot(before, picked.astype(bf16), 1, 0)
    slot = jnp.where(picked, rank, -1.0)
    slot_turned = slot.T
    slot_index = jnp.arange(ROWS, dtype=jnp.int32).astype(f32)
    sending = slot_turned[:, None, :] == slot_index[None, :, None]
    send_matrix = sending.astype(bf16).reshape(experts_all * ROWS, local_rows)

    cot_send = dot(send_matrix, cotangent, 1, 0).astype(bf16)
    cot_rows = exchange(cot_send.reshape(experts_all, ROWS, model_width))
    cot_rows = cot_rows.reshape(experts_all * ROWS, model_width)

    inputs = tokens.astype(jnp.float32)
    normed, inv_rms_one = norm_rows(inputs, norm_gains[0])
    sequence = gather_tensor(normed.astype(jnp.bfloat16), place)
    sequence_length = sequence.shape[0]
    joined_weight = jnp.concatenate(
        [query_matrix, key_value_weight.reshape(model_width, 2 * keyval_width)], axis=1
    )
    projected_rows = jnp.dot(sequence, joined_weight, preferred_element_type=jnp.float32)
    cosine_table, sine_table = rotary_tables(sequence_length, head_width)
    query_rows = apply_rotary(
        projected_rows[:, :query_width].reshape(sequence_length, local_heads, head_width),
        cosine_table,
        sine_table,
        1.0,
    ).astype(jnp.bfloat16)
    keys_low = apply_rotary(
        projected_rows[:, query_width : query_width + keyval_width].reshape(
            sequence_length, kv_heads, head_width
        ),
        cosine_table,
        sine_table,
        1.0,
    ).astype(jnp.bfloat16)
    values_low = (
        projected_rows[:, query_width + keyval_width :]
        .reshape(sequence_length, kv_heads, head_width)
        .astype(jnp.bfloat16)
    )
    rows_per_block = min(512, sequence_length)
    block_count = sequence_length // rows_per_block
    query_block_list = query_rows.reshape(
        block_count, rows_per_block, kv_heads, group_width, head_width
    )
    block_starts = jnp.arange(block_count, dtype=jnp.int32) * rows_per_block
    key_index = jnp.arange(sequence_length, dtype=jnp.int32)
    factor = head_width ** (-0.5)

    def masked_scores(query_piece, row_start):
        raw_scores = (
            jnp.einsum("qhgd,shd->hgqs", query_piece, keys_low, preferred_element_type=jnp.float32)
            * factor
        )
        row_index = row_start + jnp.arange(rows_per_block, dtype=jnp.int32)
        return jnp.where(row_index[:, None] >= key_index[None, :], raw_scores, -1e30)

    def forward_block(operands):
        query_piece, row_start = operands
        scores = masked_scores(query_piece, row_start)
        row_max = jnp.max(scores, axis=-1, keepdims=True)
        exp_scores = jnp.exp(scores - row_max)
        row_total = jnp.sum(exp_scores, axis=-1, keepdims=True)
        attn_probs = (exp_scores / row_total).astype(jnp.bfloat16)
        attended_piece = jnp.einsum(
            "hgqs,shd->qhgd", attn_probs, values_low, preferred_element_type=jnp.float32
        )
        return (attended_piece.astype(jnp.bfloat16), row_max + jnp.log(row_total))

    attended_blocks, log_totals = lax.map(forward_block, (query_block_list, block_starts))
    attended = attended_blocks.reshape(sequence_length, query_width)

    def output_chunk(k):
        start = lax.rem(place + k, 4) * local_rows
        return dot(lax.dynamic_slice_in_dim(attended, start, local_rows, 0), output_weight, 1, 0)

    middle = inputs + scatter_tensor(output_chunk)
    mixed_norm, inv_rms_two = norm_rows(middle, norm_gains[1])
    mixed_low = mixed_norm.astype(jnp.bfloat16)
    logits = dot(mixed_low, router, 1, 1)
    chosen = jnp.where(picked, logits, -jnp.inf)
    chosen_exp = jnp.exp(chosen - jnp.max(chosen, axis=1, keepdims=True))
    gates = chosen_exp / jnp.sum(chosen_exp, axis=1, keepdims=True)

    spare = jnp.arange(ROWS, dtype=jnp.int32)[None, :, None]

    def with_spare(rows, slot_values):
        high, low = split_two(slot_values)
        wide = ((0, 0), (0, model_width - ROWS))
        high = jnp.pad(high, wide)[:, None, :]
        low = jnp.pad(low, wide)[:, None, :]
        rows = jnp.where(spare == CAP, high, rows)
        return jnp.where(spare == CAP + 1, low, rows).astype(bf16)

    def from_spare(rows):
        return rows[:, CAP, :ROWS].astype(f32) + rows[:, CAP + 1, :ROWS].astype(f32)

    gates_slot = jnp.sum(jnp.where(sending, gates.T[:, None, :], 0.0), axis=2)
    mixed_send = dot(send_matrix, mixed_low, 1, 0).reshape(experts_all, ROWS, model_width)
    received = exchange(with_spare(mixed_send, gates_slot))
    gate_column = from_spare(received).reshape(experts_all * ROWS, 1)
    rows_in = received.reshape(experts_all * ROWS, model_width)

    up_matrix, down_matrix = expert_up[0], expert_down[0]
    grad_hidden_one = dot(cot_rows, down_matrix, 1, 1)
    gate_up = dot(rows_in, up_matrix, 1, 0)
    gate_part = gate_up[:, :FF]
    up_part = gate_up[:, FF:]
    sigmoid_gate = jax.nn.sigmoid(gate_part)
    hidden = gate_part * sigmoid_gate * up_part
    hidden_gated = (gate_column * hidden).astype(bf16)
    grad_gate_slot = jnp.sum(hidden * grad_hidden_one, axis=1).reshape(experts_all, ROWS)
    grad_hidden = grad_hidden_one * gate_column
    grad_gate_part = grad_hidden * up_part * sigmoid_gate * (1.0 + gate_part * (1.0 - sigmoid_gate))
    grad_up_part = grad_hidden * gate_part * sigmoid_gate
    grad_gate_up = jnp.concatenate([grad_gate_part, grad_up_part], axis=-1).astype(jnp.bfloat16)
    grad_rows = dot(grad_gate_up, up_matrix, 1, 1).reshape(experts_all, ROWS, model_width)
    grad_back = exchange(with_spare(grad_rows, grad_gate_slot))

    expert_result = dot(hidden_gated, down_matrix, 1, 0).astype(bf16)
    result_back = exchange(expert_result.reshape(experts_all, ROWS, model_width))
    up_grad = dot(rows_in, grad_gate_up, 0, 0).astype(bf16)
    down_grad = dot(cot_rows, hidden_gated, 0, 0).astype(bf16)
    expert_up_grad = lax.psum_scatter(up_grad, "tensor", scatter_dimension=0, tiled=True)
    expert_down_grad = lax.psum_scatter(down_grad, "tensor", scatter_dimension=0, tiled=True)
    expert_up_grad = expert_up_grad.astype(f32)[None]
    expert_down_grad = expert_down_grad.astype(f32).T[None]

    grad_gate = jnp.sum(jnp.where(sending, from_spare(grad_back)[:, :, None], 0.0), axis=1).T
    grad_logits = gates * (grad_gate - jnp.sum(gates * grad_gate, axis=1, keepdims=True))
    grad_mixed = dot(send_matrix, grad_back.reshape(experts_all * ROWS, model_width), 0, 0)
    grad_mixed = grad_mixed + dot(grad_logits, router.astype(f32), 1, 0, highest)
    router_part = dot(mixed_low.astype(f32), grad_logits, 0, 0, highest)
    grad_out = cotangent.astype(jnp.float32)
    grad_middle = grad_out + norm_back(middle, inv_rms_two, norm_gains[1], grad_mixed)
    gain_two_part = jnp.sum(grad_mixed * middle * inv_rms_two, axis=0)

    grad_attn_seq = gather_tensor(grad_middle.astype(jnp.bfloat16), place)
    output_grad_turned = dot(grad_attn_seq, attended, 0, 0)
    router_high, router_low = split_two(router_part)
    gain_high, gain_low = split_two(gain_two_part)
    output_joined = jnp.concatenate(
        [
            output_grad_turned.astype(bf16),
            router_high.astype(bf16),
            router_low.astype(bf16),
            gain_high.astype(bf16)[:, None],
            gain_low.astype(bf16)[:, None],
            jnp.zeros((model_width, 62), bf16),
        ],
        axis=1,
    )
    dp_size = 32
    dp_rows = model_width // dp_size
    output_all = jnp.sum(
        exchange(output_joined.reshape(dp_size, dp_rows, query_width + 128)).astype(f32), axis=0
    )
    output_weight_grad = output_all[:, :query_width].T

    grad_attended = dot(grad_attn_seq, output_weight, 1, 1).astype(jnp.bfloat16)
    grad_blocks = grad_attended.reshape(
        block_count, rows_per_block, kv_heads, group_width, head_width
    )

    def backward_block(totals, operands):
        key_total, value_total = totals
        query_piece, grad_piece, row_start, log_total = operands
        attn_probs = jnp.exp(masked_scores(query_piece, row_start) - log_total)
        value_total = value_total + jnp.einsum(
            "hgqs,qhgd->shd",
            attn_probs.astype(jnp.bfloat16),
            grad_piece,
            preferred_element_type=jnp.float32,
        )
        grad_probs = jnp.einsum(
            "qhgd,shd->hgqs", grad_piece, values_low, preferred_element_type=jnp.float32
        )
        row_inner = jnp.sum(attn_probs * grad_probs, axis=-1, keepdims=True)
        grad_scores = (attn_probs * (grad_probs - row_inner)).astype(jnp.bfloat16)
        query_grad = (
            jnp.einsum("hgqs,shd->qhgd", grad_scores, keys_low, preferred_element_type=jnp.float32)
            * factor
        )
        key_total = (
            key_total
            + jnp.einsum(
                "hgqs,qhgd->shd", grad_scores, query_piece, preferred_element_type=jnp.float32
            )
            * factor
        )
        return ((key_total, value_total), query_grad)

    zero_keys = jnp.zeros((sequence_length, kv_heads, head_width), jnp.float32)
    (key_grad, value_grad), query_grads = lax.scan(
        backward_block,
        (zero_keys, zero_keys),
        (query_block_list, grad_blocks, block_starts, log_totals),
    )
    query_grad_back = apply_rotary(
        query_grads.reshape(sequence_length, local_heads, head_width),
        cosine_table,
        sine_table,
        -1.0,
    )
    key_grad_back = apply_rotary(key_grad, cosine_table, sine_table, -1.0)
    grad_projected = jnp.concatenate(
        [
            query_grad_back.reshape(sequence_length, query_width),
            key_grad_back.reshape(sequence_length, keyval_width),
            value_grad.reshape(sequence_length, keyval_width),
        ],
        axis=1,
    ).astype(jnp.bfloat16)
    joined_grad = dot(sequence, grad_projected, 0, 0).astype(bf16)
    joined_all = jnp.sum(
        exchange(joined_grad.reshape(dp_size, dp_rows, query_width + 2 * keyval_width)).astype(f32),
        axis=0,
    )
    query_weight_grad = joined_all[:, :query_width]
    keyval_weight_grad = joined_all[:, query_width:].reshape(dp_rows, 2, keyval_width)

    def normed_chunk(k):
        start = lax.rem(place + k, 4) * local_rows
        piece = lax.dynamic_slice_in_dim(grad_projected, start, local_rows, 0)
        return dot(piece, joined_weight, 1, 1)

    grad_normed = scatter_tensor(normed_chunk)
    tokens_grad = grad_middle + norm_back(inputs, inv_rms_one, norm_gains[0], grad_normed)

    weight_rows = lax.dynamic_slice_in_dim(joined_weight, group * dp_rows, dp_rows, 0)
    gain_rows = lax.dynamic_slice_in_dim(norm_gains[0], group * dp_rows, dp_rows, 0)
    gain_one_part = jnp.sum(weight_rows.astype(f32) * joined_all, axis=1) / gain_rows
    base = query_width
    small = jnp.concatenate(
        [
            output_all[:, base : base + 32] + output_all[:, base + 32 : base + 64],
            gain_one_part[:, None],
            (output_all[:, base + 64] + output_all[:, base + 65])[:, None],
            jnp.zeros((dp_rows, 94), f32),
        ],
        axis=1,
    ).reshape(4, dp_rows // 4, 128)
    small = jnp.pad(small, ((0, 0), (0, 4), (0, 0)))
    small = lax.all_to_all(small, "tensor", split_axis=0, concat_axis=0, tiled=True)
    small = jnp.sum(small, axis=0)[: dp_rows // 4].T
    router_grad = small[:experts_all]
    gains_grad = small[experts_all : experts_all + 2]

    moe_sum = dot(send_matrix, result_back.reshape(experts_all * ROWS, model_width), 0, 0)
    layer_out = (middle + moe_sum).astype(jnp.bfloat16)
    return (
        layer_out,
        tokens_grad,
        gains_grad,
        query_weight_grad,
        keyval_weight_grad,
        output_weight_grad,
        router_grad,
        expert_up_grad,
        expert_down_grad,
    )


def solution(mesh):
    placed = (
        P(("dp", "tensor"), None),
        P(),
        P(None, "tensor"),
        P(None, None, "tensor"),
        P("tensor", None),
        P(),
        P("dp", None, None),
        P("dp", None, None),
        P(("dp", "tensor"), None),
        P(("dp", "tensor"), None),
    )
    return jax.shard_map(
        per_device,
        mesh=mesh,
        in_specs=placed,
        out_specs=(
            P(("dp", "tensor"), None),
            P(("dp", "tensor"), None),
            P(None, ("dp", "tensor")),
            P("dp", "tensor"),
            P("dp", None, "tensor"),
            P("tensor", "dp"),
            P(None, ("dp", "tensor")),
            P("dp", "tensor", None),
            P("dp", None, "tensor"),
        ),
        check_vma=False,
    )
```

time: 1720 us -> 757 us (0.44)
  blocking collectives: 381 us -> 0 us
  other arithmetic: 412 us -> 59.9 us
  local copies, waits for them, and re-layouts: 340 us -> 95.1 us
  starting transfers between devices: 170 us -> 128 us
  waiting for transfers between devices: 243 us -> 285 us
  matrix products: 137 us -> 165 us
    unnamed x2 -> x0, blocking collectives: 381 us -> none
    all_to_all x2 -> x0, other arithmetic: 284 us -> none  [the longest x1 142 us: per_device(): lax.all_to_all(grad_rows, 'dp', split_axis=0, concat_axis=1, tiled=True)]
    unnamed x135 -> x148, local copies, waits for them, and re-layouts: 124 us -> 12.3 us
    gather x2 -> x0, local copies, waits for them, and re-layouts: 92.4 us -> none  [the longest x1 46.4 us: per_device(): grad_returned[slot_index, flat_routes]]
    unnamed x32 -> x0, starting transfers between devices: 90.8 us -> none
    ppermute x0 -> x16, waiting for transfers between devices: none -> 56.4 us  [shift_tensor(): lax.ppermute(values, 'tensor', [(i, (i + step) % 4) for i in range(4)])]
    all_gather x2 -> x0, waiting for transfers between devices: 55.3 us -> none  [the longest x1 38 us: per_device(): lax.all_gather(normed.astype(jnp.bfloat16), 'tensor', axis=0, tiled=True)]
    all_to_all x4 -> x7, waiting for transfers between devices: 174 us -> 228 us  [the longest x6 226 us: exchange(): return lax.all_to_all(values, 'dp', split_axis=0, concat_axis=0, tiled=True)]
  transfers between devices with their start and end apart: 44 -> 25, of which waited for: 6 -> 16; matrix products, arithmetic and copies ran while one was open for 47% -> 30% of each run, Pallas kernels for 0% -> 0%
where the time goes in v1:
time: 757 us; the launch traced here: 749 us
  waiting for transfers between devices  285 us (38%)
  matrix products  165 us (22%)
  starting transfers between devices  128 us (17%)
  local copies, waits for them, and re-layouts  95.1 us (13%)
  other arithmetic  59.9 us (8%)
  between operations  15.5 us (2%)
    all_to_all x6, waiting for transfers between devices, exchange(): return lax.all_to_all(values, 'dp', split_axis=0, concat_axis=0, tiled=True)  226 us
    dot_general x25, matrix products, dot(): lax.dot_general(a, b, (((ca,), (cb,)), ((), ())), preferred_element_type=...  112 us
    all_to_all x6, starting transfers between devices, exchange(): return lax.all_to_all(values, 'dp', split_axis=0, concat_axis=0, tiled=True)  99.9 us
    ppermute x16, waiting for transfers between devices, shift_tensor(): lax.ppermute(values, 'tensor', [(i, (i + step) % 4) for i in range(4)])  56.4 us
    dynamic_update_slice x4, local copies, waits for them, and re-layouts, per_device(): lax.scan(backward_block, (zero_keys, zero_keys), (query_block_list, grad_...  31.6 us
    ppermute x16, starting transfers between devices, shift_tensor(): lax.ppermute(values, 'tensor', [(i, (i + step) % 4) for i in range(4)])  24.5 us
    dot_general x2, matrix products, backward_block(): jnp.einsum('qhgd,shd->hgqs', grad_piece, values_low, preferred_element_ty...  15.4 us
  transfers between devices with their start and end apart: 25, of which 16 were waited for; matrix products, arithmetic and copies ran while one was open for 30% of the time, Pallas kernels for 0%

profile of v1, /device:TPU:1, one launch (start us, length us, event | category | flops | bytes accessed | tf_op | source)
XLA Modules:
  0.0 749.1 jit_solution(17449093604570406040)
XLA Ops:
  20.4 13.0 %collective-permute-done = bf16[256,1536]{1,0:T(8,128)(2,1)} collective-permute-done((bf16[256,1536]{1,0:T(8,128)(2,1)}, bf16[256,1536]{1,0:T(8,128)(2,1)}, u32[]{:S(2)}, u32[]{:S(2)}) %collective-permute-start) | collective-permute-done | bytes 786464 | tf_op jit(solution)/shard_map/ppermute | solution.py:66
  58.2 28.9 %while.28 = (s32[]{:T(128)}, bf16[2,512,2,3,64]{1,4,3,2,0:T(8,128)(2,1)}, f32[2,2,3,512,1]{3,2,1,4,0:T(4,128)}, s32[2]{0:T(128)S(1)}, bf16[2,512,2,3,64]{1,4,3,2...) while((s32[]{:T(128)}, ...), condition=%wide.region_4.5_spmd.clone, body=%wide.region_1.4_spmd.clone.sunk | while | flops 843773440 | bytes 48816388 | solution.py:202
  104.2 11.5 %collective-permute-done.7 = bf16[256,1536]{1,0:T(8,128)(2,1)S(1)} collective-permute-done((bf16[256,1536]{1,0:T(8,128)(2,1)S(1)}, bf16[256,1536]{1,0:T(8,128)(2,1)S(1)}, u32[]{:S(2)}, u32[]{:S(2)}) %collective-permute-start.7) | collective-permute-done | bytes 786464 | tf_op jit(solution)/shard_map/ppermute | solution.py:66
  128.0 13.7 %all-to-all-start = ((bf16[32,72,1536]{2,1,0:T(8,128)(2,1)}), bf16[32,72,1536]{2,1,0:T(8,128)(2,1)}, u32[]{:S(2)}, u32[]{:S(2)}) async-start(bf16[32,72,1536]{2,1,0:T(8,128)(2,1)} %select_convert_fusion.1), calls=%async_computation | async-start | bytes 14155776 | tf_op jit(solution)/shard_map/all_to_all | solution.py:104
  151.5 77.8 %all-to-all-done = bf16[32,72,1536]{2,1,0:T(8,128)(2,1)} async-done(((bf16[32,72,1536]{2,1,0:T(8,128)(2,1)}), bf16[32,72,1536]{2,1,0:T(8,128)(2,1)}, u32[]{:S(2)}, u32[]{:S(2)}) %all-to-all-start) | async-done | bytes 7077920 | tf_op jit(solution)/shard_map/all_to_all | solution.py:104
  229.3 24.1 %all-to-all-start.2 = ((bf16[32,72,1536]{2,1,0:T(8,128)(2,1)}), bf16[32,72,1536]{2,1,0:T(8,128)(2,1)}, u32[]{:S(2)}, u32[]{:S(2)}) async-start(bf16[32,72,1536]{2,1,0:T(8,128)(2,1)} %bitcast.302), calls=%async_computation.2 | async-start | bytes 14155776 | tf_op jit(solution)/shard_map/all_to_all | solution.py:104
  256.4 11.9 %fusion.71 = f32[2304,1024]{1,0:T(8,128)} fusion(bf16[2304,1536]{1,0:T(8,128)(2,1)} %bitcast.6, bf16[1,1536,1024]{2,1,0:T(8,128)(2,1)S(1)} %copy-done), kind=kOutput, calls=%fused_computation.91 | convolution fusion | flops 7247757312 | bytes 19660800 | tf_op jit(solution)/shard_map/dot_general | solution.py:22
  268.3 72.7 %all-to-all-done.2 = bf16[32,72,1536]{2,1,0:T(8,128)(2,1)} async-done(((bf16[32,72,1536]{2,1,0:T(8,128)(2,1)}), bf16[32,72,1536]{2,1,0:T(8,128)(2,1)}, u32[]{:S(2)}, u32[]{:S(2)}) %all-to-all-start.2) | async-done | bytes 7077920 | tf_op jit(solution)/shard_map/all_to_all | solution.py:104
  340.9 13.2 %multiply_convert_fusion.1 = (bf16[2304,512]{1,0:T(8,128)(2,1)}, bf16[2304,512]{1,0:T(8,128)(2,1)}, f32[2304]{0:T(1024)}, f32[2304,512]{1,0:T(8,128)}) fusion(f32[2304,1024]{1,0:T(8,128)} %fusion.71, f32[2304]{0:T(1024)} %add.244, bf16[2304,1536]{1,0:T(8,128)(2,1)} %bitcast.13, bf16[1,512,1536]{2,1,0:T(8,128)(2,1)} %param.21), kind=kOutput, calls=%fused_computation.82 | convolution fusion | flops 3645110016 | bytes 27543552 | tf_op jit(solution)/shard_map/dot_general | solution.py:22
  356.3 12.2 %select_convert_fusion = bf16[32,72,1536]{2,1,0:T(8,128)(2,1)} fusion(bf16[32,1536]{1,0:T(8,128)(2,1)S(1)} %pad.20, bf16[32,1536]{1,0:T(8,128)(2,1)S(1)} %pad.19, pred[72]{0:T(512)(128)(4,1)} %copy-done.74, pred[72]{0:T(512)(128)(4,1)} %copy-done.75, bf16[32,72,512]{2,1,0:T(8,128)(2,1)} %bitcast.327, bf16[32,72,512]{2,1,0:T(8,128)(2,1)} %bitcast.326, ...), kind=kOutput, calls=%fused_computation.63 | convolution fusion | flops 7264272384 | bytes 15138960 | tf_op jit(solution)/shard_map/dot_general | solution.py:22
  368.4 23.7 %all-to-all-start.3 = ((bf16[32,72,1536]{2,1,0:T(8,128)(2,1)}), bf16[32,72,1536]{2,1,0:T(8,128)(2,1)}, u32[]{:S(2)}, u32[]{:S(2)}) async-start(bf16[32,72,1536]{2,1,0:T(8,128)(2,1)} %select_convert_fusion), calls=%async_computation.3 | async-start | bytes 14155776 | tf_op jit(solution)/shard_map/all_to_all | solution.py:104
  392.4 9.6 %convolution_convert_fusion.3 = bf16[1536,512]{1,0:T(8,128)(2,1)} fusion(bf16[2304,1536]{1,0:T(8,128)(2,1)} %bitcast.13, f32[2304,512]{1,0:T(8,128)} %get-tuple-element.292, f32[2304]{0:T(1024)S(1)} %copy-done.57), kind=kOutput, calls=%fused_computation.99 | convolution fusion | flops 3627024384 | bytes 13378560 | tf_op jit(solution)/shard_map/dot_general | solution.py:22
  402.1 11.7 %fusion.67 = bf16[1536,1024]{1,0:T(8,128)(2,1)} fusion(bf16[2304,1536]{1,0:T(8,128)(2,1)} %bitcast.6, bf16[2304,512]{1,0:T(8,128)(2,1)} %get-tuple-element.290, bf16[2304,512]{1,0:T(8,128)(2,1)S(1)} %copy-done.71), kind=kOutput, calls=%fused_computation.88 | convolution fusion | flops 7258767360 | bytes 14942208 | tf_op jit(solution)/shard_map/dot_general | solution.py:22
  416.0 8.4 %convolution_convert_fusion.1 = bf16[2304,1536]{1,0:T(8,128)(2,1)} fusion(bf16[1,512,1536]{2,1,0:T(8,128)(2,1)S(1)} %copy-done.70, f32[2304,512]{1,0:T(8,128)} %get-tuple-element.292, f32[2304]{0:T(1024)S(1)} %copy-done.57), kind=kOutput, calls=%fused_computation.66 | convolution fusion | flops 3629776896 | bytes 13378560 | tf_op jit(solution)/shard_map/dot_general | solution.py:22
  424.4 55.3 %all-to-all-done.3 = bf16[32,72,1536]{2,1,0:T(8,128)(2,1)} async-done(((bf16[32,72,1536]{2,1,0:T(8,128)(2,1)}), bf16[32,72,1536]{2,1,0:T(8,128)(2,1)}, u32[]{:S(2)}, u32[]{:S(2)}) %all-to-all-start.3) | async-done | bytes 7077920 | tf_op jit(solution)/shard_map/all_to_all | solution.py:104
  479.8 24.0 %all-to-all-start.1 = ((bf16[32,72,1536]{2,1,0:T(8,128)(2,1)}), bf16[32,72,1536]{2,1,0:T(8,128)(2,1)}, u32[]{:S(2)}, u32[]{:S(2)}) async-start(bf16[32,72,1536]{2,1,0:T(8,128)(2,1)} %bitcast.304), calls=%async_computation.1 | async-start | bytes 14155776 | tf_op jit(solution)/shard_map/all_to_all | solution.py:104
  528.7 8.6 %collective-permute-done.8 = bf16[256,1536]{1,0:T(8,128)(2,1)S(1)} collective-permute-done((bf16[256,1536]{1,0:T(8,128)(2,1)}, bf16[256,1536]{1,0:T(8,128)(2,1)S(1)}, u32[]{:S(2)}, u32[]{:S(2)}) %collective-permute-start.8) | collective-permute-done | bytes 786464 | tf_op jit(solution)/shard_map/ppermute | solution.py:66
  555.8 85.0 %while.29 = (s32[]{:T(128)}, f32[1024,2,64]{0,2,1:T(8,128)S(1)}, f32[1024,2,64]{0,2,1:T(8,128)}, f32[2,512,2,3,64]{1,0,4,3,2:T(2,128)}, bf16[2,512,2,3,64]{1,4,3...) while((s32[]{:T(128)}, f32[1024,2,64]{0,2,1:T(8,128)S(1)}, ...), condition=%wide.region_16.17_spmd.clone, body=%wide.region_14.16_spmd.clone.sunk | while | flops 2061825536 | bytes 104947896 | solution.py:326
  564.8 7.7 %fusion.216 = (f32[2,3,512]{2,1,0:T(4,128)S(1)}, f32[2,512,3,1024]{3,1,2,0:T(8,128)}) fusion(f32[2,512,3,1024]{3,1,2,0:T(8,128)S(1)} %fusion.215, f32[2,3,512]{2,1,0:T(4,128)S(1)} %dynamic-slice_bitcast_fusion.2, pred[512,1024]{1,0:T(8,128)(4,1)S(1)} %iota_compare_fusion.10, bf16[1024,2,64]{0,2,1:T(8,128)(2,1)S(1)} %get-tuple-element.497, ...), kind=kOutput, calls=%fused_computation.25.clone.1 | convolution fusion | flops 418378752 | bytes 26370052 | tf_op jit(solution)/shard_map/while/body/eval_jaxpr/qhgd,shd->hgqs/dot_general | solution.py:307
  583.4 15.0 %dynamic_update_slice.72 = f32[2,512,2,3,64]{1,0,4,3,2:T(2,128)} dynamic-update-slice(f32[2,512,2,3,64]{1,0,4,3,2:T(2,128)} %get-tuple-element.479, f32[1,512,2,3,64]{1,0,4,3,2:T(1,128)S(1)} %copy.89, s32[]{:T(128)S(6)} %copy.117, s32[]{:T(128)} %constant.52.clone.1..sunk, s32[]{:T(128)} %constant.52.clone.1..sunk, s32[]{:T(128)} %constant.52.clone.1..sunk, s32[]{:T(128)} %constant.52.clone.1..sunk) | dynamic-update-slice | bytes 1572868 | tf_op jit(solution)/shard_map/while/body/jit(dynamic_update_index_in_dim)/dynamic_update_slice | solution.py:326
  625.8 15.0 %dynamic_update_slice.72 = f32[2,512,2,3,64]{1,0,4,3,2:T(2,128)} dynamic-update-slice(f32[2,512,2,3,64]{1,0,4,3,2:T(2,128)} %get-tuple-element.479, f32[1,512,2,3,64]{1,0,4,3,2:T(1,128)S(1)} %copy.89, s32[]{:T(128)S(6)} %copy.117, s32[]{:T(128)} %constant.52.clone.1..sunk, s32[]{:T(128)} %constant.52.clone.1..sunk, s32[]{:T(128)} %constant.52.clone.1..sunk, s32[]{:T(128)} %constant.52.clone.1..sunk) | dynamic-update-slice | bytes 1572868 | tf_op jit(solution)/shard_map/while/body/jit(dynamic_update_index_in_dim)/dynamic_update_slice | solution.py:326
  666.0 9.0 %all-to-all-start.4 = ((bf16[32,48,512]{2,1,0:T(8,128)(2,1)}), bf16[32,48,512]{2,1,0:T(8,128)(2,1)}, u32[]{:S(2)}, u32[]{:S(2)}) async-start(bf16[32,48,512]{2,1,0:T(8,128)(2,1)} %concatenate.92), calls=%async_computation.4 | async-start | bytes 3145728 | tf_op jit(solution)/shard_map/all_to_all | solution.py:104
  689.9 7.9 %all-to-all-done.4 = bf16[32,48,512]{2,1,0:T(8,128)(2,1)} async-done(((bf16[32,48,512]{2,1,0:T(8,128)(2,1)}), bf16[32,48,512]{2,1,0:T(8,128)(2,1)}, u32[]{:S(2)}, u32[]{:S(2)}) %all-to-all-start.4) | async-done | bytes 1572896 | tf_op jit(solution)/shard_map/all_to_all | solution.py:104
  717.9 12.1 %all-to-all-done.5 = bf16[32,48,640]{2,1,0:T(8,128)(2,1)} async-done(((bf16[32,48,640]{2,1,0:T(8,128)(2,1)}), bf16[32,48,640]{2,1,0:T(8,128)(2,1)}, u32[]{:S(2)}, u32[]{:S(2)}) %all-to-all-start.5) | async-done | bytes 1966112 | tf_op jit(solution)/shard_map/all_to_all | solution.py:104
  (384 shorter events, 274.7 us)
Async XLA Ops:
  13.0 20.4 %collective-permute-start = (bf16[256,1536]{1,0:T(8,128)(2,1)}, bf16[256,1536]{1,0:T(8,128)(2,1)}, u32[]{:S(2)}, u32[]{:S(2)}) collective-permute-start(bf16[256,1536]{1,0:T(8,128)(2,1)} %get-tuple-element.284), channel_id=1, source_target_pairs={{0,1},{1,2},{2,3},{3,0},{4,5},{5,6},{6,7},{7,4},{8,9},{9,10},{10,1... | collective-permute-start | bytes 2359304 | tf_op jit(solution)/shard_map/ppermute | solution.py:66
  15.0 19.8 %collective-permute-start.1 = (bf16[256,1536]{1,0:T(8,128)(2,1)}, bf16[256,1536]{1,0:T(8,128)(2,1)}, u32[]{:S(2)}, u32[]{:S(2)}) collective-permute-start(bf16[256,1536]{1,0:T(8,128)(2,1)} %get-tuple-element.284), channel_id=1, source_target_pairs={{0,3},{1,0},{2,1},{3,2},{4,7},{5,4},{6,5},{7,6},{8,11},{9,8},{10,9... | collective-permute-start | bytes 2359304 | tf_op jit(solution)/shard_map/ppermute | solution.py:66
  34.4 10.2 %collective-permute-start.2 = (bf16[128,1536]{1,0:T(8,128)(2,1)S(1)}, bf16[128,1536]{1,0:T(8,128)(2,1)S(1)}, u32[]{:S(2)}, u32[]{:S(2)}) collective-permute-start(bf16[128,1536]{1,0:T(8,128)(2,1)S(1)} %slice.188), channel_id=1, source_target_pairs={{0,1},{1,2},{2,3},{3,0},{4,5},{5,6},{6,7},{7,4},{8,9},{9,10},{10,1... | collective-permute-start | bytes 1179656 | tf_op jit(solution)/shard_map/ppermute | solution.py:66
  35.9 9.0 %collective-permute-start.3 = (bf16[128,1536]{1,0:T(8,128)(2,1)S(1)}, bf16[128,1536]{1,0:T(8,128)(2,1)S(1)}, u32[]{:S(2)}, u32[]{:S(2)}) collective-permute-start(bf16[128,1536]{1,0:T(8,128)(2,1)S(1)} %slice.189), channel_id=1, source_target_pairs={{0,3},{1,0},{2,1},{3,2},{4,7},{5,4},{6,5},{7,6},{8,11},{9,8},{10,9... | collective-permute-start | bytes 1179656 | tf_op jit(solution)/shard_map/ppermute | solution.py:66
  90.1 9.0 %collective-permute-start.6 = (bf16[128,1536]{1,0:T(8,128)(2,1)S(1)}, bf16[128,1536]{1,0:T(8,128)(2,1)S(1)}, u32[]{:S(2)}, u32[]{:S(2)}) collective-permute-start(bf16[128,1536]{1,0:T(8,128)(2,1)S(1)} %get-tuple-element.302), channel_id=1, source_target_pairs={{0,3},{1,0},{2,1},{3,2},{4,7},{5,4},{6,5},{7,6},{8,11},{9,8},{10,9... | collective-permute-start | bytes 1179656 | tf_op jit(solution)/shard_map/ppermute | solution.py:66
  94.1 8.9 %collective-permute-start.4 = (bf16[128,1536]{1,0:T(8,128)(2,1)S(1)}, bf16[128,1536]{1,0:T(8,128)(2,1)S(1)}, u32[]{:S(2)}, u32[]{:S(2)}) collective-permute-start(bf16[128,1536]{1,0:T(8,128)(2,1)S(1)} %get-tuple-element.301), channel_id=1, source_target_pairs={{0,1},{1,2},{2,3},{3,0},{4,5},{5,6},{6,7},{7,4},{8,9},{9,10},{10,1... | collective-permute-start | bytes 1179656 | tf_op jit(solution)/shard_map/ppermute | solution.py:66
  99.2 16.5 %collective-permute-start.7 = (bf16[256,1536]{1,0:T(8,128)(2,1)S(1)}, bf16[256,1536]{1,0:T(8,128)(2,1)S(1)}, u32[]{:S(2)}, u32[]{:S(2)}) collective-permute-start(bf16[256,1536]{1,0:T(8,128)(2,1)S(1)} %pad_maximum_fusion.3), channel_id=1, source_target_pairs={{0,3},{1,0},{2,1},{3,2},{4,7},{5,4},{6,5},{7,6},{8,11},{9,8},{10,9... | collective-permute-start | bytes 2359304 | tf_op jit(solution)/shard_map/ppermute | solution.py:66
  103.2 16.2 %collective-permute-start.5 = (bf16[256,1536]{1,0:T(8,128)(2,1)S(1)}, bf16[256,1536]{1,0:T(8,128)(2,1)S(1)}, u32[]{:S(2)}, u32[]{:S(2)}) collective-permute-start(bf16[256,1536]{1,0:T(8,128)(2,1)S(1)} %pad_maximum_fusion.2), channel_id=1, source_target_pairs={{0,1},{1,2},{2,3},{3,0},{4,5},{5,6},{6,7},{7,4},{8,9},{9,10},{10,1... | collective-permute-start | bytes 2359304 | tf_op jit(solution)/shard_map/ppermute | solution.py:66
  128.0 101.4 %all-to-all-start = ((bf16[32,72,1536]{2,1,0:T(8,128)(2,1)}), bf16[32,72,1536]{2,1,0:T(8,128)(2,1)}, u32[]{:S(2)}, u32[]{:S(2)}) async-start(bf16[32,72,1536]{2,1,0:T(8,128)(2,1)} %select_convert_fusion.1), calls=%async_computation | async-start | bytes 14155776 | tf_op jit(solution)/shard_map/all_to_all | solution.py:104
  229.3 111.6 %all-to-all-start.2 = ((bf16[32,72,1536]{2,1,0:T(8,128)(2,1)}), bf16[32,72,1536]{2,1,0:T(8,128)(2,1)}, u32[]{:S(2)}, u32[]{:S(2)}) async-start(bf16[32,72,1536]{2,1,0:T(8,128)(2,1)} %bitcast.302), calls=%async_computation.2 | async-start | bytes 14155776 | tf_op jit(solution)/shard_map/all_to_all | solution.py:104
  368.4 111.4 %all-to-all-start.3 = ((bf16[32,72,1536]{2,1,0:T(8,128)(2,1)}), bf16[32,72,1536]{2,1,0:T(8,128)(2,1)}, u32[]{:S(2)}, u32[]{:S(2)}) async-start(bf16[32,72,1536]{2,1,0:T(8,128)(2,1)} %select_convert_fusion), calls=%async_computation.3 | async-start | bytes 14155776 | tf_op jit(solution)/shard_map/all_to_all | solution.py:104
  392.2 127.3 %reduce-scatter.5.cloned.1.call-start = ((), (), s32[]{:S(2)}) async-start(), calls=%async_computation.10 | async-start | bytes 1966080 | tf_op jit(solution)/shard_map/reduce_scatter | solution.py:257
  402.0 119.7 %reduce-scatter.3.cloned.1.call-start = ((), (), s32[]{:S(2)}) async-start(), calls=%async_computation.9 | async-start | bytes 3932160 | tf_op jit(solution)/shard_map/reduce_scatter | solution.py:256
  479.8 186.2 %all-to-all-start.1 = ((bf16[32,72,1536]{2,1,0:T(8,128)(2,1)}), bf16[32,72,1536]{2,1,0:T(8,128)(2,1)}, u32[]{:S(2)}, u32[]{:S(2)}) async-start(bf16[32,72,1536]{2,1,0:T(8,128)(2,1)} %bitcast.304), calls=%async_computation.1 | async-start | bytes 14155776 | tf_op jit(solution)/shard_map/all_to_all | solution.py:104
  516.8 20.5 %collective-permute-start.8 = (bf16[256,1536]{1,0:T(8,128)(2,1)}, bf16[256,1536]{1,0:T(8,128)(2,1)S(1)}, u32[]{:S(2)}, u32[]{:S(2)}) collective-permute-start(bf16[256,1536]{1,0:T(8,128)(2,1)} %get-tuple-element.277), channel_id=1, source_target_pairs={{0,1},{1,2},{2,3},{3,0},{4,5},{5,6},{6,7},{7,4},{8,9},{9,10},{10,1... | collective-permute-start | bytes 2359304 | tf_op jit(solution)/shard_map/ppermute | solution.py:66
  516.8 20.7 %collective-permute-start.9 = (bf16[256,1536]{1,0:T(8,128)(2,1)}, bf16[256,1536]{1,0:T(8,128)(2,1)}, u32[]{:S(2)}, u32[]{:S(2)}) collective-permute-start(bf16[256,1536]{1,0:T(8,128)(2,1)} %get-tuple-element.277), channel_id=1, source_target_pairs={{0,3},{1,0},{2,1},{3,2},{4,7},{5,4},{6,5},{7,6},{8,11},{9,8},{10,9... | collective-permute-start | bytes 2359304 | tf_op jit(solution)/shard_map/ppermute | solution.py:66
  537.4 11.2 %collective-permute-start.10 = (bf16[128,1536]{1,0:T(8,128)(2,1)S(1)}, bf16[128,1536]{1,0:T(8,128)(2,1)S(1)}, u32[]{:S(2)}, u32[]{:S(2)}) collective-permute-start(bf16[128,1536]{1,0:T(8,128)(2,1)S(1)} %slice.209), channel_id=1, source_target_pairs={{0,1},{1,2},{2,3},{3,0},{4,5},{5,6},{6,7},{7,4},{8,9},{9,10},{10,1... | collective-permute-start | bytes 1179656 | tf_op jit(solution)/shard_map/ppermute | solution.py:66
  538.6 10.8 %collective-permute-start.11 = (bf16[128,1536]{1,0:T(8,128)(2,1)S(1)}, bf16[128,1536]{1,0:T(8,128)(2,1)S(1)}, u32[]{:S(2)}, u32[]{:S(2)}) collective-permute-start(bf16[128,1536]{1,0:T(8,128)(2,1)S(1)} %slice.210), channel_id=1, source_target_pairs={{0,3},{1,0},{2,1},{3,2},{4,7},{5,4},{6,5},{7,6},{8,11},{9,8},{10,9... | collective-permute-start | bytes 1179656 | tf_op jit(solution)/shard_map/ppermute | solution.py:66
  648.4 28.8 %collective-permute-start.14 = (bf16[128,1536]{1,0:T(8,128)(2,1)}, bf16[128,1536]{1,0:T(8,128)(2,1)}, u32[]{:S(2)}, u32[]{:S(2)}) collective-permute-start(bf16[128,1536]{1,0:T(8,128)(2,1)} %get-tuple-element.298), channel_id=1, source_target_pairs={{0,3},{1,0},{2,1},{3,2},{4,7},{5,4},{6,5},{7,6},{8,11},{9,8},{10,9... | collective-permute-start | bytes 1179656 | tf_op jit(solution)/shard_map/ppermute | solution.py:66
  666.0 31.8 %all-to-all-start.4 = ((bf16[32,48,512]{2,1,0:T(8,128)(2,1)}), bf16[32,48,512]{2,1,0:T(8,128)(2,1)}, u32[]{:S(2)}, u32[]{:S(2)}) async-start(bf16[32,48,512]{2,1,0:T(8,128)(2,1)} %concatenate.92), calls=%async_computation.4 | async-start | bytes 3145728 | tf_op jit(solution)/shard_map/all_to_all | solution.py:104
  677.0 11.8 %collective-permute-start.12 = (bf16[128,1536]{1,0:T(8,128)(2,1)S(1)}, bf16[128,1536]{1,0:T(8,128)(2,1)S(1)}, u32[]{:S(2)}, u32[]{:S(2)}) collective-permute-start(bf16[128,1536]{1,0:T(8,128)(2,1)S(1)} %copy-done.40), channel_id=1, source_target_pairs={{0,1},{1,2},{2,3},{3,0},{4,5},{5,6},{6,7},{7,4},{8,9},{9,10},{10,1... | collective-permute-start | bytes 1179656 | tf_op jit(solution)/shard_map/ppermute | solution.py:66
  679.2 30.5 %collective-permute-start.15 = (bf16[256,1536]{1,0:T(8,128)(2,1)}, bf16[256,1536]{1,0:T(8,128)(2,1)S(1)}, u32[]{:S(2)}, u32[]{:S(2)}) collective-permute-start(bf16[256,1536]{1,0:T(8,128)(2,1)} %pad_maximum_fusion.6), channel_id=1, source_target_pairs={{0,3},{1,0},{2,1},{3,2},{4,7},{5,4},{6,5},{7,6},{8,11},{9,8},{10,9... | collective-permute-start | bytes 2359304 | tf_op jit(solution)/shard_map/ppermute | solution.py:66
  689.9 19.8 %collective-permute-start.13 = (bf16[256,1536]{1,0:T(8,128)(2,1)}, bf16[256,1536]{1,0:T(8,128)(2,1)}, u32[]{:S(2)}, u32[]{:S(2)}) collective-permute-start(bf16[256,1536]{1,0:T(8,128)(2,1)} %pad_maximum_fusion.5), channel_id=1, source_target_pairs={{0,1},{1,2},{2,3},{3,0},{4,5},{5,6},{6,7},{7,4},{8,9},{9,10},{10,1... | collective-permute-start | bytes 2359304 | tf_op jit(solution)/shard_map/ppermute | solution.py:66
  697.8 32.2 %all-to-all-start.5 = ((bf16[32,48,640]{2,1,0:T(8,128)(2,1)}), bf16[32,48,640]{2,1,0:T(8,128)(2,1)}, u32[]{:S(2)}, u32[]{:S(2)}) async-start(bf16[32,48,640]{2,1,0:T(8,128)(2,1)} %bitcast.315), calls=%async_computation.5 | async-start | bytes 3932160 | tf_op jit(solution)/shard_map/all_to_all | solution.py:104
  (82 other events, 884.5 us)
Sparse Core Ops, SparseCore 0:
  402.1 23.1 reduce-scatter.4
  427.7 39.0 reduce-scatter.2

commit v2 on v1

--- a/solution.py
+++ b/solution.py
@@ -1,6 +1,8 @@
 import jax
 import jax.numpy as jnp
 from jax import lax
+from jax.experimental import pallas as pl
+from jax.experimental.pallas import tpu as pltpu
 from jax.sharding import PartitionSpec as P
 
 QUERY_HEADS = 24
@@ -13,6 +15,12 @@
 
 epsilon = 1e-06
 theta = 10000.0
+BLOCK = 256
+GROUP = QUERY_HEADS // KEY_VALUE_HEADS
+QUERY_LOCAL = QUERY_HEADS // 4
+KEY_LOCAL = KEY_VALUE_HEADS // 4
+FACTOR = HEAD_DIM**-0.5
+SCALE = FACTOR * 1.4426950408889634
 highest = lax.Precision.HIGHEST
 f32 = jnp.float32
 bf16 = jnp.bfloat16
@@ -38,23 +46,8 @@
 def rotary_tables(sequence_length, head_width):
     half_width = head_width // 2
     freqs = theta ** (-(jnp.arange(half_width).astype(jnp.float32) * 2.0 / head_width))
-    angles = jnp.arange(sequence_length).astype(jnp.float32)[:, None] * freqs[None, :]
+    angles = freqs[:, None] * jnp.arange(sequence_length).astype(jnp.float32)[None, :]
     return (jnp.cos(angles), jnp.sin(angles))
-
-
-def apply_rotary(values, cosine_table, sine_table, direction):
-    half_width = values.shape[-1] // 2
-    first_half = values[..., :half_width]
-    second_half = values[..., half_width:]
-    cos_rows = cosine_table[:, None, :]
-    sin_rows = sine_table[:, None, :] * direction
-    return jnp.concatenate(
-        [
-            first_half * cos_rows - second_half * sin_rows,
-            second_half * cos_rows + first_half * sin_rows,
-        ],
-        axis=-1,
-    )
 
 
 def split_two(values):
@@ -104,6 +97,181 @@
     return lax.all_to_all(values, "dp", split_axis=0, concat_axis=0, tiled=True)
 
 
+def turn(values, cos, sin):
+    half = values.shape[0] // 2
+    low, high = values[:half], values[half:]
+    return jnp.concatenate([low * cos - high * sin, high * cos + low * sin], axis=0)
+
+
+def diagonal_mask():
+    key = lax.broadcasted_iota(jnp.int32, (BLOCK, BLOCK), 0)
+    query = lax.broadcasted_iota(jnp.int32, (BLOCK, BLOCK), 1)
+    return key <= query
+
+
+def attend_kernel(q_ref, k_ref, v_ref, cos_ref, sin_ref, out_ref, total_ref, turned_ref, key_s):
+    group, member = pl.program_id(0), pl.program_id(1)
+    cos, sin = cos_ref[...], sin_ref[...]
+
+    @pl.when(member == 0)
+    def _():
+        keys = turn(k_ref[...], cos, sin)
+        key_s[...] = keys.T.astype(bf16)
+        first = pl.multiple_of((QUERY_LOCAL + group) * HEAD_DIM, HEAD_DIM)
+        turned_ref[pl.ds(first, HEAD_DIM), :] = keys.astype(bf16)
+        second = pl.multiple_of((QUERY_LOCAL + KEY_LOCAL + group) * HEAD_DIM, HEAD_DIM)
+        turned_ref[pl.ds(second, HEAD_DIM), :] = v_ref[...].astype(bf16)
+
+    queries = turn(q_ref[...], cos, sin).astype(bf16)
+    values = v_ref[...].astype(bf16)
+    head = pl.multiple_of((group * GROUP + member) * HEAD_DIM, HEAD_DIM)
+    turned_ref[pl.ds(head, HEAD_DIM), :] = queries
+    causal = diagonal_mask()
+    for j in range(queries.shape[1] // BLOCK):
+        columns = slice(j * BLOCK, (j + 1) * BLOCK)
+        query = queries[:, columns]
+        tiles = []
+        top = None
+        for i in range(j + 1):
+            tile = dot(key_s[i * BLOCK : (i + 1) * BLOCK, :], query, 1, 0) * SCALE
+            if i == j:
+                tile = jnp.where(causal, tile, -1e30)
+            tiles.append(tile)
+            peak = jnp.max(tile, axis=0, keepdims=True)
+            top = peak if top is None else jnp.maximum(top, peak)
+        total = jnp.zeros_like(top)
+        summed = jnp.zeros((HEAD_DIM, BLOCK), f32)
+        for i in range(j + 1):
+            tile = jnp.exp2(tiles[i] - top)
+            total = total + jnp.sum(tile, axis=0, keepdims=True)
+            summed = summed + dot(values[:, i * BLOCK : (i + 1) * BLOCK], tile.astype(bf16), 1, 0)
+        out_ref[pl.ds(head, HEAD_DIM), columns] = (summed / total).astype(bf16)
+        total_ref[0, :, columns] = top + jnp.log2(total)
+
+
+def attend_back_kernel(
+    q_ref, k_ref, v_ref, out_ref, grad_ref, total_ref, cos_ref, sin_ref, back_ref, key_s, val_s, gk_s, gv_s
+):
+    group, member = pl.program_id(0), pl.program_id(1)
+    cos, sin = cos_ref[...], sin_ref[...]
+
+    @pl.when(member == 0)
+    def _():
+        key_s[...] = k_ref[...].astype(f32).T.astype(bf16)
+        val_s[...] = v_ref[...].astype(f32).T.astype(bf16)
+        gk_s[...] = jnp.zeros_like(gk_s)
+        gv_s[...] = jnp.zeros_like(gv_s)
+
+    queries, grads, keys = q_ref[...], grad_ref[...], k_ref[...]
+    inner = jnp.sum(out_ref[...].astype(f32) * grads.astype(f32), axis=0, keepdims=True)
+    totals = total_ref[0]
+    causal = diagonal_mask()
+    pieces = []
+    for j in range(queries.shape[1] // BLOCK):
+        columns = slice(j * BLOCK, (j + 1) * BLOCK)
+        query, grad = queries[:, columns], grads[:, columns]
+        query_grad = jnp.zeros((HEAD_DIM, BLOCK), f32)
+        for i in range(j + 1):
+            rows = slice(i * BLOCK, (i + 1) * BLOCK)
+            probs = jnp.exp2(dot(key_s[rows, :], query, 1, 0) * SCALE - totals[:, columns])
+            if i == j:
+                probs = jnp.where(causal, probs, 0.0)
+            gv_s[rows, :] += dot(probs.astype(bf16), grad, 1, 1)
+            grad_probs = dot(val_s[rows, :], grad, 1, 0)
+            grad_scores = (probs * (grad_probs - inner[:, columns])).astype(bf16)
+            query_grad = query_grad + dot(keys[:, rows], grad_scores, 1, 0)
+            gk_s[rows, :] += dot(grad_scores, query, 1, 1)
+        pieces.append(query_grad * FACTOR)
+    head = pl.multiple_of((group * GROUP + member) * HEAD_DIM, HEAD_DIM)
+    query_back = turn(jnp.concatenate(pieces, axis=1), cos, -sin)
+    back_ref[pl.ds(head, HEAD_DIM), :] = query_back.astype(bf16)
+
+    @pl.when(member == GROUP - 1)
+    def _():
+        first = pl.multiple_of((QUERY_LOCAL + group) * HEAD_DIM, HEAD_DIM)
+        back_ref[pl.ds(first, HEAD_DIM), :] = turn(gk_s[...].T * FACTOR, cos, -sin).astype(bf16)
+        second = pl.multiple_of((QUERY_LOCAL + KEY_LOCAL + group) * HEAD_DIM, HEAD_DIM)
+        back_ref[pl.ds(second, HEAD_DIM), :] = gv_s[...].T.astype(bf16)
+
+
+def head_block(first, per_group, tokens):
+    if per_group:
+        return pl.BlockSpec((HEAD_DIM, tokens), lambda g, m: (first + g * per_group + m, 0))
+    return pl.BlockSpec((HEAD_DIM, tokens), lambda g, m: (first + g, 0))
+
+
+def whole_block(shape):
+    return pl.BlockSpec(shape, lambda g, m: (0,) * len(shape))
+
+
+def attend(projected, cos, sin):
+    width, tokens = projected.shape
+    total_block = pl.BlockSpec((1, 1, tokens), lambda g, m: (g * GROUP + m, 0, 0))
+    return pl.pallas_call(
+        attend_kernel,
+        grid=(KEY_LOCAL, GROUP),
+        in_specs=[
+            head_block(0, GROUP, tokens),
+            head_block(QUERY_LOCAL, 0, tokens),
+            head_block(QUERY_LOCAL + KEY_LOCAL, 0, tokens),
+            whole_block(cos.shape),
+            whole_block(sin.shape),
+        ],
+        out_specs=(
+            whole_block((QUERY_LOCAL * HEAD_DIM, tokens)),
+            total_block,
+            whole_block((width, tokens)),
+        ),
+        out_shape=(
+            jax.ShapeDtypeStruct((QUERY_LOCAL * HEAD_DIM, tokens), bf16),
+            jax.ShapeDtypeStruct((QUERY_LOCAL, 1, tokens), f32),
+            jax.ShapeDtypeStruct((width, tokens), bf16),
+        ),
+        scratch_shapes=[pltpu.VMEM((tokens, HEAD_DIM), bf16)],
+        compiler_params=pltpu.CompilerParams(vmem_limit_bytes=40 * 2**20),
+        cost_estimate=pl.CostEstimate(
+            flops=QUERY_LOCAL * tokens * tokens * HEAD_DIM * 3,
+            bytes_accessed=6 * width * tokens,
+            transcendentals=QUERY_LOCAL * tokens * tokens,
+        ),
+        name="attend",
+    )(projected, projected, projected, cos, sin)
+
+
+def attend_back(turned, out, grad, totals, cos, sin):
+    width, tokens = turned.shape
+    total_block = pl.BlockSpec((1, 1, tokens), lambda g, m: (g * GROUP + m, 0, 0))
+    return pl.pallas_call(
+        attend_back_kernel,
+        grid=(KEY_LOCAL, GROUP),
+        in_specs=[
+            head_block(0, GROUP, tokens),
+            head_block(QUERY_LOCAL, 0, tokens),
+            head_block(QUERY_LOCAL + KEY_LOCAL, 0, tokens),
+            head_block(0, GROUP, tokens),
+            head_block(0, GROUP, tokens),
+            total_block,
+            whole_block(cos.shape),
+            whole_block(sin.shape),
+        ],
+        out_specs=whole_block((width, tokens)),
+        out_shape=jax.ShapeDtypeStruct((width, tokens), bf16),
+        scratch_shapes=[
+            pltpu.VMEM((tokens, HEAD_DIM), bf16),
+            pltpu.VMEM((tokens, HEAD_DIM), bf16),
+            pltpu.VMEM((tokens, HEAD_DIM), f32),
+            pltpu.VMEM((tokens, HEAD_DIM), f32),
+        ],
+        compiler_params=pltpu.CompilerParams(vmem_limit_bytes=40 * 2**20),
+        cost_estimate=pl.CostEstimate(
+            flops=QUERY_LOCAL * tokens * tokens * HEAD_DIM * 7,
+            bytes_accessed=6 * width * tokens,
+            transcendentals=QUERY_LOCAL * tokens * tokens,
+        ),
+        name="attend_back",
+    )(turned, turned, turned, out, grad, totals, cos, sin)
+
+
 def per_device(
     tokens,
     norm_gains,
@@ -119,10 +287,6 @@
     local_rows, model_width = tokens.shape
     query_width = query_matrix.shape[1]
     keyval_width = key_value_weight.shape[2]
-    head_width = HEAD_DIM
-    group_width = QUERY_HEADS // KEY_VALUE_HEADS
-    kv_heads = keyval_width // head_width
-    local_heads = query_width // head_width
     experts_all = router.shape[0]
     place = lax.axis_index("tensor")
     group = lax.axis_index("dp")
@@ -149,62 +313,14 @@
     joined_weight = jnp.concatenate(
         [query_matrix, key_value_weight.reshape(model_width, 2 * keyval_width)], axis=1
     )
-    projected_rows = jnp.dot(sequence, joined_weight, preferred_element_type=jnp.float32)
-    cosine_table, sine_table = rotary_tables(sequence_length, head_width)
-    query_rows = apply_rotary(
-        projected_rows[:, :query_width].reshape(sequence_length, local_heads, head_width),
-        cosine_table,
-        sine_table,
-        1.0,
-    ).astype(jnp.bfloat16)
-    keys_low = apply_rotary(
-        projected_rows[:, query_width : query_width + keyval_width].reshape(
-            sequence_length, kv_heads, head_width
-        ),
-        cosine_table,
-        sine_table,
-        1.0,
-    ).astype(jnp.bfloat16)
-    values_low = (
-        projected_rows[:, query_width + keyval_width :]
-        .reshape(sequence_length, kv_heads, head_width)
-        .astype(jnp.bfloat16)
-    )
-    rows_per_block = min(512, sequence_length)
-    block_count = sequence_length // rows_per_block
-    query_block_list = query_rows.reshape(
-        block_count, rows_per_block, kv_heads, group_width, head_width
-    )
-    block_starts = jnp.arange(block_count, dtype=jnp.int32) * rows_per_block
-    key_index = jnp.arange(sequence_length, dtype=jnp.int32)
-    factor = head_width ** (-0.5)
-
-    def masked_scores(query_piece, row_start):
-        raw_scores = (
-            jnp.einsum("qhgd,shd->hgqs", query_piece, keys_low, preferred_element_type=jnp.float32)
-            * factor
-        )
-        row_index = row_start + jnp.arange(rows_per_block, dtype=jnp.int32)
-        return jnp.where(row_index[:, None] >= key_index[None, :], raw_scores, -1e30)
-
-    def forward_block(operands):
-        query_piece, row_start = operands
-        scores = masked_scores(query_piece, row_start)
-        row_max = jnp.max(scores, axis=-1, keepdims=True)
-        exp_scores = jnp.exp(scores - row_max)
-        row_total = jnp.sum(exp_scores, axis=-1, keepdims=True)
-        attn_probs = (exp_scores / row_total).astype(jnp.bfloat16)
-        attended_piece = jnp.einsum(
-            "hgqs,shd->qhgd", attn_probs, values_low, preferred_element_type=jnp.float32
-        )
-        return (attended_piece.astype(jnp.bfloat16), row_max + jnp.log(row_total))
-
-    attended_blocks, log_totals = lax.map(forward_block, (query_block_list, block_starts))
-    attended = attended_blocks.reshape(sequence_length, query_width)
+    weight_turned = joined_weight.T
+    cos, sin = rotary_tables(sequence_length, HEAD_DIM)
+    projected = dot(weight_turned, sequence, 1, 1)
+    attended, log_totals, turned = attend(projected, cos, sin)
 
     def output_chunk(k):
         start = lax.rem(place + k, 4) * local_rows
-        return dot(lax.dynamic_slice_in_dim(attended, start, local_rows, 0), output_weight, 1, 0)
+        return dot(lax.dynamic_slice_in_dim(attended, start, local_rows, 1), output_weight, 0, 0)
 
     middle = inputs + scatter_tensor(output_chunk)
     mixed_norm, inv_rms_two = norm_rows(middle, norm_gains[1])
@@ -229,7 +345,10 @@
 
     gates_slot = jnp.sum(jnp.where(sending, gates.T[:, None, :], 0.0), axis=2)
     mixed_send = dot(send_matrix, mixed_low, 1, 0).reshape(experts_all, ROWS, model_width)
-    received = exchange(with_spare(mixed_send, gates_slot))
+    mixed_send, cot_rows = lax.optimization_barrier(
+        (with_spare(mixed_send, gates_slot), cot_rows)
+    )
+    received = exchange(mixed_send)
     gate_column = from_spare(received).reshape(experts_all * ROWS, 1)
     rows_in = received.reshape(experts_all * ROWS, model_width)
 
@@ -268,7 +387,7 @@
     gain_two_part = jnp.sum(grad_mixed * middle * inv_rms_two, axis=0)
 
     grad_attn_seq = gather_tensor(grad_middle.astype(jnp.bfloat16), place)
-    output_grad_turned = dot(grad_attn_seq, attended, 0, 0)
+    output_grad_turned = dot(grad_attn_seq, attended, 0, 1)
     router_high, router_low = split_two(router_part)
     gain_high, gain_low = split_two(gain_two_part)
     output_joined = jnp.concatenate(
@@ -289,61 +408,9 @@
     )
     output_weight_grad = output_all[:, :query_width].T
 
-    grad_attended = dot(grad_attn_seq, output_weight, 1, 1).astype(jnp.bfloat16)
-    grad_blocks = grad_attended.reshape(
-        block_count, rows_per_block, kv_heads, group_width, head_width
-    )
-
-    def backward_block(totals, operands):
-        key_total, value_total = totals
-        query_piece, grad_piece, row_start, log_total = operands
-        attn_probs = jnp.exp(masked_scores(query_piece, row_start) - log_total)
-        value_total = value_total + jnp.einsum(
-            "hgqs,qhgd->shd",
-            attn_probs.astype(jnp.bfloat16),
-            grad_piece,
-            preferred_element_type=jnp.float32,
-        )
-        grad_probs = jnp.einsum(
-            "qhgd,shd->hgqs", grad_piece, values_low, preferred_element_type=jnp.float32
-        )
-        row_inner = jnp.sum(attn_probs * grad_probs, axis=-1, keepdims=True)
-        grad_scores = (attn_probs * (grad_probs - row_inner)).astype(jnp.bfloat16)
-        query_grad = (
-            jnp.einsum("hgqs,shd->qhgd", grad_scores, keys_low, preferred_element_type=jnp.float32)
-            * factor
-        )
-        key_total = (
-            key_total
-            + jnp.einsum(
-                "hgqs,qhgd->shd", grad_scores, query_piece, preferred_element_type=jnp.float32
-            )
-            * factor
-        )
-        return ((key_total, value_total), query_grad)
-
-    zero_keys = jnp.zeros((sequence_length, kv_heads, head_width), jnp.float32)
-    (key_grad, value_grad), query_grads = lax.scan(
-        backward_block,
-        (zero_keys, zero_keys),
-        (query_block_list, grad_blocks, block_starts, log_totals),
-    )
-    query_grad_back = apply_rotary(
-        query_grads.reshape(sequence_length, local_heads, head_width),
-        cosine_table,
-        sine_table,
-        -1.0,
-    )
-    key_grad_back = apply_rotary(key_grad, cosine_table, sine_table, -1.0)
-    grad_projected = jnp.concatenate(
-        [
-            query_grad_back.reshape(sequence_length, query_width),
-            key_grad_back.reshape(sequence_length, keyval_width),
-            value_grad.reshape(sequence_length, keyval_width),
-        ],
-        axis=1,
-    ).astype(jnp.bfloat16)
-    joined_grad = dot(sequence, grad_projected, 0, 0).astype(bf16)
+    grad_attended = dot(output_weight, grad_attn_seq, 1, 1).astype(bf16)
+    grad_projected = attend_back(turned, attended, grad_attended, log_totals, cos, sin)
+    joined_grad = dot(sequence, grad_projected, 0, 1).astype(bf16)
     joined_all = jnp.sum(
         exchange(joined_grad.reshape(dp_size, dp_rows, query_width + 2 * keyval_width)).astype(f32),
         axis=0,
@@ -353,8 +420,8 @@
 
     def normed_chunk(k):
         start = lax.rem(place + k, 4) * local_rows
-        piece = lax.dynamic_slice_in_dim(grad_projected, start, local_rows, 0)
-        return dot(piece, joined_weight, 1, 1)
+        piece = lax.dynamic_slice_in_dim(grad_projected, start, local_rows, 1)
+        return dot(piece, weight_turned, 0, 0)
 
     grad_normed = scatter_tensor(normed_chunk)
     tokens_grad = grad_middle + norm_back(inputs, inv_rms_one, norm_gains[0], grad_normed)

time: 757 us -> 577 us (0.76)
  waiting for transfers between devices: 285 us -> 141 us
  blocking collectives: 0 us -> 105 us
  matrix products: 165 us -> 110 us
  local copies, waits for them, and re-layouts: 95.1 us -> 40.5 us
  other arithmetic: 59.9 us -> 24.6 us
  Pallas kernels: 0 us -> 25.5 us
  starting transfers between devices: 128 us -> 104 us
    all_to_all x6 -> x5, waiting for transfers between devices: 226 us -> 91.5 us  [exchange(): return lax.all_to_all(values, 'dp', split_axis=0, concat_axis=0, tiled=True)]
    all_to_all x0 -> x1, blocking collectives: none -> 105 us  [exchange(): return lax.all_to_all(values, 'dp', split_axis=0, concat_axis=0, tiled=True)]
    dot_general x15 -> x0, matrix products: 53.7 us -> none  [the longest x2 15.4 us: backward_block(): jnp.einsum('qhgd,shd->hgqs', grad_piece, values_low, preferred_element_ty...]
    all_to_all x6 -> x5, starting transfers between devices: 99.9 us -> 66.9 us  [exchange(): return lax.all_to_all(values, 'dp', split_axis=0, concat_axis=0, tiled=True)]
    dynamic_update_slice x4 -> x0, local copies, waits for them, and re-layouts: 31.6 us -> none  [per_device(): lax.scan(backward_block, (zero_keys, zero_keys), (query_block_list, grad_...]
    pallas_call x0 -> x2, Pallas kernels: none -> 25.5 us  [the longest x1 15.3 us: attend_back(): pl.pallas_call(attend_back_kernel, grid=(KEY_LOCAL, GROUP), in_specs=[hea...]
    convert_element_type x3 -> x1, other arithmetic: 13.6 us -> 0.01 us  [rotary_tables(): jnp.arange(sequence_length).astype(jnp.float32)[None, :]]
    ppermute x16, waiting for transfers between devices: 56.4 us -> 47.1 us  [shift_tensor(): lax.ppermute(values, 'tensor', [(i, (i + step) % 4) for i in range(4)])]
  transfers between devices with their start and end apart: 25 -> 24, of which waited for: 16 -> 13; matrix products, arithmetic and copies ran while one was open for 30% -> 21% of each run, Pallas kernels for 0% -> 5%
where the time goes in v2:
time: 577 us; the launch traced here: 567 us
  waiting for transfers between devices  141 us (24%)
  matrix products  110 us (19%)
  blocking collectives  105 us (18%)
  starting transfers between devices  104 us (18%)
  local copies, waits for them, and re-layouts  40.5 us (7%)
  Pallas kernels  25.5 us (4%)
  other arithmetic  24.6 us (4%)
  between operations  15.4 us (3%)
    dot_general x26, matrix products, dot(): lax.dot_general(a, b, (((ca,), (cb,)), ((), ())), preferred_element_type=...  110 us
    all_to_all x1, blocking collectives, exchange(): return lax.all_to_all(values, 'dp', split_axis=0, concat_axis=0, tiled=True)  105 us
    all_to_all x5, waiting for transfers between devices, exchange(): return lax.all_to_all(values, 'dp', split_axis=0, concat_axis=0, tiled=True)  91.5 us
    all_to_all x5, starting transfers between devices, exchange(): return lax.all_to_all(values, 'dp', split_axis=0, concat_axis=0, tiled=True)  66.9 us
    ppermute x16, waiting for transfers between devices, shift_tensor(): lax.ppermute(values, 'tensor', [(i, (i + step) % 4) for i in range(4)])  47.1 us
    ppermute x16, starting transfers between devices, shift_tensor(): lax.ppermute(values, 'tensor', [(i, (i + step) % 4) for i in range(4)])  33.6 us
    pallas_call x1, Pallas kernels, attend_back(): pl.pallas_call(attend_back_kernel, grid=(KEY_LOCAL, GROUP), in_specs=[hea...  15.3 us
    unnamed x123, local copies, waits for them, and re-layouts  13.1 us
  transfers between devices with their start and end apart: 24, of which 13 were waited for; matrix products, arithmetic and copies ran while one was open for 21% of the time, Pallas kernels for 5%

profile of v2, /device:TPU:1, one launch (start us, length us, event | category | flops | bytes accessed | tf_op | source)
XLA Modules:
  0.0 566.6 jit_solution(17706808130726275052)
XLA Ops:
  24.9 9.6 %all-to-all-start = ((bf16[32,72,1536]{2,1,0:T(8,128)(2,1)}), bf16[32,72,1536]{2,1,0:T(8,128)(2,1)}, u32[]{:S(2)}, u32[]{:S(2)}) async-start(bf16[32,72,1536]{2,1,0:T(8,128)(2,1)} %bitcast.107), calls=%async_computation | async-start | bytes 14155776 | tf_op jit(solution)/shard_map/all_to_all | solution.py:97
  53.4 10.3 %attend.1 = (bf16[384,1024]{1,0:T(8,128)(2,1)S(1)}, f32[6,1,1024]{2,1,0:T(1,128)S(1)}, bf16[640,1024]{1,0:T(8,128)(2,1)S(1)}) custom-call(f32[640,1024]{1,0:T(8,128)S(1)} %fusion.102.q_ref.k_ref.v_ref, f32[640,1024]{1,0:T(8,128)S(1)} %fusion.102.q_ref.k_ref.v_ref, f32[640,1024]{1,0:T(8,128)S(1)} %fusion.102.q_ref.k_ref.v_ref, ...), custom_call_target="tpu_custom_call" | custom-call | flops 1207959552 | bytes 3932160 | tf_op jit(solution)/shard_map/attend/pallas_call | solution.py:210
  65.9 13.3 %collective-permute-start.6 = (bf16[128,1536]{1,0:T(8,128)(2,1)S(1)}, bf16[128,1536]{1,0:T(8,128)(2,1)S(1)}, u32[]{:S(2)}, u32[]{:S(2)}) collective-permute-start(bf16[128,1536]{1,0:T(8,128)(2,1)S(1)} %get-tuple-element.66), channel_id=1, source_target_pairs={{0,3},{1,0},{2,1},{3,2},{4,7},{5,4},{6,5},{7,6},{8,11},{9,8},{10,9... | collective-permute-start | bytes 1179656 | tf_op jit(solution)/shard_map/ppermute | solution.py:59
  80.1 6.2 %collective-permute-done.6 = bf16[128,1536]{1,0:T(8,128)(2,1)S(1)} collective-permute-done((bf16[128,1536]{1,0:T(8,128)(2,1)S(1)}, bf16[128,1536]{1,0:T(8,128)(2,1)S(1)}, u32[]{:S(2)}, u32[]{:S(2)}) %collective-permute-start.6) | collective-permute-done | bytes 393248 | tf_op jit(solution)/shard_map/ppermute | solution.py:59
  90.6 8.2 %collective-permute-done.5 = bf16[256,1536]{1,0:T(8,128)(2,1)S(1)} collective-permute-done((bf16[256,1536]{1,0:T(8,128)(2,1)S(1)}, bf16[256,1536]{1,0:T(8,128)(2,1)S(1)}, u32[]{:S(2)}, u32[]{:S(2)}) %collective-permute-start.5) | collective-permute-done | bytes 786464 | tf_op jit(solution)/shard_map/ppermute | solution.py:59
  112.1 10.0 %all-to-all-done = bf16[32,72,1536]{2,1,0:T(8,128)(2,1)} async-done(((bf16[32,72,1536]{2,1,0:T(8,128)(2,1)}), bf16[32,72,1536]{2,1,0:T(8,128)(2,1)}, u32[]{:S(2)}, u32[]{:S(2)}) %all-to-all-start) | async-done | bytes 7077920 | tf_op jit(solution)/shard_map/all_to_all | solution.py:97
  122.1 105.1 %all_to_all.35 = bf16[32,72,1536]{2,1,0:T(8,128)(2,1)S(1)} all-to-all(bf16[32,72,1536]{2,1,0:T(8,128)(2,1)} %select_convert_fusion.1), channel_id=1, replica_groups=mesh['dp'=32,'tensor'=4] {'dp'}, dimensions={0} | all-to-all | bytes 14155776 | tf_op jit(solution)/shard_map/all_to_all | solution.py:97
  230.3 10.0 %fusion.16 = f32[2304,1024]{1,0:T(8,128)S(1)} fusion(bf16[2304,1536]{1,0:T(8,128)(2,1)} %bitcast.108, bf16[1,1536,1024]{2,1,0:T(8,128)(2,1)S(1)} %copy-done), kind=kOutput, calls=%fused_computation.28 | convolution fusion | flops 7247757312 | bytes 19660800 | tf_op jit(solution)/shard_map/dot_general | solution.py:30
  240.3 11.7 %multiply_convert_fusion.1 = (bf16[2304,512]{1,0:T(8,128)(2,1)}, bf16[2304,512]{1,0:T(8,128)(2,1)}, f32[2304]{0:T(1024)}, f32[2304,512]{1,0:T(8,128)}) fusion(f32[2304,1024]{1,0:T(8,128)S(1)} %fusion.16, f32[2304]{0:T(1024)S(1)} %add.183, bf16[2304,1536]{1,0:T(8,128)(2,1)} %bitcast.5, bf16[1,512,1536]{2,1,0:T(8,128)(2,1)S(1)} %copy-done.55), kind=kOutput, calls=%fused_computation.19 | convolution fusion | flops 3645110016 | bytes 27543552 | tf_op jit(solution)/shard_map/dot_general | solution.py:30
  252.9 12.3 %select_convert_fusion = bf16[32,72,1536]{2,1,0:T(8,128)(2,1)} fusion(bf16[32,1536]{1,0:T(8,128)(2,1)S(1)} %pad.20, bf16[32,1536]{1,0:T(8,128)(2,1)S(1)} %pad.19, pred[72]{0:T(512)(128)(4,1)} %copy-done.58, pred[72]{0:T(512)(128)(4,1)} %copy-done.59, bf16[32,72,512]{2,1,0:T(8,128)(2,1)} %bitcast.119, bf16[32,72,512]{2,1,0:T(8,128)(2,1)} %bitcast.118, ...), kind=kOutput, calls=%fused_computation | convolution fusion | flops 7264272384 | bytes 15138960 | tf_op jit(solution)/shard_map/dot_general | solution.py:30
  270.3 9.6 %convolution_convert_fusion.3 = bf16[1536,512]{1,0:T(8,128)(2,1)} fusion(bf16[2304,1536]{1,0:T(8,128)(2,1)} %bitcast.5, f32[2304,512]{1,0:T(8,128)} %get-tuple-element.62, f32[2304]{0:T(1024)S(1)} %copy-done.42), kind=kOutput, calls=%fused_computation.36 | convolution fusion | flops 3627024384 | bytes 13378560 | tf_op jit(solution)/shard_map/dot_general | solution.py:30
  280.0 11.7 %fusion.12 = bf16[1536,1024]{1,0:T(8,128)(2,1)} fusion(bf16[2304,1536]{1,0:T(8,128)(2,1)} %bitcast.109, bf16[2304,512]{1,0:T(8,128)(2,1)} %get-tuple-element.60, bf16[2304,512]{1,0:T(8,128)(2,1)S(1)} %copy-done.57), kind=kOutput, calls=%fused_computation.25 | convolution fusion | flops 7258767360 | bytes 14942208 | tf_op jit(solution)/shard_map/dot_general | solution.py:30
  293.8 8.4 %convolution_convert_fusion = bf16[2304,1536]{1,0:T(8,128)(2,1)} fusion(bf16[1,512,1536]{2,1,0:T(8,128)(2,1)S(1)} %copy-done.56, f32[2304,512]{1,0:T(8,128)} %get-tuple-element.62, f32[2304]{0:T(1024)S(1)} %copy-done.42), kind=kOutput, calls=%fused_computation.2 | convolution fusion | flops 3629776896 | bytes 13378560 | tf_op jit(solution)/shard_map/dot_general | solution.py:30
  302.2 55.5 %all-to-all-done.3 = bf16[32,72,1536]{2,1,0:T(8,128)(2,1)} async-done(((bf16[32,72,1536]{2,1,0:T(8,128)(2,1)}), bf16[32,72,1536]{2,1,0:T(8,128)(2,1)}, u32[]{:S(2)}, u32[]{:S(2)}) %all-to-all-start.3) | async-done | bytes 7077920 | tf_op jit(solution)/shard_map/all_to_all | solution.py:97
  357.7 24.0 %all-to-all-start.2 = ((bf16[32,72,1536]{2,1,0:T(8,128)(2,1)}), bf16[32,72,1536]{2,1,0:T(8,128)(2,1)}, u32[]{:S(2)}, u32[]{:S(2)}) async-start(bf16[32,72,1536]{2,1,0:T(8,128)(2,1)} %bitcast.110), calls=%async_computation.2 | async-start | bytes 14155776 | tf_op jit(solution)/shard_map/all_to_all | solution.py:97
  407.7 7.9 %collective-permute-done.8 = bf16[256,1536]{1,0:T(8,128)(2,1)S(1)} collective-permute-done((bf16[256,1536]{1,0:T(8,128)(2,1)}, bf16[256,1536]{1,0:T(8,128)(2,1)S(1)}, u32[]{:S(2)}, u32[]{:S(2)}) %collective-permute-start.8) | collective-permute-done | bytes 786464 | tf_op jit(solution)/shard_map/ppermute | solution.py:59
  420.4 6.4 %collective-permute-done.10 = bf16[128,1536]{1,0:T(8,128)(2,1)S(1)} collective-permute-done((bf16[128,1536]{1,0:T(8,128)(2,1)S(1)}, bf16[128,1536]{1,0:T(8,128)(2,1)S(1)}, u32[]{:S(2)}, u32[]{:S(2)}) %collective-permute-start.10) | collective-permute-done | bytes 393248 | tf_op jit(solution)/shard_map/ppermute | solution.py:59
  431.9 15.3 %attend_back.1 = bf16[640,1024]{1,0:T(8,128)(2,1)S(1)} custom-call(bf16[640,1024]{1,0:T(8,128)(2,1)S(1)} %copy-done.5, bf16[640,1024]{1,0:T(8,128)(2,1)S(1)} %copy-done.5, bf16[640,1024]{1,0:T(8,128)(2,1)S(1)} %copy-done.5, bf16[384,1024]{1,0:T(8,128)(2,1)S(1)} %copy-done.3, bf16[384,1024]{1,0:T(8,128)(2,1)S(1)} %fusion.42.grad_ref, ...), custom_call_target="tpu_custom_call" | custom-call | flops 2818572288 | bytes 3932160 | tf_op jit(solution)/shard_map/attend_back/pallas_call | solution.py:244
  462.7 6.5 %all-to-all-done.2 = bf16[32,72,1536]{2,1,0:T(8,128)(2,1)} async-done(((bf16[32,72,1536]{2,1,0:T(8,128)(2,1)}), bf16[32,72,1536]{2,1,0:T(8,128)(2,1)}, u32[]{:S(2)}, u32[]{:S(2)}) %all-to-all-start.2) | async-done | bytes 7077920 | tf_op jit(solution)/shard_map/all_to_all | solution.py:97
  469.2 23.6 %all-to-all-start.4 = ((bf16[32,48,512]{2,1,0:T(8,128)(2,1)}), bf16[32,48,512]{2,1,0:T(8,128)(2,1)}, u32[]{:S(2)}, u32[]{:S(2)}) async-start(bf16[32,48,512]{2,1,0:T(8,128)(2,1)} %concatenate.60), calls=%async_computation.4 | async-start | bytes 3145728 | tf_op jit(solution)/shard_map/all_to_all | solution.py:97
  497.9 7.0 %collective-permute-done.14 = bf16[128,1536]{1,0:T(8,128)(2,1)S(1)} collective-permute-done((bf16[128,1536]{1,0:T(8,128)(2,1)S(1)}, bf16[128,1536]{1,0:T(8,128)(2,1)S(1)}, u32[]{:S(2)}, u32[]{:S(2)}) %collective-permute-start.14) | collective-permute-done | bytes 393248 | tf_op jit(solution)/shard_map/ppermute | solution.py:59
  508.4 7.1 %all-to-all-done.4 = bf16[32,48,512]{2,1,0:T(8,128)(2,1)} async-done(((bf16[32,48,512]{2,1,0:T(8,128)(2,1)}), bf16[32,48,512]{2,1,0:T(8,128)(2,1)}, u32[]{:S(2)}, u32[]{:S(2)}) %all-to-all-start.4) | async-done | bytes 1572896 | tf_op jit(solution)/shard_map/all_to_all | solution.py:97
  520.5 6.5 %fusion.27 = bf16[256,1536]{1,0:T(8,128)(2,1)} fusion(f32[256,1536]{1,0:T(8,128)} %copy-done.9, bf16[32,72,1536]{2,1,0:T(8,128)(2,1)} %all-to-all-done.2, f32[32,256]{1,0:T(8,128)S(1)} %convolution_select_fusion, f32[72]{0:T(128)S(1)} %copy-done.51), kind=kOutput, calls=%fused_computation.44 | convolution fusion | flops 1813315584 | bytes 9470240 | tf_op jit(solution)/shard_map/dot_general | solution.py:30
  535.2 12.4 %all-to-all-done.5 = bf16[32,48,640]{2,1,0:T(8,128)(2,1)} async-done(((bf16[32,48,640]{2,1,0:T(8,128)(2,1)}), bf16[32,48,640]{2,1,0:T(8,128)(2,1)}, u32[]{:S(2)}, u32[]{:S(2)}) %all-to-all-start.5) | async-done | bytes 1966112 | tf_op jit(solution)/shard_map/all_to_all | solution.py:97
  (275 shorter events, 153.0 us)
Async XLA Ops:
  14.5 23.4 %collective-permute-start = (bf16[256,1536]{1,0:T(8,128)(2,1)}, bf16[256,1536]{1,0:T(8,128)(2,1)}, u32[]{:S(2)}, u32[]{:S(2)}) collective-permute-start(bf16[256,1536]{1,0:T(8,128)(2,1)} %get-tuple-element.58), channel_id=1, source_target_pairs={{0,1},{1,2},{2,3},{3,0},{4,5},{5,6},{6,7},{7,4},{8,9},{9,10},{10,1... | collective-permute-start | bytes 2359304 | tf_op jit(solution)/shard_map/ppermute | solution.py:59
  16.6 22.8 %collective-permute-start.1 = (bf16[256,1536]{1,0:T(8,128)(2,1)}, bf16[256,1536]{1,0:T(8,128)(2,1)}, u32[]{:S(2)}, u32[]{:S(2)}) collective-permute-start(bf16[256,1536]{1,0:T(8,128)(2,1)} %get-tuple-element.58), channel_id=1, source_target_pairs={{0,3},{1,0},{2,1},{3,2},{4,7},{5,4},{6,5},{7,6},{8,11},{9,8},{10,9... | collective-permute-start | bytes 2359304 | tf_op jit(solution)/shard_map/ppermute | solution.py:59
  24.9 97.2 %all-to-all-start = ((bf16[32,72,1536]{2,1,0:T(8,128)(2,1)}), bf16[32,72,1536]{2,1,0:T(8,128)(2,1)}, u32[]{:S(2)}, u32[]{:S(2)}) async-start(bf16[32,72,1536]{2,1,0:T(8,128)(2,1)} %bitcast.107), calls=%async_computation | async-start | bytes 14155776 | tf_op jit(solution)/shard_map/all_to_all | solution.py:97
  39.3 11.8 %collective-permute-start.2 = (bf16[128,1536]{1,0:T(8,128)(2,1)S(1)}, bf16[128,1536]{1,0:T(8,128)(2,1)S(1)}, u32[]{:S(2)}, u32[]{:S(2)}) collective-permute-start(bf16[128,1536]{1,0:T(8,128)(2,1)S(1)} %slice.143), channel_id=1, source_target_pairs={{0,1},{1,2},{2,3},{3,0},{4,5},{5,6},{6,7},{7,4},{8,9},{9,10},{10,1... | collective-permute-start | bytes 1179656 | tf_op jit(solution)/shard_map/ppermute | solution.py:59
  40.4 10.7 %collective-permute-start.3 = (bf16[128,1536]{1,0:T(8,128)(2,1)S(1)}, bf16[128,1536]{1,0:T(8,128)(2,1)S(1)}, u32[]{:S(2)}, u32[]{:S(2)}) collective-permute-start(bf16[128,1536]{1,0:T(8,128)(2,1)S(1)} %slice.144), channel_id=1, source_target_pairs={{0,3},{1,0},{2,1},{3,2},{4,7},{5,4},{6,5},{7,6},{8,11},{9,8},{10,9... | collective-permute-start | bytes 1179656 | tf_op jit(solution)/shard_map/ppermute | solution.py:59
  64.4 15.5 %collective-permute-start.4 = (bf16[128,1536]{1,0:T(8,128)(2,1)S(1)}, bf16[128,1536]{1,0:T(8,128)(2,1)S(1)}, u32[]{:S(2)}, u32[]{:S(2)}) collective-permute-start(bf16[128,1536]{1,0:T(8,128)(2,1)S(1)} %get-tuple-element.65), channel_id=1, source_target_pairs={{0,1},{1,2},{2,3},{3,0},{4,5},{5,6},{6,7},{7,4},{8,9},{9,10},{10,1... | collective-permute-start | bytes 1179656 | tf_op jit(solution)/shard_map/ppermute | solution.py:59
  65.9 20.4 %collective-permute-start.6 = (bf16[128,1536]{1,0:T(8,128)(2,1)S(1)}, bf16[128,1536]{1,0:T(8,128)(2,1)S(1)}, u32[]{:S(2)}, u32[]{:S(2)}) collective-permute-start(bf16[128,1536]{1,0:T(8,128)(2,1)S(1)} %get-tuple-element.66), channel_id=1, source_target_pairs={{0,3},{1,0},{2,1},{3,2},{4,7},{5,4},{6,5},{7,6},{8,11},{9,8},{10,9... | collective-permute-start | bytes 1179656 | tf_op jit(solution)/shard_map/ppermute | solution.py:59
  80.0 18.8 %collective-permute-start.5 = (bf16[256,1536]{1,0:T(8,128)(2,1)S(1)}, bf16[256,1536]{1,0:T(8,128)(2,1)S(1)}, u32[]{:S(2)}, u32[]{:S(2)}) collective-permute-start(bf16[256,1536]{1,0:T(8,128)(2,1)S(1)} %pad_maximum_fusion), channel_id=1, source_target_pairs={{0,1},{1,2},{2,3},{3,0},{4,5},{5,6},{6,7},{7,4},{8,9},{9,10},{10,1... | collective-permute-start | bytes 2359304 | tf_op jit(solution)/shard_map/ppermute | solution.py:59
  86.4 18.3 %collective-permute-start.7 = (bf16[256,1536]{1,0:T(8,128)(2,1)S(1)}, bf16[256,1536]{1,0:T(8,128)(2,1)S(1)}, u32[]{:S(2)}, u32[]{:S(2)}) collective-permute-start(bf16[256,1536]{1,0:T(8,128)(2,1)S(1)} %pad_maximum_fusion.1), channel_id=1, source_target_pairs={{0,3},{1,0},{2,1},{3,2},{4,7},{5,4},{6,5},{7,6},{8,11},{9,8},{10,9... | collective-permute-start | bytes 2359304 | tf_op jit(solution)/shard_map/ppermute | solution.py:59
  265.2 92.5 %all-to-all-start.3 = ((bf16[32,72,1536]{2,1,0:T(8,128)(2,1)}), bf16[32,72,1536]{2,1,0:T(8,128)(2,1)}, u32[]{:S(2)}, u32[]{:S(2)}) async-start(bf16[32,72,1536]{2,1,0:T(8,128)(2,1)} %select_convert_fusion), calls=%async_computation.3 | async-start | bytes 14155776 | tf_op jit(solution)/shard_map/all_to_all | solution.py:97
  270.0 127.7 %reduce-scatter.5.cloned.1.call-start = ((), (), s32[]{:S(2)}) async-start(), calls=%async_computation.10 | async-start | bytes 1966080 | tf_op jit(solution)/shard_map/reduce_scatter | solution.py:376
  279.9 120.1 %reduce-scatter.3.cloned.1.call-start = ((), (), s32[]{:S(2)}) async-start(), calls=%async_computation.9 | async-start | bytes 3932160 | tf_op jit(solution)/shard_map/reduce_scatter | solution.py:375
  357.7 111.5 %all-to-all-start.2 = ((bf16[32,72,1536]{2,1,0:T(8,128)(2,1)}), bf16[32,72,1536]{2,1,0:T(8,128)(2,1)}, u32[]{:S(2)}, u32[]{:S(2)}) async-start(bf16[32,72,1536]{2,1,0:T(8,128)(2,1)} %bitcast.110), calls=%async_computation.2 | async-start | bytes 14155776 | tf_op jit(solution)/shard_map/all_to_all | solution.py:97
  395.1 20.5 %collective-permute-start.8 = (bf16[256,1536]{1,0:T(8,128)(2,1)}, bf16[256,1536]{1,0:T(8,128)(2,1)S(1)}, u32[]{:S(2)}, u32[]{:S(2)}) collective-permute-start(bf16[256,1536]{1,0:T(8,128)(2,1)} %get-tuple-element.51), channel_id=1, source_target_pairs={{0,1},{1,2},{2,3},{3,0},{4,5},{5,6},{6,7},{7,4},{8,9},{9,10},{10,1... | collective-permute-start | bytes 2359304 | tf_op jit(solution)/shard_map/ppermute | solution.py:59
  395.1 20.6 %collective-permute-start.9 = (bf16[256,1536]{1,0:T(8,128)(2,1)}, bf16[256,1536]{1,0:T(8,128)(2,1)S(1)}, u32[]{:S(2)}, u32[]{:S(2)}) collective-permute-start(bf16[256,1536]{1,0:T(8,128)(2,1)} %get-tuple-element.51), channel_id=1, source_target_pairs={{0,3},{1,0},{2,1},{3,2},{4,7},{5,4},{6,5},{7,6},{8,11},{9,8},{10,9... | collective-permute-start | bytes 2359304 | tf_op jit(solution)/shard_map/ppermute | solution.py:59
  415.6 11.2 %collective-permute-start.10 = (bf16[128,1536]{1,0:T(8,128)(2,1)S(1)}, bf16[128,1536]{1,0:T(8,128)(2,1)S(1)}, u32[]{:S(2)}, u32[]{:S(2)}) collective-permute-start(bf16[128,1536]{1,0:T(8,128)(2,1)S(1)} %slice.157), channel_id=1, source_target_pairs={{0,1},{1,2},{2,3},{3,0},{4,5},{5,6},{6,7},{7,4},{8,9},{9,10},{10,1... | collective-permute-start | bytes 1179656 | tf_op jit(solution)/shard_map/ppermute | solution.py:59
  415.8 11.8 %collective-permute-start.11 = (bf16[128,1536]{1,0:T(8,128)(2,1)S(1)}, bf16[128,1536]{1,0:T(8,128)(2,1)S(1)}, u32[]{:S(2)}, u32[]{:S(2)}) collective-permute-start(bf16[128,1536]{1,0:T(8,128)(2,1)S(1)} %slice.158), channel_id=1, source_target_pairs={{0,3},{1,0},{2,1},{3,2},{4,7},{5,4},{6,5},{7,6},{8,11},{9,8},{10,9... | collective-permute-start | bytes 1179656 | tf_op jit(solution)/shard_map/ppermute | solution.py:59
  449.0 46.7 %collective-permute-start.12 = (bf16[128,1536]{1,0:T(8,128)(2,1)}, bf16[128,1536]{1,0:T(8,128)(2,1)}, u32[]{:S(2)}, u32[]{:S(2)}) collective-permute-start(bf16[128,1536]{1,0:T(8,128)(2,1)} %get-tuple-element.63), channel_id=1, source_target_pairs={{0,1},{1,2},{2,3},{3,0},{4,5},{5,6},{6,7},{7,4},{8,9},{9,10},{10,1... | collective-permute-start | bytes 1179656 | tf_op jit(solution)/shard_map/ppermute | solution.py:59
  469.2 46.3 %all-to-all-start.4 = ((bf16[32,48,512]{2,1,0:T(8,128)(2,1)}), bf16[32,48,512]{2,1,0:T(8,128)(2,1)}, u32[]{:S(2)}, u32[]{:S(2)}) async-start(bf16[32,48,512]{2,1,0:T(8,128)(2,1)} %concatenate.60), calls=%async_computation.4 | async-start | bytes 3145728 | tf_op jit(solution)/shard_map/all_to_all | solution.py:97
  494.2 10.6 %collective-permute-start.14 = (bf16[128,1536]{1,0:T(8,128)(2,1)S(1)}, bf16[128,1536]{1,0:T(8,128)(2,1)S(1)}, u32[]{:S(2)}, u32[]{:S(2)}) collective-permute-start(bf16[128,1536]{1,0:T(8,128)(2,1)S(1)} %copy-done.32), channel_id=1, source_target_pairs={{0,3},{1,0},{2,1},{3,2},{4,7},{5,4},{6,5},{7,6},{8,11},{9,8},{10,9... | collective-permute-start | bytes 1179656 | tf_op jit(solution)/shard_map/ppermute | solution.py:59
  497.7 29.4 %collective-permute-start.13 = (bf16[256,1536]{1,0:T(8,128)(2,1)}, bf16[256,1536]{1,0:T(8,128)(2,1)}, u32[]{:S(2)}, u32[]{:S(2)}) collective-permute-start(bf16[256,1536]{1,0:T(8,128)(2,1)} %pad_maximum_fusion.2), channel_id=1, source_target_pairs={{0,1},{1,2},{2,3},{3,0},{4,5},{5,6},{6,7},{7,4},{8,9},{9,10},{10,1... | collective-permute-start | bytes 2359304 | tf_op jit(solution)/shard_map/ppermute | solution.py:59
  505.9 21.1 %collective-permute-start.15 = (bf16[256,1536]{1,0:T(8,128)(2,1)}, bf16[256,1536]{1,0:T(8,128)(2,1)}, u32[]{:S(2)}, u32[]{:S(2)}) collective-permute-start(bf16[256,1536]{1,0:T(8,128)(2,1)} %pad_maximum_fusion.3), channel_id=1, source_target_pairs={{0,3},{1,0},{2,1},{3,2},{4,7},{5,4},{6,5},{7,6},{8,11},{9,8},{10,9... | collective-permute-start | bytes 2359304 | tf_op jit(solution)/shard_map/ppermute | solution.py:59
  515.5 32.0 %all-to-all-start.5 = ((bf16[32,48,640]{2,1,0:T(8,128)(2,1)}), bf16[32,48,640]{2,1,0:T(8,128)(2,1)}, u32[]{:S(2)}, u32[]{:S(2)}) async-start(bf16[32,48,640]{2,1,0:T(8,128)(2,1)} %bitcast.111), calls=%async_computation.5 | async-start | bytes 3932160 | tf_op jit(solution)/shard_map/all_to_all | solution.py:97
  551.3 7.5 %all-to-all-start.6 = ((f32[4,16,128]{2,1,0:T(8,128)}), f32[4,16,128]{2,1,0:T(8,128)S(1)}, u32[]{:S(2)}, u32[]{:S(2)}) async-start(f32[4,16,128]{2,1,0:T(8,128)} %pad.21), calls=%async_computation.6 | async-start | bytes 65536 | tf_op jit(solution)/shard_map/all_to_all | solution.py:443
  (60 other events, 644.7 us)
Sparse Core Ops, SparseCore 0:
  280.0 24.2 reduce-scatter.4
  306.7 38.9 reduce-scatter.2

commit v3 on v2

v3 whole, which is shorter than its diff:
```python
import jax
import jax.numpy as jnp
from jax import lax
from jax.experimental import pallas as pl
from jax.experimental.pallas import tpu as pltpu
from jax.sharding import PartitionSpec as P

QUERY_HEADS = 24
KEY_VALUE_HEADS = 8
HEAD_DIM = 64
FF = 512
CAP = 68
ROWS = 72
PAIR = 2 * ROWS
LINE = 4 * PAIR
HALF = 768
EXTRA = 128


epsilon = 1e-06
theta = 10000.0
BLOCK = 256
GROUP = QUERY_HEADS // KEY_VALUE_HEADS
QUERY_LOCAL = QUERY_HEADS // 4
KEY_LOCAL = KEY_VALUE_HEADS // 4
FACTOR = HEAD_DIM**-0.5
SCALE = FACTOR * 1.4426950408889634
highest = lax.Precision.HIGHEST
BRIEF = pl.CostEstimate(flops=1, bytes_accessed=1, transcendentals=0)
LONG = pl.CostEstimate(flops=10**11, bytes_accessed=1, transcendentals=0)
VMEM_LIMIT = 56 * 2**20
f32 = jnp.float32
bf16 = jnp.bfloat16


def dot(a, b, ca, cb, precision=None):
    return lax.dot_general(
        a, b, (((ca,), (cb,)), ((), ())), preferred_element_type=f32, precision=precision
    )


def inverse_rms(values):
    return lax.rsqrt(jnp.mean(values * values, axis=-1, keepdims=True) + epsilon)


def norm_rows(values, gain_row):
    inv_rms = inverse_rms(values)
    return (values * inv_rms * gain_row, inv_rms)


def norm_back(values, inv_rms, gain_row, upstream):
    scaled = upstream * gain_row
    inner_sum = jnp.mean(scaled * values, axis=-1, keepdims=True)
    return inv_rms * scaled - values * (inv_rms * inv_rms * inv_rms) * inner_sum


def rotary_tables(sequence_length, head_width):
    half_width = head_width // 2
    freqs = theta ** (-(jnp.arange(half_width).astype(jnp.float32) * 2.0 / head_width))
    angles = freqs[:, None] * jnp.arange(sequence_length).astype(jnp.float32)[None, :]
    return (jnp.cos(angles), jnp.sin(angles))


def split_two(values):
    high = lax.reduce_precision(values, 8, 7)
    return high, values - high


def shift_tensor(values, step):
    return lax.ppermute(values, "tensor", [(i, (i + step) % 4) for i in range(4)])


def gather_near(mine, halves):
    if not halves:
        return shift_tensor(mine, 1), shift_tensor(mine, -1)
    half = mine.shape[0] // 2
    top, low = mine[:half], mine[half:]
    left_top, right_low = shift_tensor(top, 1), shift_tensor(low, -1)
    return left_top, right_low, shift_tensor(low, 1), shift_tensor(top, -1)


def gather_far(mine, near, place):
    rows = mine.shape[0]
    half = rows // 2
    if len(near) == 2:
        left, right = near
        far = shift_tensor(left[:half], 1), shift_tensor(right[half:], -1)
        pieces = [(mine, 0, 0), (left, 3, 0), (right, 1, 0)]
    else:
        far = shift_tensor(near[0], 1), shift_tensor(near[1], -1)
        pieces = [(mine, 0, 0), (near[0], 3, 0), (near[2], 3, half)]
        pieces += [(near[3], 1, 0), (near[1], 1, half)]
    pieces += [(far[0], 2, 0), (far[1], 2, half)]
    return [
        (piece, lax.rem(place + owner, 4) * rows + offset) for piece, owner, offset in pieces
    ]


def scatter_far(chunk):
    far = chunk(2).astype(bf16)
    half = far.shape[0] // 2
    return shift_tensor(far[:half], 1), shift_tensor(far[half:], -1)


def scatter_plain(chunk):
    right, left = chunk(1), chunk(3)
    half = right.shape[0] // 2
    return shift_tensor(right[half:].astype(bf16), 1), shift_tensor(left[:half].astype(bf16), -1)


def scatter_summed(chunk, from_left, from_right):
    right, left = chunk(1), chunk(3)
    half = right.shape[0] // 2
    return (
        shift_tensor((right[:half] + from_left.astype(f32)).astype(bf16), 1),
        shift_tensor((left[half:] + from_right.astype(f32)).astype(bf16), -1),
    )


def scatter_near(chunk, from_left, from_right):
    left_low, right_top = scatter_plain(chunk)
    left_top, right_low = scatter_summed(chunk, from_left, from_right)
    return left_top, left_low, right_top, right_low


def scatter_whole(chunk, from_left, from_right):
    right, left = chunk(1), chunk(3)
    half = right.shape[0] // 2
    right = jnp.concatenate([right[:half] + from_left, right[half:]], axis=0).astype(bf16)
    left = jnp.concatenate([left[:half], left[half:] + from_right], axis=0).astype(bf16)
    return shift_tensor(right, 1), shift_tensor(left, -1)


def add_near(mine, near):
    left_top, left_low, right_top, right_low = near
    return mine + jnp.concatenate(
        [left_top.astype(f32) + right_top, left_low.astype(f32) + right_low], axis=0
    )


def exchange_tensor(values):
    parts = values.reshape(4, values.shape[0] // 4, values.shape[1])
    return lax.all_to_all(parts, "tensor", split_axis=0, concat_axis=0, tiled=True)


def add_terms(terms):
    return jnp.sum(terms.astype(f32), axis=0)


def sync(*values):
    return lax.optimization_barrier(values)


def dp_index(y, z, core):
    return (y % 4) * 8 + (z % 4) * 2 + core


def move(values, axes, step, cross):
    pairs = []
    for y in range(4):
        for z in range(4):
            for core in range(2):
                there = (y + step, z) if axes[core] == 0 else (y, z + step)
                pairs.append((dp_index(y, z, core), dp_index(*there, core ^ cross)))
    return lax.ppermute(values, "dp", pairs)


ALONG, ACROSS = (0, 1), (1, 0)


def swap_core(values):
    return move(values, ALONG, 0, 1)


def spread_near(values, extra, core):
    mine = lax.dynamic_slice_in_dim(values, core * HALF, HALF, 1)
    other = lax.dynamic_slice_in_dim(values, (1 - core) * HALF, HALF, 1)
    mine = jnp.concatenate([mine, extra], axis=1)
    other = jnp.concatenate([other, extra], axis=1)
    return mine, other, move(mine, ALONG, 1, 0), move(other, ACROSS, -1, 1), swap_core(other)


def spread_far(mine, other, back_mine, ahead_other, swapped):
    ahead_mine = move(mine, ALONG, -1, 0)
    back_other = move(other, ACROSS, 1, 1)
    far_mine = move(back_mine, ALONG, 1, 0)
    far_other = move(ahead_other, ALONG, -1, 0)
    return [mine, swapped, back_mine, back_other, far_mine, far_other, ahead_mine, ahead_other]


def send_first(chunks):
    middle = [move(chunks[2][0], ACROSS, 1, 0), move(chunks[2][1], ACROSS, -1, 0)]
    return middle, move(chunks[1][0], ACROSS, 1, 0), move(chunks[3][0], ACROSS, -1, 0)


def send_cross(chunks):
    return (
        swap_core(chunks[0][1]),
        move(chunks[1][1], ACROSS, 1, 1),
        move(chunks[3][1], ACROSS, -1, 1),
    )


def send_far(middle):
    return move(middle[0], ACROSS, 1, 0), move(middle[1], ACROSS, -1, 1)


def gather_rows(chunks, first, cross, far):
    _, near, wide = first
    swapped, other_near, other_wide = cross
    return [chunks[0][0], near, far[0], wide], [swapped, other_near, far[1], other_wide]


def send_rest(chunks, middle, near, wide):
    return gather_rows(chunks, (middle, near, wide), send_cross(chunks), send_far(middle))


def return_first(mine, other):
    middle = [move(mine[2], ACROSS, 1, 0), move(other[2], ALONG, -1, 1)]
    return middle, move(mine[1], ACROSS, -1, 0), move(mine[3], ACROSS, 1, 0)


def return_rest(mine, other, middle, near, wide):
    other_near = move(other[1], ALONG, -1, 1)
    other_wide = move(other[3], ALONG, 1, 1)
    far = [move(middle[0], ACROSS, 1, 0), move(middle[1], ACROSS, -1, 0)]
    return [[mine[0], swap_core(other[0])], [near, other_near], far, [wide, other_wide]]


def sum_far(blocks):
    return move(blocks[4], ALONG, 1, 0), move(blocks[5], ALONG, -1, 0)


def sum_near(blocks, passing, core):
    here, back, ahead = blocks[0:2], blocks[2:4], blocks[6:8]
    add = lambda a, b: (a.astype(f32) + b.astype(f32)).astype(bf16)
    far_one, far_two = passing
    mine_two = move(back[0], ALONG, -1, 0)
    other_one = move(ahead[1], ALONG, 1, 1)
    other_here = swap_core(here[1])
    mine_one = move(add(ahead[0], far_one), ALONG, 1, 0)
    other_two = move(add(back[1], far_two), ALONG, -1, 1)
    mine = here[0].astype(f32) + mine_one.astype(f32) + mine_two.astype(f32)
    other = other_here.astype(f32) + other_one.astype(f32) + other_two.astype(f32)
    first = core == 0
    left = jnp.where(first, mine[:, :HALF], other[:, :HALF])
    right = jnp.where(first, other[:, :HALF], mine[:, :HALF])
    return jnp.concatenate([left, right], axis=1), mine[:, HALF:] + other[:, HALF:]


def exchange(values):
    return lax.all_to_all(values, "dp", split_axis=0, concat_axis=0, tiled=True)


def turn(values, cos, sin):
    half = values.shape[0] // 2
    low, high = values[:half], values[half:]
    return jnp.concatenate([low * cos - high * sin, high * cos + low * sin], axis=0)


def diagonal_mask():
    key = lax.broadcasted_iota(jnp.int32, (BLOCK, BLOCK), 0)
    query = lax.broadcasted_iota(jnp.int32, (BLOCK, BLOCK), 1)
    return key <= query


def attend_kernel(
    q_ref, k_ref, v_ref, inverse_ref, cos_ref, sin_ref, out_ref, total_ref, turned_ref, key_s
):
    group, member = pl.program_id(0), pl.program_id(1)
    inverse = inverse_ref[...]
    cos, sin = cos_ref[...] * inverse, sin_ref[...] * inverse

    @pl.when(member == 0)
    def _():
        keys = turn(k_ref[...], cos, sin)
        key_s[...] = keys.T.astype(bf16)
        first = pl.multiple_of((QUERY_LOCAL + group) * HEAD_DIM, HEAD_DIM)
        turned_ref[pl.ds(first, HEAD_DIM), :] = keys.astype(bf16)
        second = pl.multiple_of((QUERY_LOCAL + KEY_LOCAL + group) * HEAD_DIM, HEAD_DIM)
        turned_ref[pl.ds(second, HEAD_DIM), :] = (v_ref[...] * inverse).astype(bf16)

    queries = turn(q_ref[...], cos, sin).astype(bf16)
    values = (v_ref[...] * inverse).astype(bf16)
    head = pl.multiple_of((group * GROUP + member) * HEAD_DIM, HEAD_DIM)
    turned_ref[pl.ds(head, HEAD_DIM), :] = queries
    causal = diagonal_mask()
    for j in range(queries.shape[1] // BLOCK):
        columns = slice(j * BLOCK, (j + 1) * BLOCK)
        query = queries[:, columns]
        tiles = []
        top = None
        for i in range(j + 1):
            tile = dot(key_s[i * BLOCK : (i + 1) * BLOCK, :], query, 1, 0) * SCALE
            if i == j:
                tile = jnp.where(causal, tile, -1e30)
            tiles.append(tile)
            peak = jnp.max(tile, axis=0, keepdims=True)
            top = peak if top is None else jnp.maximum(top, peak)
        total = jnp.zeros_like(top)
        summed = jnp.zeros((HEAD_DIM, BLOCK), f32)
        for i in range(j + 1):
            tile = jnp.exp2(tiles[i] - top)
            total = total + jnp.sum(tile, axis=0, keepdims=True)
            summed = summed + dot(values[:, i * BLOCK : (i + 1) * BLOCK], tile.astype(bf16), 1, 0)
        out_ref[pl.ds(head, HEAD_DIM), columns] = (summed / total).astype(bf16)
        total_ref[0, :, columns] = top + jnp.log2(total)


def attend_back_kernel(*refs):
    q_ref, k_ref, v_ref, out_ref, grad_ref, total_ref, inverse_ref, cos_ref, sin_ref = refs[:9]
    back_ref, scaled_ref, key_s, val_s, gk_s, gv_s = refs[9:]
    inverse = inverse_ref[...]

    def put(row, values):
        row = pl.multiple_of(row * HEAD_DIM, HEAD_DIM)
        back_ref[pl.ds(row, HEAD_DIM), :] = values.astype(bf16)
        scaled_ref[pl.ds(row, HEAD_DIM), :] = (values * inverse).astype(bf16)

    group, member = pl.program_id(0), pl.program_id(1)
    cos, sin = cos_ref[...], sin_ref[...]

    @pl.when(member == 0)
    def _():
        key_s[...] = k_ref[...].astype(f32).T.astype(bf16)
        val_s[...] = v_ref[...].astype(f32).T.astype(bf16)
        gk_s[...] = jnp.zeros_like(gk_s)
        gv_s[...] = jnp.zeros_like(gv_s)

    queries, grads, keys = q_ref[...], grad_ref[...], k_ref[...]
    inner = jnp.sum(out_ref[...].astype(f32) * grads.astype(f32), axis=0, keepdims=True)
    totals = total_ref[0]
    causal = diagonal_mask()
    pieces = []
    for j in range(queries.shape[1] // BLOCK):
        columns = slice(j * BLOCK, (j + 1) * BLOCK)
        query, grad = queries[:, columns], grads[:, columns]
        query_grad = jnp.zeros((HEAD_DIM, BLOCK), f32)
        for i in range(j + 1):
            rows = slice(i * BLOCK, (i + 1) * BLOCK)
            probs = jnp.exp2(dot(key_s[rows, :], query, 1, 0) * SCALE - totals[:, columns])
            if i == j:
                probs = jnp.where(causal, probs, 0.0)
            gv_s[rows, :] += dot(probs.astype(bf16), grad, 1, 1)
            grad_probs = dot(val_s[rows, :], grad, 1, 0)
            grad_scores = (probs * (grad_probs - inner[:, columns])).astype(bf16)
            query_grad = query_grad + dot(keys[:, rows], grad_scores, 1, 0)
            gk_s[rows, :] += dot(grad_scores, query, 1, 1)
        pieces.append(query_grad * FACTOR)
    put(group * GROUP + member, turn(jnp.concatenate(pieces, axis=1), cos, -sin))

    @pl.when(member == GROUP - 1)
    def _():
        put(QUERY_LOCAL + group, turn(gk_s[...].T * FACTOR, cos, -sin))
        put(QUERY_LOCAL + KEY_LOCAL + group, gv_s[...].T)


def head_block(first, per_group, tokens):
    if per_group:
        return pl.BlockSpec((HEAD_DIM, tokens), lambda g, m: (first + g * per_group + m, 0))
    return pl.BlockSpec((HEAD_DIM, tokens), lambda g, m: (first + g, 0))


def whole_block(shape):
    return pl.BlockSpec(shape, lambda g, m: (0,) * len(shape))


def project_kernel(start_ref, *refs):
    pieces, weight_ref = refs[:-4], refs[-4]
    out_ref, sequence_ref, inverse_ref = refs[-3:]
    ones = jnp.ones((8, weight_ref.shape[1]), bf16)
    for i, piece in enumerate(pieces):
        count = piece.shape[0]
        start = pl.multiple_of(start_ref[i], 128)
        rows = piece[...]
        sequence_ref[pl.ds(start, count), :] = rows
        out_ref[:, pl.ds(start, count)] = dot(weight_ref[...], rows, 1, 1)
        wide = rows.astype(f32)
        squares = dot(ones, (wide * wide).astype(bf16), 1, 1)[0:1]
        inverse_ref[:, pl.ds(start, count)] = lax.rsqrt(squares * (1.0 / rows.shape[1]) + epsilon)


def project_back_kernel(start_ref, *refs):
    pieces, weight_ref = refs[:-3], refs[-3]
    out_ref, sequence_ref = refs[-2:]
    for i, piece in enumerate(pieces):
        count = piece.shape[0]
        start = pl.multiple_of(start_ref[i], 128)
        rows = piece[...]
        sequence_ref[pl.ds(start, count), :] = rows
        out_ref[:, pl.ds(start, count)] = dot(weight_ref[...], rows, 1, 1).astype(bf16)


def project(pieces, weight, back):
    tokens = sum(piece.shape[0] for piece, _ in pieces)
    width, depth = weight.shape
    outs = [
        jax.ShapeDtypeStruct((width, tokens), bf16 if back else f32),
        jax.ShapeDtypeStruct((tokens, depth), bf16),
    ]
    if not back:
        outs.append(jax.ShapeDtypeStruct((1, tokens), f32))
    spec = pl.BlockSpec(memory_space=pltpu.VMEM)
    return pl.pallas_call(
        project_back_kernel if back else project_kernel,
        in_specs=[pl.BlockSpec(memory_space=pltpu.SMEM)] + [spec] * (len(pieces) + 1),
        out_specs=[spec] * len(outs),
        out_shape=outs,
        compiler_params=pltpu.CompilerParams(vmem_limit_bytes=20 * 2**20),
        cost_estimate=BRIEF,
        name="project_back" if back else "project",
    )(jnp.stack([start for _, start in pieces]), *[piece for piece, _ in pieces], weight)


def weight_grads_kernel(one_ref, rows_ref, scale_ref, two_ref, other_ref, extra_ref, out_ref):
    one, two = one_ref.shape[0], two_ref.shape[0]
    total = dot(one_ref[...], rows_ref[...], 1, 0) * scale_ref[...]
    out_ref[:, :one] = total.T.astype(bf16)
    total = dot(two_ref[...], other_ref[...], 1, 0)
    out_ref[:, one : one + two] = total.T.astype(bf16)
    out_ref[:, one + two :] = extra_ref[...].T.astype(bf16)


def weight_grads(one, rows, scale, two, other, extra):
    tokens, depth = rows.shape
    block = 256
    width = one.shape[0] + two.shape[0] + extra.shape[0]
    whole = lambda shape: pl.BlockSpec(shape, lambda d: (0, 0))
    return pl.pallas_call(
        weight_grads_kernel,
        grid=(depth // block,),
        in_specs=[
            whole(one.shape),
            pl.BlockSpec((tokens, block), lambda d: (0, d)),
            pl.BlockSpec((1, block), lambda d: (0, d)),
            whole(two.shape),
            pl.BlockSpec((tokens, block), lambda d: (0, d)),
            pl.BlockSpec((extra.shape[0], block), lambda d: (0, d)),
        ],
        out_specs=pl.BlockSpec((block, width), lambda d: (d, 0)),
        out_shape=jax.ShapeDtypeStruct((depth, width), bf16),
        compiler_params=pltpu.CompilerParams(vmem_limit_bytes=30 * 2**20),
        cost_estimate=BRIEF,
        name="weight_grads",
    )(one, rows, scale, two, other, extra)


def expert_sums_kernel(place_ref, mine_ref, left_ref, right_ref, up_ref, down_ref):
    total = mine_ref[...].astype(f32) + left_ref[...].astype(f32) + right_ref[...].astype(f32)
    up_ref[...] = total[:, : 2 * FF]
    down_ref[...] = total[:, 2 * FF :].T


def expert_sums(place, grads, left, right):
    rows, width = left.shape
    whole = lambda shape: pl.BlockSpec(shape, lambda i, at: (0, 0))
    return pl.pallas_call(
        expert_sums_kernel,
        grid_spec=pltpu.PrefetchScalarGridSpec(
            num_scalar_prefetch=1,
            grid=(1,),
            in_specs=[pl.BlockSpec((rows, width), lambda i, at: (at[0], 0))] + [whole((rows, width))] * 2,
            out_specs=[whole((rows, 2 * FF)), whole((FF, rows))],
        ),
        out_shape=[
            jax.ShapeDtypeStruct((rows, 2 * FF), f32),
            jax.ShapeDtypeStruct((FF, rows), f32),
        ],
        compiler_params=pltpu.CompilerParams(vmem_limit_bytes=24 * 2**20),
        cost_estimate=BRIEF,
        name="expert_sums",
    )(place, grads, left, right)


def attend(projected, inverse, cos, sin):
    width, tokens = projected.shape
    total_block = pl.BlockSpec((1, 1, tokens), lambda g, m: (g * GROUP + m, 0, 0))
    return pl.pallas_call(
        attend_kernel,
        grid=(KEY_LOCAL, GROUP),
        in_specs=[
            head_block(0, GROUP, tokens),
            head_block(QUERY_LOCAL, 0, tokens),
            head_block(QUERY_LOCAL + KEY_LOCAL, 0, tokens),
            whole_block(inverse.shape),
            whole_block(cos.shape),
            whole_block(sin.shape),
        ],
        out_specs=(
            whole_block((QUERY_LOCAL * HEAD_DIM, tokens)),
            total_block,
            whole_block((width, tokens)),
        ),
        out_shape=(
            jax.ShapeDtypeStruct((QUERY_LOCAL * HEAD_DIM, tokens), bf16),
            jax.ShapeDtypeStruct((QUERY_LOCAL, 1, tokens), f32),
            jax.ShapeDtypeStruct((width, tokens), bf16),
        ),
        scratch_shapes=[pltpu.VMEM((tokens, HEAD_DIM), bf16)],
        compiler_params=pltpu.CompilerParams(vmem_limit_bytes=20 * 2**20),
        cost_estimate=BRIEF,
        name="attend",
    )(projected, projected, projected, inverse, cos, sin)


def attend_back(turned, out, grad, totals, inverse, cos, sin):
    width, tokens = turned.shape
    total_block = pl.BlockSpec((1, 1, tokens), lambda g, m: (g * GROUP + m, 0, 0))
    return pl.pallas_call(
        attend_back_kernel,
        grid=(KEY_LOCAL, GROUP),
        in_specs=[
            head_block(0, GROUP, tokens),
            head_block(QUERY_LOCAL, 0, tokens),
            head_block(QUERY_LOCAL + KEY_LOCAL, 0, tokens),
            head_block(0, GROUP, tokens),
            head_block(0, GROUP, tokens),
            total_block,
            whole_block(inverse.shape),
            whole_block(cos.shape),
            whole_block(sin.shape),
        ],
        out_specs=[whole_block((width, tokens))] * 2,
        out_shape=[jax.ShapeDtypeStruct((width, tokens), bf16)] * 2,
        scratch_shapes=[
            pltpu.VMEM((tokens, HEAD_DIM), bf16),
            pltpu.VMEM((tokens, HEAD_DIM), bf16),
            pltpu.VMEM((tokens, HEAD_DIM), f32),
            pltpu.VMEM((tokens, HEAD_DIM), f32),
        ],
        compiler_params=pltpu.CompilerParams(vmem_limit_bytes=20 * 2**20),
        cost_estimate=LONG,
        name="attend_back",
    )(turned, turned, turned, out, grad, totals, inverse, cos, sin)


def build_kernel(*refs):
    tokens, (expand_ref, pick_ref, core_ref) = refs[:8], refs[8:11]
    outs, token_s = refs[11:19], refs[19]
    step = pl.program_id(0)
    for r in range(4):

        @pl.when(step == r)
        def _(r=r):
            token_s[0] = tokens[2 * r][...]
            token_s[1] = tokens[2 * r + 1][...]

    count = tokens[0].shape[0]
    index = lax.broadcasted_iota(jnp.int32, (ROWS, count), 0).astype(f32)
    below = lax.broadcasted_iota(jnp.int32, (8, 128), 0)
    across = lax.broadcasted_iota(jnp.int32, (8, 128), 1)
    pieces = []
    for s in (core_ref[0], 1 - core_ref[0]):
        slots = dot(expand_ref[...], token_s[s, :, HALF:], 1, 1)
        hot = jnp.concatenate(
            [
                jnp.where(slots[k * ROWS : (k + 1) * ROWS] == index, 1.0, 0.0)
                for k in range(8)
            ],
            axis=0,
        ).astype(bf16)
        rows = dot(hot, token_s[s, :, :HALF], 1, 0)
        parts = [rows[k * ROWS : (k + 1) * ROWS] for k in range(8)]
        gates = dot(pick_ref[...], token_s[s, :, HALF:], 1, 1).astype(bf16)
        for d in range(4):
            values = dot(gates, hot[d * PAIR : d * PAIR + 128], 1, 1)
            high, low = values[2 * d : 2 * d + 1], values[2 * d + 1 : 2 * d + 2]
            spare = jnp.where(below == 4, high, jnp.where(below == 5, low, 0.0))
            spare = jnp.where(across < ROWS, spare, 0.0)
            part = parts[2 * d]
            last = jnp.concatenate([part[64:, :128] + spare, part[64:, 128:]], axis=1)
            parts[2 * d] = jnp.concatenate([part[:64], last], axis=0)
        pieces.append(parts)
    for k in range(8):
        outs[k][0] = jnp.concatenate([pieces[0][k], pieces[1][k]], axis=0).astype(bf16)


def build(core, blocks, expand, pick, cost):
    count, width = blocks[0].shape
    whole = lambda shape: pl.BlockSpec(shape, lambda r: (0,) * len(shape))
    outs = pl.pallas_call(
        build_kernel,
        grid=(4,),
        in_specs=[whole((count, width))] * 8
        + [whole(expand.shape), whole(pick.shape), pl.BlockSpec(memory_space=pltpu.SMEM)],
        out_specs=[pl.BlockSpec((1, PAIR, HALF), lambda r: (r, 0, 0))] * 8,
        out_shape=[jax.ShapeDtypeStruct((4, PAIR, HALF), bf16)] * 8,
        scratch_shapes=[pltpu.VMEM((2, count, width), bf16)],
        compiler_params=pltpu.CompilerParams(vmem_limit_bytes=VMEM_LIMIT),
        cost_estimate=cost,
        name="build_rows",
    )(*blocks, expand, pick, core)
    return [[outs[2 * d], outs[2 * d + 1]] for d in range(4)]


def combine_kernel(gated, refs):
    given, slots, (expand_ref, aim_ref, pick_ref, core_ref) = refs[:8], refs[8:16], refs[16:20]
    outs, total_s, slot_s = refs[20:28], refs[28], refs[29]
    core = core_ref[0]
    step = pl.program_id(0)
    for r in range(4):

        @pl.when(step == r)
        def _(r=r):
            slot_s[0] = slots[2 * r][...]
            slot_s[1] = slots[2 * r + 1][...]

    rows = jnp.concatenate([ref[0] for ref in given], axis=0)
    if gated:
        own = lax.broadcasted_iota(jnp.int32, (ROWS, 128), 0)
        own = own == lax.broadcasted_iota(jnp.int32, (ROWS, 128), 1)
        columns = []
        for d in range(4):
            head = given[2 * d][0, :, :128].astype(f32)
            for s in range(2):
                at = s * ROWS + CAP
                high = jnp.sum(jnp.where(own, head[at : at + 1], 0.0), axis=1, keepdims=True)
                low = jnp.sum(jnp.where(own, head[at + 1 : at + 2], 0.0), axis=1, keepdims=True)
                columns.append(
                    high * pick_ref[2 * d : 2 * d + 1] + low * pick_ref[2 * d + 1 : 2 * d + 2]
                )
            columns.append(jnp.zeros((PAIR, EXTRA), f32))
        rows = jnp.concatenate([rows, jnp.concatenate(columns, axis=0).astype(bf16)], axis=1)
    hots = []
    for s in range(2):
        hot = dot(slot_s[core if s == 0 else 1 - core], expand_ref[...], 1, 0)
        hot = hot == aim_ref[s : s + 1]
        hots.append(jnp.where(hot, 1.0, 0.0).astype(bf16))
    total = dot(jnp.concatenate(hots, axis=0), rows, 1, 0).astype(bf16)
    count = slot_s.shape[1]
    total_s[0] = total[:count]
    total_s[1] = total[count:]
    for r in range(4):

        @pl.when(step == r)
        def _(r=r):
            outs[2 * r][...] = total_s[core]
            outs[2 * r + 1][...] = total_s[1 - core]


def combine(core, chunks, blocks, expand, aim, pick, gated):
    count = blocks[0].shape[0]
    width = HALF + (EXTRA if gated else 0)
    whole = lambda shape: pl.BlockSpec(shape, lambda r: (0,) * len(shape))
    return pl.pallas_call(
        lambda *refs: combine_kernel(gated, refs),
        grid=(4,),
        in_specs=[pl.BlockSpec((1, PAIR, HALF), lambda r: (r, 0, 0))] * 8
        + [pl.BlockSpec((count, EXTRA), lambda r: (0, HALF // EXTRA))] * 8
        + [
            whole(expand.shape),
            whole(aim.shape),
            whole(pick.shape),
            pl.BlockSpec(memory_space=pltpu.SMEM),
        ],
        out_specs=[whole((count, width))] * 8,
        out_shape=[jax.ShapeDtypeStruct((count, width), bf16)] * 8,
        scratch_shapes=[
            pltpu.VMEM((2, count, width), bf16),
            pltpu.VMEM((2, count, EXTRA), bf16),
        ],
        compiler_params=pltpu.CompilerParams(vmem_limit_bytes=VMEM_LIMIT),
        cost_estimate=LONG if gated else BRIEF,
        name="combine_rows",
    )(*[piece for chunk in chunks for piece in chunk], *blocks, expand, aim, pick, core)


def whole_rows(core_ref, mine, other, mine_s):
    step = pl.program_id(0)
    for d in range(4):

        @pl.when(step == d)
        def _(d=d):
            for r in range(4):
                mine_s[r * PAIR : (r + 1) * PAIR, :] = mine[d][r]

    one = mine_s[...]
    two = jnp.concatenate([ref[0] for ref in other], axis=0)
    first = core_ref[0] == 0
    return one, jnp.concatenate([jnp.where(first, one, two), jnp.where(first, two, one)], axis=1)


def store_halves(core_ref, values, spare, mine, other):
    step = pl.program_id(0)
    first = core_ref[0] == 0
    one = jnp.where(first, values[:, :HALF], values[:, HALF:])
    two = jnp.where(first, values[:, HALF:], values[:, :HALF]).astype(bf16)
    if spare is not None:
        one = jnp.concatenate([one[:, :128] + spare, one[:, 128:]], axis=1)
    one = one.astype(bf16)
    for d in range(4):

        @pl.when(step == d)
        def _(d=d):
            for r in range(4):
                mine[d][r] = one[r * PAIR : (r + 1) * PAIR]

    for r in range(4):
        other[r][0] = two[r * PAIR : (r + 1) * PAIR]


def cotangent_kernel(*refs):
    core_ref, mine, other = refs[0], refs[1:5], refs[5:9]
    down_ref, rows_ref, hidden_ref, mine_s = refs[9:]
    _, rows = whole_rows(core_ref, mine, other, mine_s)
    rows_ref[0] = rows
    hidden_ref[0] = dot(rows, down_ref[...], 1, 1)


def expert_kernel(*refs):
    core_ref, mine, other, up_ref, back_ref = refs[0], refs[1:5], refs[5:9], refs[9], refs[10]
    rows_ref, grad_ref, hidden_ref = refs[11:14]
    mine_out, other_out, mine_s = refs[14:18], refs[18:22], refs[22]
    one, rows = whole_rows(core_ref, mine, other, mine_s)
    rows_ref[0] = rows
    own = lax.broadcasted_iota(jnp.int32, (ROWS, 128), 0)
    own = own == lax.broadcasted_iota(jnp.int32, (ROWS, 128), 1)
    head = one[:, :128].astype(f32)
    gates = []
    for i in range(LINE // ROWS):
        at = i * ROWS + CAP
        line = head[at : at + 1] + head[at + 1 : at + 2]
        gates.append(jnp.sum(jnp.where(own, line, 0.0), axis=1, keepdims=True))
    gate = jnp.concatenate(gates, axis=0)
    inner, total = 0.0, 0.0
    width = FF // 2
    for c in range(2):
        low, high = slice(c * width, (c + 1) * width), slice(FF + c * width, FF + (c + 1) * width)
        gate_part = dot(rows, up_ref[:, low], 1, 0)
        up_part = dot(rows, up_ref[:, high], 1, 0)
        sigmoid = 1.0 / (1.0 + jnp.exp(-gate_part))
        silu = gate_part * sigmoid
        hidden = silu * up_part
        back = back_ref[0, :, low]
        inner = inner + jnp.sum(hidden * back, axis=1, keepdims=True)
        hidden_ref[0, :, low] = (gate * hidden).astype(bf16)
        back = gate * back
        grad_one = (back * up_part * (sigmoid + silu * (1.0 - sigmoid))).astype(bf16)
        grad_two = (back * silu).astype(bf16)
        grad_ref[0, :, low] = grad_one
        grad_ref[0, :, high] = grad_two
        total = total + dot(grad_one, up_ref[:, low], 1, 1) + dot(grad_two, up_ref[:, high], 1, 1)
    below = lax.broadcasted_iota(jnp.int32, (8, 128), 0)
    spares = []
    for i in range(LINE // ROWS):
        line = jnp.where(own, inner[i * ROWS : (i + 1) * ROWS], 0.0)
        line = jnp.sum(line, axis=0, keepdims=True)
        high = line.astype(bf16).astype(f32)
        spare = jnp.where(below == 4, high, jnp.where(below == 5, line - high, 0.0))
        spares += [jnp.zeros((ROWS - 8, 128), f32), spare]
    store_halves(
        core_ref, total, jnp.concatenate(spares, axis=0), mine_out, other_out
    )


def result_kernel(*refs):
    core_ref, hidden_ref, down_ref = refs[:3]
    store_halves(core_ref, dot(hidden_ref[0], down_ref[...], 1, 0), None, refs[3:7], refs[7:11])


def whole_spec(shape):
    return pl.BlockSpec(shape, lambda d: (0,) * len(shape))


def line_spec(rows, width):
    return pl.BlockSpec((1, rows, width), lambda d: (d, 0, 0))


CORE_SPEC = pl.BlockSpec(memory_space=pltpu.SMEM)
EXPERT_PARAMS = dict(compiler_params=pltpu.CompilerParams(vmem_limit_bytes=VMEM_LIMIT))


def cotangent_rows(core, mine, other, down):
    return pl.pallas_call(
        cotangent_kernel,
        grid=(4,),
        in_specs=[CORE_SPEC]
        + [whole_spec((4, PAIR, HALF))] * 4
        + [line_spec(PAIR, HALF)] * 4
        + [whole_spec(down.shape)],
        out_specs=(line_spec(LINE, 2 * HALF), line_spec(LINE, FF)),
        out_shape=(
            jax.ShapeDtypeStruct((4, LINE, 2 * HALF), bf16),
            jax.ShapeDtypeStruct((4, LINE, FF), f32),
        ),
        scratch_shapes=[pltpu.VMEM((LINE, HALF), bf16)],
        cost_estimate=BRIEF,
        name="cotangent_rows",
        compiler_params=pltpu.CompilerParams(vmem_limit_bytes=28 * 2**20),
    )(core, *mine, *other, down)


def expert_rows(core, mine, other, up, back):
    outs = pl.pallas_call(
        expert_kernel,
        grid=(4,),
        in_specs=[CORE_SPEC]
        + [whole_spec((4, PAIR, HALF))] * 4
        + [line_spec(PAIR, HALF)] * 4
        + [whole_spec(up.shape), line_spec(LINE, FF)],
        out_specs=[line_spec(LINE, 2 * HALF), line_spec(LINE, 2 * FF), line_spec(LINE, FF)]
        + [whole_spec((4, PAIR, HALF))] * 4
        + [line_spec(PAIR, HALF)] * 4,
        out_shape=[
            jax.ShapeDtypeStruct((4, LINE, 2 * HALF), bf16),
            jax.ShapeDtypeStruct((4, LINE, 2 * FF), bf16),
            jax.ShapeDtypeStruct((4, LINE, FF), bf16),
        ]
        + [jax.ShapeDtypeStruct((4, PAIR, HALF), bf16)] * 8,
        scratch_shapes=[pltpu.VMEM((LINE, HALF), bf16)],
        cost_estimate=BRIEF,
        name="expert_rows",
        **EXPERT_PARAMS,
    )(core, *mine, *other, up, back)
    return outs[0], outs[1], outs[2], outs[3:7], outs[7:11]


def result_rows(core, hidden, down):
    outs = pl.pallas_call(
        result_kernel,
        grid=(4,),
        in_specs=[CORE_SPEC, line_spec(LINE, FF), whole_spec(down.shape)],
        out_specs=[whole_spec((4, PAIR, HALF))] * 4 + [line_spec(PAIR, HALF)] * 4,
        out_shape=[jax.ShapeDtypeStruct((4, PAIR, HALF), bf16)] * 8,
        cost_estimate=LONG,
        name="result_rows",
        **EXPERT_PARAMS,
    )(core, hidden, down)
    return outs[:4], outs[4:]


def per_device(
    tokens,
    norm_gains,
    query_matrix,
    key_value_weight,
    output_weight,
    router,
    expert_up,
    expert_down,
    routes,
    cotangent,
):
    local_rows, model_width = tokens.shape
    query_width = query_matrix.shape[1]
    keyval_width = key_value_weight.shape[2]
    experts_all = router.shape[0]
    place = lax.axis_index("tensor")
    group = lax.axis_index("dp")

    expert_index = jnp.arange(experts_all, dtype=jnp.int32)
    picked = jnp.any(routes[:, :, None] == expert_index[None, None, :], axis=1)
    token_index = jnp.arange(local_rows, dtype=jnp.int32)
    before = (token_index[:, None] > token_index[None, :]).astype(bf16)
    rank = dot(before, picked.astype(bf16), 1, 0)
    slot = jnp.where(picked, rank, -1.0)
    core = lax.rem(group, 2)
    line_y, line_z = group // 8, lax.rem(group // 2, 4)
    core_scalar = jnp.reshape(core, (1,)).astype(jnp.int32)

    distance = jnp.arange(4, dtype=jnp.int32)
    chip = jnp.where(
        core == 0, line_y * 4 + (line_z + distance) % 4, ((line_y + distance) % 4) * 4 + line_z
    )
    partner = jnp.stack([2 * chip + core, 2 * chip + 1 - core], axis=1).reshape(8)
    lane = jnp.arange(EXTRA, dtype=jnp.int32)
    hit = lane[None, :] == partner[:, None] + 64
    expand = jnp.repeat(hit, ROWS, axis=0).astype(bf16)
    expand_turned = jnp.repeat(hit, PAIR, axis=0).T.astype(bf16)
    near = partner.reshape(4, 2)[:, 0]
    pick = jnp.stack([near, near + 32], axis=1).reshape(8)
    pick = jnp.pad((lane[None, :] == pick[:, None]).astype(bf16), ((0, 8), (0, 0)))
    pick_wide = pick.astype(f32)
    spot = jnp.arange(8 * PAIR, dtype=jnp.int32)
    aim = jnp.stack(
        [
            jnp.where((spot // ROWS) % 2 == s, spot % ROWS, -5 if s < 2 else -6).astype(f32)
            for s in range(8)
        ],
        axis=0,
    )

    def wide(values):
        return jnp.pad(values, ((0, 0), (0, EXTRA - values.shape[1])))

    up_matrix, down_matrix = expert_up[0], expert_down[0]

    inputs = tokens.astype(jnp.float32)
    inv_rms_one = inverse_rms(inputs)
    near = gather_near(tokens, False)
    cot_near = spread_near(
        cotangent, wide(jnp.concatenate([jnp.zeros((local_rows, 64), f32), slot], axis=1).astype(bf16)), core
    )
    sequence_length = 4 * local_rows
    joined_weight = jnp.concatenate(
        [query_matrix, key_value_weight.reshape(model_width, 2 * keyval_width)], axis=1
    )
    weight_turned = joined_weight.T
    gained_turned = (norm_gains[0][:, None] * joined_weight.astype(f32)).astype(bf16).T
    cos, sin = rotary_tables(sequence_length, HEAD_DIM)
    near, cot_near, gained_turned, weight_turned, cos, sin, expand_turned, aim, pick_wide = sync(
        near, cot_near, gained_turned, weight_turned, cos, sin, expand_turned, aim, pick_wide
    )
    pieces = gather_far(tokens, near, place)
    cot_chunks = build(core_scalar, spread_far(*cot_near), expand, pick, LONG)
    pieces, cot_chunks = sync(pieces, cot_chunks)
    cot_first = send_first(cot_chunks)
    projected, sequence, inverse = project(pieces, gained_turned, False)
    attended, log_totals, turned = attend(projected, inverse, cos, sin)
    def output_chunk(k):
        start = lax.rem(place + k, 4) * local_rows
        return dot(lax.dynamic_slice_in_dim(attended, start, local_rows, 1), output_weight, 0, 0)

    attended, cot_first = sync(attended, cot_first)
    far = scatter_far(output_chunk)
    cot_swapped = send_cross(cot_chunks)
    far, cot_swapped = sync(far, cot_swapped)
    near = scatter_whole(output_chunk, *far)
    near, cot_far = sync(near, send_far(cot_first[0]))
    cot_got = gather_rows(cot_chunks, cot_first, cot_swapped, cot_far)
    middle = inputs + output_chunk(0) + near[0].astype(f32) + near[1].astype(f32)
    mixed_norm, inv_rms_two = norm_rows(middle, norm_gains[1])
    mixed_low = mixed_norm.astype(jnp.bfloat16)
    logits = dot(mixed_low, router, 1, 1)
    chosen = jnp.where(picked, logits, -jnp.inf)
    chosen_exp = jnp.exp(chosen - jnp.max(chosen, axis=1, keepdims=True))
    gates = chosen_exp / jnp.sum(chosen_exp, axis=1, keepdims=True)

    gates_high, gates_low = split_two(gates)
    mixed_near = spread_near(
        mixed_low, wide(jnp.concatenate([gates_high, gates_low, slot], axis=1).astype(bf16)), core
    )
    mixed_blocks = spread_far(*mixed_near)
    mixed_chunks = build(core_scalar, mixed_blocks, expand, pick, BRIEF)
    cot_rows, grad_hidden_one = cotangent_rows(core_scalar, *cot_got, down_matrix)
    mixed_first, grad_hidden_one = sync(send_first(mixed_chunks), grad_hidden_one)
    mixed_got = send_rest(mixed_chunks, *mixed_first)
    mixed_got, grad_hidden_one = sync(mixed_got, grad_hidden_one)
    rows_in, grad_gate_up, hidden_gated, grad_mine, grad_other = expert_rows(
        core_scalar, *mixed_got, up_matrix, grad_hidden_one
    )

    rows_in = rows_in.reshape(4 * LINE, model_width)
    cot_rows = cot_rows.reshape(4 * LINE, model_width)
    grad_gate_up = grad_gate_up.reshape(4 * LINE, 2 * FF)
    hidden_flat = hidden_gated.reshape(4 * LINE, FF)
    up_grad = dot(rows_in, grad_gate_up, 0, 0).astype(bf16)
    grad_first, up_grad = sync(return_first(grad_mine, grad_other), up_grad)
    down_grad = dot(cot_rows, hidden_flat, 0, 0).astype(bf16)
    grad_chunks = return_rest(grad_mine, grad_other, *grad_first)
    expert_grads = jnp.concatenate([up_grad, down_grad], axis=1)
    grad_chunks, expert_grads, hidden_gated = sync(grad_chunks, expert_grads, hidden_gated)
    expert_rows_out = model_width // 4

    def expert_chunk(k):
        start = lax.rem(place + k, 4) * expert_rows_out
        return lax.dynamic_slice_in_dim(expert_grads, start, expert_rows_out, 0)

    grad_blocks = combine(core_scalar, grad_chunks, mixed_blocks, expand_turned, aim, pick_wide, True)
    grad_blocks, expert_far, hidden_gated = sync(
        grad_blocks, scatter_far(expert_chunk), hidden_gated
    )
    result_mine, result_other = result_rows(core_scalar, hidden_gated, down_matrix)
    grad_mixed, grad_gate = sum_near(grad_blocks, sum_far(grad_blocks), core)
    grad_mixed, grad_gate, result_mine, result_other = sync(
        grad_mixed, grad_gate, result_mine, result_other
    )
    grad_gate = grad_gate[:, :32] + grad_gate[:, 32:64]

    grad_logits = gates * (grad_gate - jnp.sum(gates * grad_gate, axis=1, keepdims=True))
    grad_mixed = grad_mixed + dot(grad_logits, router.astype(f32), 1, 0, highest)
    router_part = dot(grad_logits, mixed_low.astype(f32), 0, 0, highest)
    grad_out = cotangent.astype(jnp.float32)
    grad_middle = grad_out + norm_back(middle, inv_rms_two, norm_gains[1], grad_mixed)
    gain_two_part = jnp.sum(grad_mixed * middle * inv_rms_two, axis=0)

    grad_low = grad_middle.astype(bf16)
    router_part, result_mine, result_other = sync(router_part, result_mine, result_other)
    near = gather_near(grad_low, False)
    middle_rows = [move(result_mine[2], ACROSS, 1, 0), move(result_other[2], ALONG, -1, 1)]
    back_near = move(result_mine[1], ACROSS, -1, 0)
    near, middle_rows, back_near = sync(near, middle_rows, back_near)
    pieces = gather_far(grad_low, near, place)
    back_wide = move(result_mine[3], ACROSS, 1, 0)
    other_near = move(result_other[1], ALONG, -1, 1)
    other_wide = move(result_other[3], ALONG, 1, 1)
    grad_attended, grad_attn_seq = project(pieces, output_weight, True)
    small_high, small_low = split_two(
        jnp.concatenate([router_part, gain_two_part[None], jnp.zeros((31, model_width), f32)], axis=0)
    )
    small_rows = jnp.concatenate([small_high, small_low], axis=0)
    dp_size = 32
    dp_rows = model_width // dp_size
    grad_attended, back_wide, other_near, other_wide, expert_far = sync(
        grad_attended, back_wide, other_near, other_wide, expert_far
    )
    far_rows = [move(middle_rows[0], ACROSS, 1, 0), move(middle_rows[1], ACROSS, -1, 0)]
    swapped = swap_core(result_other[0])
    expert_near = scatter_whole(expert_chunk, *expert_far)
    grad_projected, grad_scaled = attend_back(
        turned, attended, grad_attended, log_totals, inverse, cos, sin
    )
    grad_projected, grad_scaled, far_rows, swapped = sync(
        grad_projected, grad_scaled, far_rows, swapped
    )
    joined_grad = weight_grads(
        grad_scaled, sequence, norm_gains[0:1], attended, grad_attn_seq, small_rows
    )
    grad_projected, joined_grad = sync(grad_projected, joined_grad)

    def normed_chunk(grads, k):
        start = lax.rem(place + k, 4) * local_rows
        piece = lax.dynamic_slice_in_dim(grads, start, local_rows, 1)
        return dot(piece, weight_turned, 0, 0)

    far = scatter_far(lambda k: normed_chunk(grad_projected, k))
    far, expert_near = sync(far, expert_near)
    near = scatter_whole(lambda k: normed_chunk(grad_projected, k), *far)
    result_chunks = [
        [result_mine[0], swapped],
        [back_near, other_near],
        far_rows,
        [back_wide, other_wide],
    ]
    joined_terms = exchange(joined_grad.reshape(dp_size, dp_rows, joined_grad.shape[1]))
    result_blocks = combine(
        core_scalar, result_chunks, mixed_blocks, expand_turned, aim, pick_wide, False
    )
    result_far, joined_terms, near = sync(sum_far(result_blocks), joined_terms, near)
    moe_sum, _ = sum_near(result_blocks, result_far, core)
    grad_normed = normed_chunk(grad_projected, 0) + near[0].astype(f32) + near[1].astype(f32)
    weight_all = add_terms(joined_terms)
    joined_all = weight_all[:, : query_width + 2 * keyval_width]
    output_all = weight_all[:, query_width + 2 * keyval_width :]
    expert_up_grad, expert_down_grad = expert_sums(
        jnp.reshape(place, (1,)), expert_grads, *expert_near
    )
    expert_up_grad, expert_down_grad = expert_up_grad[None], expert_down_grad[None]
    query_weight_grad = joined_all[:, :query_width]
    keyval_weight_grad = joined_all[:, query_width:].reshape(dp_rows, 2, keyval_width)
    output_weight_grad = output_all[:, :query_width].T
    tokens_grad = grad_middle + norm_back(inputs, inv_rms_one, norm_gains[0], grad_normed)

    weight_rows = lax.dynamic_slice_in_dim(joined_weight, group * dp_rows, dp_rows, 0)
    gain_rows = lax.dynamic_slice_in_dim(norm_gains[0], group * dp_rows, dp_rows, 0)
    gain_one_part = jnp.sum(weight_rows.astype(f32) * joined_all, axis=1) / gain_rows
    base = query_width
    small = jnp.concatenate(
        [
            output_all[:, base : base + 33] + output_all[:, base + 64 : base + 97],
            gain_one_part[:, None],
            jnp.zeros((dp_rows, 94), f32),
        ],
        axis=1,
    ).reshape(4, dp_rows // 4, 128)
    small = jnp.pad(small, ((0, 0), (0, 4), (0, 0)))
    small = lax.all_to_all(small, "tensor", split_axis=0, concat_axis=0, tiled=True)
    small = jnp.sum(small, axis=0)[: dp_rows // 4].T
    router_grad = small[:experts_all]
    gains_grad = jnp.stack([small[experts_all + 1], small[experts_all]])

    layer_out = (middle + moe_sum).astype(jnp.bfloat16)
    return (
        layer_out,
        tokens_grad,
        gains_grad,
        query_weight_grad,
        keyval_weight_grad,
        output_weight_grad,
        router_grad,
        expert_up_grad,
        expert_down_grad,
    )


def solution(mesh):
    placed = (
        P(("dp", "tensor"), None),
        P(),
        P(None, "tensor"),
        P(None, None, "tensor"),
        P("tensor", None),
        P(),
        P("dp", None, None),
        P("dp", None, None),
        P(("dp", "tensor"), None),
        P(("dp", "tensor"), None),
    )
    return jax.shard_map(
        per_device,
        mesh=mesh,
        in_specs=placed,
        out_specs=(
            P(("dp", "tensor"), None),
            P(("dp", "tensor"), None),
            P(None, ("dp", "tensor")),
            P("dp", "tensor"),
            P("dp", None, "tensor"),
            P("tensor", "dp"),
            P(None, ("dp", "tensor")),
            P("dp", "tensor", None),
            P("dp", None, "tensor"),
        ),
        check_vma=False,
    )
```

time: 577 us -> 490 us (0.85)
  blocking collectives: 105 us -> 0 us
  Pallas kernels: 25.5 us -> 122 us
  matrix products: 110 us -> 26.9 us
  starting transfers between devices: 104 us -> 127 us
  between operations: 15.4 us -> 2.6 us
  other arithmetic: 24.6 us -> 30.8 us
    all_to_all x1 -> x0, blocking collectives: 105 us -> none  [exchange(): return lax.all_to_all(values, 'dp', split_axis=0, concat_axis=0, tiled=True)]
    pallas_call x0 -> x11, Pallas kernels: none -> 96.5 us  [the longest x1 25.9 us: expert_rows(): pl.pallas_call(expert_kernel, grid=(4,), in_specs=[CORE_SPEC] + [whole_sp...]
    all_to_all x5 -> x1, waiting for transfers between devices: 91.5 us -> 0.01 us  [exchange(): return lax.all_to_all(values, 'dp', split_axis=0, concat_axis=0, tiled=True)]
    ppermute x0 -> x64, waiting for transfers between devices: none -> 88.5 us  [move(): return lax.ppermute(values, 'dp', pairs)]
    ppermute x0 -> x64, starting transfers between devices: none -> 87.5 us  [move(): return lax.ppermute(values, 'dp', pairs)]
    dot_general x26 -> x14, matrix products: 110 us -> 26.9 us  [dot(): lax.dot_general(a, b, (((ca,), (cb,)), ((), ())), preferred_element_type=...]
    all_to_all x5 -> x1, starting transfers between devices: 66.9 us -> 6.01 us  [exchange(): return lax.all_to_all(values, 'dp', split_axis=0, concat_axis=0, tiled=True)]
    unnamed x123 -> x181, local copies, waits for them, and re-layouts: 13.1 us -> 25.5 us
  transfers between devices with their start and end apart: 24 -> 86, of which waited for: 13 -> 29; matrix products, arithmetic and copies ran while one was open for 21% -> 13% of each run, Pallas kernels for 5% -> 18%
where the time goes in v3:
time: 490 us; the launch traced here: 481 us
  waiting for transfers between devices  136 us (28%)
  starting transfers between devices  127 us (26%)
  Pallas kernels  122 us (25%)
  local copies, waits for them, and re-layouts  35.1 us (7%)
  other arithmetic  30.8 us (6%)
  matrix products  26.9 us (5%)
    ppermute x64, waiting for transfers between devices, move(): return lax.ppermute(values, 'dp', pairs)  88.5 us
    ppermute x64, starting transfers between devices, move(): return lax.ppermute(values, 'dp', pairs)  87.5 us
    ppermute x20, waiting for transfers between devices, shift_tensor(): lax.ppermute(values, 'tensor', [(i, (i + step) % 4) for i in range(4)])  47.8 us
    ppermute x20, starting transfers between devices, shift_tensor(): lax.ppermute(values, 'tensor', [(i, (i + step) % 4) for i in range(4)])  29.3 us
    dot_general x14, matrix products, dot(): lax.dot_general(a, b, (((ca,), (cb,)), ((), ())), preferred_element_type=...  26.9 us
    pallas_call x1, Pallas kernels, expert_rows(): pl.pallas_call(expert_kernel, grid=(4,), in_specs=[CORE_SPEC] + [whole_sp...  25.9 us
    unnamed x181, local copies, waits for them, and re-layouts  25.5 us
    pallas_call x2, Pallas kernels, combine(): pl.pallas_call(lambda *refs: combine_kernel(gated, refs), grid=(4,), in_s...  22.5 us
  transfers between devices with their start and end apart: 86, of which 29 were waited for; matrix products, arithmetic and copies ran while one was open for 13% of the time, Pallas kernels for 18%

profile of v3, /device:TPU:1, one launch (start us, length us, event | category | flops | bytes accessed | tf_op | source)
XLA Modules:
  0.0 481.0 jit_solution(18193224867906817240)
XLA Ops:
  40.5 6.3 %collective-permute-done.7.refs_3_ = bf16[256,896]{1,0:T(8,128)(2,1)} collective-permute-done((bf16[256,896]{1,0:T(8,128)(2,1)}, bf16[256,896]{1,0:T(8,128)(2,1)}, u32[]{:S(2)}, u32[]{:S(2)}) %collective-permute-start.7) | collective-permute-done | bytes 458784 | tf_op jit(solution)/shard_map/ppermute | solution.py:165
  47.5 8.1 %build_rows.2 = (bf16[4,144,768]{2,1,0:T(8,128)(2,1)}, bf16[4,144,768]{2,1,0:T(8,128)(2,1)}, bf16[4,144,768]{2,1,0:T(8,128)(2,1)}, bf16[4,144,768]{2,1,0:T(8,128...) custom-call(bf16[256,896]{1,0:T(8,128)(2,1)} %get-tuple-element.208., ...), custom_call_target="tpu_custom_call" | custom-call | flops 99999997952 | bytes 1 | tf_op jit(solution)/shard_map/build_rows/pallas_call | solution.py:581
  71.2 10.3 %attend.1 = (bf16[384,1024]{1,0:T(8,128)(2,1)S(1)}, f32[6,1,1024]{2,1,0:T(1,128)S(1)}, bf16[640,1024]{1,0:T(8,128)(2,1)S(1)}) custom-call(f32[640,1024]{1,0:T(8,128)S(1)} %get-tuple-element.232.q_ref.k_ref.v_ref, f32[640,1024]{1,0:T(8,128)S(1)} %get-tuple-element.232.q_ref.k_ref.v_ref, f32[640,1024]{1,0:T(8,128)S(1)} %get-tuple-element.232.q_ref.k_ref.v_ref, ...), custom_call_target="tpu_custom_call" | custom-call | flops 1 | bytes 1 | tf_op jit(solution)/shard_map/attend/pallas_call | solution.py:478
  88.0 7.3 %collective-permute-done.18.refs_6_ = bf16[4,144,768]{2,1,0:T(8,128)(2,1)S(1)} collective-permute-done((bf16[4,144,768]{2,1,0:T(8,128)(2,1)S(1)}, bf16[4,144,768]{2,1,0:T(8,128)(2,1)S(1)}, u32[]{:S(2)}, u32[]{:S(2)}) %collective-permute-start.18) | collective-permute-done | bytes 884768 | tf_op jit(solution)/shard_map/ppermute | solution.py:165
  104.5 4.8 %collective-permute-done.23.refs_7_ = bf16[4,144,768]{2,1,0:T(8,128)(2,1)} collective-permute-done((bf16[4,144,768]{2,1,0:T(8,128)(2,1)}, bf16[4,144,768]{2,1,0:T(8,128)(2,1)}, u32[]{:S(2)}, u32[]{:S(2)}) %collective-permute-start.23) | collective-permute-done | bytes 884768 | tf_op jit(solution)/shard_map/ppermute | solution.py:165
  109.3 8.8 %collective-permute-done.21 = bf16[256,1536]{1,0:T(8,128)(2,1)} collective-permute-done((bf16[256,1536]{1,0:T(8,128)(2,1)}, bf16[256,1536]{1,0:T(8,128)(2,1)}, u32[]{:S(2)}, u32[]{:S(2)}) %collective-permute-start.21) | collective-permute-done | bytes 786464 | tf_op jit(solution)/shard_map/ppermute | solution.py:70
  148.4 8.1 %build_rows.3 = (bf16[4,144,768]{2,1,0:T(8,128)(2,1)}, bf16[4,144,768]{2,1,0:T(8,128)(2,1)}, bf16[4,144,768]{2,1,0:T(8,128)(2,1)}, bf16[4,144,768]{2,1,0:T(8,128...) custom-call(bf16[256,896]{1,0:T(8,128)(2,1)} %copy-done.33, ...), custom_call_target="tpu_custom_call" | custom-call | flops 1 | bytes 1 | tf_op jit(solution)/shard_map/build_rows/pallas_call | solution.py:581
  161.9 6.8 %cotangent_rows.1 = (bf16[4,576,1536]{2,1,0:T(8,128)(2,1)S(1)}, f32[4,576,512]{2,1,0:T(8,128)S(1)}) custom-call(s32[1]{0:T(128)} %bitcast.6.refs_10_.refs_0_.refs_19_, bf16[4,144,768]{2,1,0:T(8,128)(2,1)S(1)} %copy-done.14, bf16[4,144,768]{2,1,0:T(8,128)(2,1)} %collective-permute-done.13.refs_2_, bf16[4,144,768]{2,1,0:T(8,128)(2,1)} %collective-permute-done.22.refs_3_, ...), custom_call_target="tpu_custom_call" | custom-call | flops 1 | bytes 1 | tf_op jit(solution)/shard_map/cotangent_rows/pallas_call | solution.py:774
  180.7 5.6 %collective-permute-start.38 = (bf16[4,144,768]{2,1,0:T(8,128)(2,1)}, bf16[4,144,768]{2,1,0:T(8,128)(2,1)}, u32[]{:S(2)}, u32[]{:S(2)}) collective-permute-start(bf16[4,144,768]{2,1,0:T(8,128)(2,1)} %collective-permute-done.32), channel_id=1, source_target_pairs={{0,28},{4,96},{8,4},{12,104},{16,12},{20,112},{24,20},{28,120},{32... | collective-permute-start | bytes 2654216 | tf_op jit(solution)/shard_map/ppermute | solution.py:165
  186.4 5.3 %collective-permute-done.37.refs_6_ = bf16[4,144,768]{2,1,0:T(8,128)(2,1)S(1)} collective-permute-done((bf16[4,144,768]{2,1,0:T(8,128)(2,1)}, bf16[4,144,768]{2,1,0:T(8,128)(2,1)S(1)}, u32[]{:S(2)}, u32[]{:S(2)}) %collective-permute-start.37) | collective-permute-done | bytes 884768 | tf_op jit(solution)/shard_map/ppermute | solution.py:165
  191.7 9.6 %collective-permute-done.35.refs_3_ = bf16[4,144,768]{2,1,0:T(8,128)(2,1)} collective-permute-done((bf16[4,144,768]{2,1,0:T(8,128)(2,1)}, bf16[4,144,768]{2,1,0:T(8,128)(2,1)}, u32[]{:S(2)}, u32[]{:S(2)}) %collective-permute-start.35) | collective-permute-done | bytes 884768 | tf_op jit(solution)/shard_map/ppermute | solution.py:165
  201.3 25.9 %expert_rows.1 = (bf16[4,576,1536]{2,1,0:T(8,128)(2,1)}, bf16[4,576,1024]{2,1,0:T(8,128)(2,1)}, bf16[4,576,512]{2,1,0:T(8,128)(2,1)}, bf16[4,144,768]{2,1,0:T(8,...) custom-call(s32[1]{0:T(128)} %bitcast.6.refs_10_.refs_0_.refs_19_, ...), custom_call_target="tpu_custom_call" | custom-call | flops 1 | bytes 1 | tf_op jit(solution)/shard_map/expert_rows/pallas_call | solution.py:794
  234.9 11.3 %bitcast_convert_fusion = bf16[1536,1024]{1,0:T(8,128)(2,1)S(1)} fusion(bf16[4,576,1536]{2,1,0:T(8,128)(2,1)} %get-tuple-element.288, bf16[4,576,1024]{2,1,0:T(8,128)(2,1)} %get-tuple-element.289), kind=kOutput, calls=%fused_computation.1 | convolution fusion | flops 7249330176 | bytes 14942208 | tf_op jit(solution)/shard_map/dot_general | solution.py:37
  263.8 9.4 %collective-permute-done.48.refs_7_ = bf16[4,144,768]{2,1,0:T(8,128)(2,1)} collective-permute-done((bf16[4,144,768]{2,1,0:T(8,128)(2,1)}, bf16[4,144,768]{2,1,0:T(8,128)(2,1)}, u32[]{:S(2)}, u32[]{:S(2)}) %collective-permute-start.48) | collective-permute-done | bytes 884768 | tf_op jit(solution)/shard_map/ppermute | solution.py:165
  276.8 11.8 %combine_rows.2 = (bf16[256,896]{1,0:T(8,128)(2,1)}, bf16[256,896]{1,0:T(8,128)(2,1)}, bf16[256,896]{1,0:T(8,128)(2,1)}, bf16[256,896]{1,0:T(8,128)(2,1)}, bf16[...) custom-call(bf16[4,144,768]{2,1,0:T(8,128)(2,1)} %get-tuple-element.299.ref, ...), custom_call_target="tpu_custom_call" | custom-call | flops 99999997952 | bytes 1 | tf_op jit(solution)/shard_map/combine_rows/pallas_call | solution.py:645
  305.3 8.8 %result_rows.1 = (bf16[4,144,768]{2,1,0:T(8,128)(2,1)}, bf16[4,144,768]{2,1,0:T(8,128)(2,1)}, bf16[4,144,768]{2,1,0:T(8,128)(2,1)}, bf16[4,144,768]{2,1,0:T(8,12...) custom-call(s32[1]{0:T(128)} %bitcast.6.refs_10_.refs_0_.refs_19_, ...), custom_call_target="tpu_custom_call" | custom-call | flops 99999997952 | bytes 1 | tf_op jit(solution)/shard_map/result_rows/pallas_call | solution.py:819
  326.0 14.1 %collective-permute-done.58.refs_1_ = bf16[256,1536]{1,0:T(8,128)(2,1)} collective-permute-done((bf16[256,1536]{1,0:T(8,128)(2,1)S(1)}, bf16[256,1536]{1,0:T(8,128)(2,1)}, u32[]{:S(2)}, u32[]{:S(2)}) %collective-permute-start.58) | collective-permute-done | bytes 786464 | tf_op jit(solution)/shard_map/ppermute | solution.py:70
  352.0 8.4 %collective-permute-done.63.refs_3_ = bf16[128,1536]{1,0:T(8,128)(2,1)S(1)} collective-permute-done((bf16[128,1536]{1,0:T(8,128)(2,1)S(1)}, bf16[128,1536]{1,0:T(8,128)(2,1)S(1)}, u32[]{:S(2)}, u32[]{:S(2)}) %collective-permute-start.63) | collective-permute-done | bytes 393248 | tf_op jit(solution)/shard_map/ppermute | solution.py:70
  372.6 15.4 %attend_back.1 = (bf16[640,1024]{1,0:T(8,128)(2,1)S(1)}, bf16[640,1024]{1,0:T(8,128)(2,1)S(1)}) custom-call(bf16[640,1024]{1,0:T(8,128)(2,1)S(1)} %copy-done.23, bf16[640,1024]{1,0:T(8,128)(2,1)S(1)} %copy-done.23, bf16[640,1024]{1,0:T(8,128)(2,1)S(1)} %copy-done.23, bf16[384,1024]{1,0:T(8,128)(2,1)S(1)} %get-tuple-element.241.refs_3_.two_ref, ...), custom_call_target="tpu_custom_call" | custom-call | flops 99999997952 | bytes 1 | tf_op jit(solution)/shard_map/attend_back/pallas_call | solution.py:509
  389.6 5.5 %weight_grads.1 = bf16[1536,1152]{1,0:T(8,128)(2,1)S(1)} custom-call(bf16[640,1024]{1,0:T(8,128)(2,1)S(1)} %get-tuple-element.379.one_ref, bf16[1024,1536]{1,0:T(8,128)(2,1)S(1)} %copy-done.11, f32[1,1536]{1,0:T(1,128)S(1)} %get-tuple-element.477.scale_ref, bf16[384,1024]{1,0:T(8,128)(2,1)S(1)} %get-tuple-element.241.refs_3_.two_ref, ...), custom_call_target="tpu_custom_call" | custom-call | flops 1 | bytes 1 | tf_op jit(solution)/shard_map/weight_grads/pallas_call | solution.py:429
  397.0 6.0 %all-to-all-start = ((bf16[32,48,1152]{2,1,0:T(8,128)(2,1)}), bf16[32,48,1152]{2,1,0:T(8,128)(2,1)}, u32[]{:S(2)}, u32[]{:S(2)}) async-start(bf16[32,48,1152]{2,1,0:T(8,128)(2,1)} %bitcast.57), calls=%async_computation | async-start | bytes 7077888 | tf_op jit(solution)/shard_map/all_to_all | solution.py:252
  408.7 7.4 %collective-permute-done.73 = bf16[128,1536]{1,0:T(8,128)(2,1)S(1)} collective-permute-done((bf16[128,1536]{1,0:T(8,128)(2,1)S(1)}, bf16[128,1536]{1,0:T(8,128)(2,1)S(1)}, u32[]{:S(2)}, u32[]{:S(2)}) %collective-permute-start.73) | collective-permute-done | bytes 393248 | tf_op jit(solution)/shard_map/ppermute | solution.py:70
  420.8 10.7 %combine_rows.3 = (bf16[256,768]{1,0:T(8,128)(2,1)}, bf16[256,768]{1,0:T(8,128)(2,1)}, bf16[256,768]{1,0:T(8,128)(2,1)}, bf16[256,768]{1,0:T(8,128)(2,1)}, bf16[...) custom-call(bf16[4,144,768]{2,1,0:T(8,128)(2,1)} %get-tuple-element.346.ref, ...), custom_call_target="tpu_custom_call" | custom-call | flops 1 | bytes 1 | tf_op jit(solution)/shard_map/combine_rows/pallas_call | solution.py:645
  441.8 7.4 %collective-permute-done.71 = bf16[256,768]{1,0:T(8,128)(2,1)S(1)} collective-permute-done((bf16[256,768]{1,0:T(8,128)(2,1)}, bf16[256,768]{1,0:T(8,128)(2,1)S(1)}, u32[]{:S(2)}, u32[]{:S(2)}) %collective-permute-start.71) | collective-permute-done | bytes 393248 | tf_op jit(solution)/shard_map/ppermute | solution.py:165
  (462 shorter events, 255.1 us)
Async XLA Ops:
  4.7 22.1 %collective-permute-start.3 = (bf16[256,896]{1,0:T(8,128)(2,1)}, bf16[256,896]{1,0:T(8,128)(2,1)}, u32[]{:S(2)}, u32[]{:S(2)}) collective-permute-start(bf16[256,896]{1,0:T(8,128)(2,1)} %get-tuple-element.211), channel_id=1, source_target_pairs={{0,28},{4,96},{8,4},{12,104},{16,12},{20,112},{24,20},{28,120},{32... | collective-permute-start | bytes 1376264 | tf_op jit(solution)/shard_map/ppermute | solution.py:165
  55.6 25.9 %collective-permute-start.11 = (bf16[4,144,768]{2,1,0:T(8,128)(2,1)}, bf16[4,144,768]{2,1,0:T(8,128)(2,1)}, u32[]{:S(2)}, u32[]{:S(2)}) collective-permute-start(bf16[4,144,768]{2,1,0:T(8,128)(2,1)} %get-tuple-element.237), channel_id=1, source_target_pairs={{0,8},{4,36},{8,16},{12,44},{16,24},{20,52},{24,0},{28,60},{32,40}... | collective-permute-start | bytes 2654216 | tf_op jit(solution)/shard_map/ppermute | solution.py:165
  55.8 25.8 %collective-permute-start.12 = (bf16[4,144,768]{2,1,0:T(8,128)(2,1)}, bf16[4,144,768]{2,1,0:T(8,128)(2,1)}, u32[]{:S(2)}, u32[]{:S(2)}) collective-permute-start(bf16[4,144,768]{2,1,0:T(8,128)(2,1)} %get-tuple-element.238), channel_id=1, source_target_pairs={{0,24},{4,100},{8,0},{12,108},{16,8},{20,116},{24,16},{28,124},{32... | collective-permute-start | bytes 2654216 | tf_op jit(solution)/shard_map/ppermute | solution.py:165
  58.3 23.6 %collective-permute-start.13 = (bf16[4,144,768]{2,1,0:T(8,128)(2,1)}, bf16[4,144,768]{2,1,0:T(8,128)(2,1)}, u32[]{:S(2)}, u32[]{:S(2)}) collective-permute-start(bf16[4,144,768]{2,1,0:T(8,128)(2,1)} %get-tuple-element.239), channel_id=1, source_target_pairs={{0,8},{4,36},{8,16},{12,44},{16,24},{20,52},{24,0},{28,60},{32,40}... | collective-permute-start | bytes 2654216 | tf_op jit(solution)/shard_map/ppermute | solution.py:165
  58.3 23.6 %collective-permute-start.14 = (bf16[4,144,768]{2,1,0:T(8,128)(2,1)}, bf16[4,144,768]{2,1,0:T(8,128)(2,1)}, u32[]{:S(2)}, u32[]{:S(2)}) collective-permute-start(bf16[4,144,768]{2,1,0:T(8,128)(2,1)} %get-tuple-element.240), channel_id=1, source_target_pairs={{0,24},{4,100},{8,0},{12,108},{16,8},{20,116},{24,16},{28,124},{32... | collective-permute-start | bytes 2654216 | tf_op jit(solution)/shard_map/ppermute | solution.py:165
  61.0 25.8 %collective-permute-start.17 = (bf16[4,144,768]{2,1,0:T(8,128)(2,1)}, bf16[4,144,768]{2,1,0:T(8,128)(2,1)}, u32[]{:S(2)}, u32[]{:S(2)}) collective-permute-start(bf16[4,144,768]{2,1,0:T(8,128)(2,1)} %get-tuple-element.242), channel_id=1, source_target_pairs={{0,4},{4,0},{8,12},{12,8},{16,20},{20,16},{24,28},{28,24},{32,36},... | collective-permute-start | bytes 2654216 | tf_op jit(solution)/shard_map/ppermute | solution.py:165
  234.7 24.3 %collective-permute-start.40 = (bf16[4,144,768]{2,1,0:T(8,128)(2,1)}, bf16[4,144,768]{2,1,0:T(8,128)(2,1)}, u32[]{:S(2)}, u32[]{:S(2)}) collective-permute-start(bf16[4,144,768]{2,1,0:T(8,128)(2,1)} %get-tuple-element.283), channel_id=1, source_target_pairs={{0,4},{4,0},{8,12},{12,8},{16,20},{20,16},{24,28},{28,24},{32,36},... | collective-permute-start | bytes 2654216 | tf_op jit(solution)/shard_map/ppermute | solution.py:165
  249.1 24.1 %collective-permute-start.48 = (bf16[4,144,768]{2,1,0:T(8,128)(2,1)}, bf16[4,144,768]{2,1,0:T(8,128)(2,1)}, u32[]{:S(2)}, u32[]{:S(2)}) collective-permute-start(bf16[4,144,768]{2,1,0:T(8,128)(2,1)} %get-tuple-element.295), channel_id=1, source_target_pairs={{0,36},{4,8},{8,44},{12,16},{16,52},{20,24},{24,60},{28,0},{32,68}... | collective-permute-start | bytes 2654216 | tf_op jit(solution)/shard_map/ppermute | solution.py:165
  251.2 22.6 %collective-permute-start.46 = (bf16[4,144,768]{2,1,0:T(8,128)(2,1)}, bf16[4,144,768]{2,1,0:T(8,128)(2,1)}, u32[]{:S(2)}, u32[]{:S(2)}) collective-permute-start(bf16[4,144,768]{2,1,0:T(8,128)(2,1)} %collective-permute-done.41), channel_id=1, source_target_pairs={{0,8},{4,36},{8,16},{12,44},{16,24},{20,52},{24,0},{28,60},{32,40}... | collective-permute-start | bytes 2654216 | tf_op jit(solution)/shard_map/ppermute | solution.py:165
  317.9 24.4 %collective-permute-start.60 = (bf16[4,144,768]{2,1,0:T(8,128)(2,1)S(1)}, bf16[4,144,768]{2,1,0:T(8,128)(2,1)}, u32[]{:S(2)}, u32[]{:S(2)}) collective-permute-start(bf16[4,144,768]{2,1,0:T(8,128)(2,1)S(1)} %copy-done.82), channel_id=1, source_target_pairs={{0,8},{4,36},{8,16},{12,44},{16,24},{20,52},{24,0},{28,60},{32,40}... | collective-permute-start | bytes 2654216 | tf_op jit(solution)/shard_map/ppermute | solution.py:165
  340.1 24.0 %collective-permute-start.65 = (bf16[4,144,768]{2,1,0:T(8,128)(2,1)}, bf16[4,144,768]{2,1,0:T(8,128)(2,1)}, u32[]{:S(2)}, u32[]{:S(2)}) collective-permute-start(bf16[4,144,768]{2,1,0:T(8,128)(2,1)} %get-tuple-element.355), channel_id=1, source_target_pairs={{0,8},{4,36},{8,16},{12,44},{16,24},{20,52},{24,0},{28,60},{32,40}... | collective-permute-start | bytes 2654216 | tf_op jit(solution)/shard_map/ppermute | solution.py:165
  340.1 26.7 %collective-permute-start.66 = (bf16[4,144,768]{2,1,0:T(8,128)(2,1)}, bf16[4,144,768]{2,1,0:T(8,128)(2,1)}, u32[]{:S(2)}, u32[]{:S(2)}) collective-permute-start(bf16[4,144,768]{2,1,0:T(8,128)(2,1)} %get-tuple-element.356), channel_id=1, source_target_pairs={{0,100},{4,24},{8,108},{12,0},{16,116},{20,8},{24,124},{28,16},{32... | collective-permute-start | bytes 2654216 | tf_op jit(solution)/shard_map/ppermute | solution.py:165
  342.4 24.4 %collective-permute-start.67 = (bf16[4,144,768]{2,1,0:T(8,128)(2,1)}, bf16[4,144,768]{2,1,0:T(8,128)(2,1)}, u32[]{:S(2)}, u32[]{:S(2)}) collective-permute-start(bf16[4,144,768]{2,1,0:T(8,128)(2,1)} %get-tuple-element.357), channel_id=1, source_target_pairs={{0,36},{4,8},{8,44},{12,16},{16,52},{20,24},{24,60},{28,0},{32,68}... | collective-permute-start | bytes 2654216 | tf_op jit(solution)/shard_map/ppermute | solution.py:165
  360.5 27.6 %collective-permute-start.70 = (bf16[4,144,768]{2,1,0:T(8,128)(2,1)S(1)}, bf16[4,144,768]{2,1,0:T(8,128)(2,1)S(1)}, u32[]{:S(2)}, u32[]{:S(2)}) collective-permute-start(bf16[4,144,768]{2,1,0:T(8,128)(2,1)S(1)} %copy-done.79), channel_id=1, source_target_pairs={{0,4},{4,0},{8,12},{12,8},{16,20},{20,16},{24,28},{28,24},{32,36},... | collective-permute-start | bytes 2654216 | tf_op jit(solution)/shard_map/ppermute | solution.py:165
  360.8 27.3 %collective-permute-start.68 = (bf16[4,144,768]{2,1,0:T(8,128)(2,1)}, bf16[4,144,768]{2,1,0:T(8,128)(2,1)S(1)}, u32[]{:S(2)}, u32[]{:S(2)}) collective-permute-start(bf16[4,144,768]{2,1,0:T(8,128)(2,1)} %collective-permute-done.60), channel_id=1, source_target_pairs={{0,8},{4,36},{8,16},{12,44},{16,24},{20,52},{24,0},{28,60},{32,40}... | collective-permute-start | bytes 2654216 | tf_op jit(solution)/shard_map/ppermute | solution.py:165
  364.1 24.0 %collective-permute-start.69 = (bf16[4,144,768]{2,1,0:T(8,128)(2,1)}, bf16[4,144,768]{2,1,0:T(8,128)(2,1)S(1)}, u32[]{:S(2)}, u32[]{:S(2)}) collective-permute-start(bf16[4,144,768]{2,1,0:T(8,128)(2,1)} %collective-permute-done.61), channel_id=1, source_target_pairs={{0,24},{4,100},{8,0},{12,108},{16,8},{20,116},{24,16},{28,124},{32... | collective-permute-start | bytes 2654216 | tf_op jit(solution)/shard_map/ppermute | solution.py:165
  368.3 47.7 %collective-permute-start.76 = (bf16[384,1536]{1,0:T(8,128)(2,1)}, bf16[384,1536]{1,0:T(8,128)(2,1)}, u32[]{:S(2)}, u32[]{:S(2)}) collective-permute-start(bf16[384,1536]{1,0:T(8,128)(2,1)} %pad_maximum_fusion.4), channel_id=1, source_target_pairs={{0,3},{1,0},{2,1},{3,2},{4,7},{5,4},{6,5},{7,6},{8,11},{9,8},{10,9... | collective-permute-start | bytes 3538952 | tf_op jit(solution)/shard_map/ppermute | solution.py:70
  372.6 43.5 %collective-permute-start.75 = (bf16[384,1536]{1,0:T(8,128)(2,1)}, bf16[384,1536]{1,0:T(8,128)(2,1)}, u32[]{:S(2)}, u32[]{:S(2)}) collective-permute-start(bf16[384,1536]{1,0:T(8,128)(2,1)} %pad_maximum_fusion.3), channel_id=1, source_target_pairs={{0,1},{1,2},{2,3},{3,0},{4,5},{5,6},{6,7},{7,4},{8,9},{9,10},{10,1... | collective-permute-start | bytes 3538952 | tf_op jit(solution)/shard_map/ppermute | solution.py:70
  397.0 54.6 %all-to-all-start = ((bf16[32,48,1152]{2,1,0:T(8,128)(2,1)}), bf16[32,48,1152]{2,1,0:T(8,128)(2,1)}, u32[]{:S(2)}, u32[]{:S(2)}) async-start(bf16[32,48,1152]{2,1,0:T(8,128)(2,1)} %bitcast.57), calls=%async_computation | async-start | bytes 7077888 | tf_op jit(solution)/shard_map/all_to_all | solution.py:252
  417.1 34.5 %collective-permute-start.78 = (bf16[256,1536]{1,0:T(8,128)(2,1)}, bf16[256,1536]{1,0:T(8,128)(2,1)S(1)}, u32[]{:S(2)}, u32[]{:S(2)}) collective-permute-start(bf16[256,1536]{1,0:T(8,128)(2,1)} %pad_maximum_fusion.9), channel_id=1, source_target_pairs={{0,3},{1,0},{2,1},{3,2},{4,7},{5,4},{6,5},{7,6},{8,11},{9,8},{10,9... | collective-permute-start | bytes 2359304 | tf_op jit(solution)/shard_map/ppermute | solution.py:70
  420.6 31.0 %collective-permute-start.77 = (bf16[256,1536]{1,0:T(8,128)(2,1)}, bf16[256,1536]{1,0:T(8,128)(2,1)}, u32[]{:S(2)}, u32[]{:S(2)}) collective-permute-start(bf16[256,1536]{1,0:T(8,128)(2,1)} %pad_maximum_fusion.8), channel_id=1, source_target_pairs={{0,1},{1,2},{2,3},{3,0},{4,5},{5,6},{6,7},{7,4},{8,9},{9,10},{10,1... | collective-permute-start | bytes 2359304 | tf_op jit(solution)/shard_map/ppermute | solution.py:70
  434.7 37.6 %collective-permute-start.80 = (bf16[256,768]{1,0:T(8,128)(2,1)}, bf16[256,768]{1,0:T(8,128)(2,1)}, u32[]{:S(2)}, u32[]{:S(2)}) collective-permute-start(bf16[256,768]{1,0:T(8,128)(2,1)} %get-tuple-element.391), channel_id=1, source_target_pairs={{0,96},{4,28},{8,104},{12,4},{16,112},{20,12},{24,120},{28,20},{32... | collective-permute-start | bytes 1179656 | tf_op jit(solution)/shard_map/ppermute | solution.py:165
  449.3 23.0 %collective-permute-start.81 = (bf16[256,768]{1,0:T(8,128)(2,1)}, bf16[256,768]{1,0:T(8,128)(2,1)}, u32[]{:S(2)}, u32[]{:S(2)}) collective-permute-start(bf16[256,768]{1,0:T(8,128)(2,1)} %get-tuple-element.392), channel_id=1, source_target_pairs={{0,4},{4,0},{8,12},{12,8},{16,20},{20,16},{24,28},{28,24},{32,36},... | collective-permute-start | bytes 1179656 | tf_op jit(solution)/shard_map/ppermute | solution.py:165
  449.8 22.5 %collective-permute-start.82 = (bf16[256,768]{1,0:T(8,128)(2,1)}, bf16[256,768]{1,0:T(8,128)(2,1)}, u32[]{:S(2)}, u32[]{:S(2)}) collective-permute-start(bf16[256,768]{1,0:T(8,128)(2,1)} %get-tuple-element.393), channel_id=1, source_target_pairs={{0,36},{4,8},{8,44},{12,16},{16,52},{20,24},{24,60},{28,0},{32,68}... | collective-permute-start | bytes 1179656 | tf_op jit(solution)/shard_map/ppermute | solution.py:165
  (152 other events, 1999.5 us)

commit v4 on v3

--- a/solution.py
+++ b/solution.py
@@ -10,6 +10,7 @@
 HEAD_DIM = 64
 FF = 512
 CAP = 68
+PART = 48
 ROWS = 72
 PAIR = 2 * ROWS
 LINE = 4 * PAIR
@@ -19,7 +20,8 @@
 
 epsilon = 1e-06
 theta = 10000.0
-BLOCK = 256
+FORWARD = 512
+BACKWARD = 256
 GROUP = QUERY_HEADS // KEY_VALUE_HEADS
 QUERY_LOCAL = QUERY_HEADS // 4
 KEY_LOCAL = KEY_VALUE_HEADS // 4
@@ -258,9 +260,9 @@
     return jnp.concatenate([low * cos - high * sin, high * cos + low * sin], axis=0)
 
 
-def diagonal_mask():
-    key = lax.broadcasted_iota(jnp.int32, (BLOCK, BLOCK), 0)
-    query = lax.broadcasted_iota(jnp.int32, (BLOCK, BLOCK), 1)
+def diagonal_mask(size):
+    key = lax.broadcasted_iota(jnp.int32, (size, size), 0)
+    query = lax.broadcasted_iota(jnp.int32, (size, size), 1)
     return key <= query
 
 
@@ -284,25 +286,25 @@
     values = (v_ref[...] * inverse).astype(bf16)
     head = pl.multiple_of((group * GROUP + member) * HEAD_DIM, HEAD_DIM)
     turned_ref[pl.ds(head, HEAD_DIM), :] = queries
-    causal = diagonal_mask()
-    for j in range(queries.shape[1] // BLOCK):
-        columns = slice(j * BLOCK, (j + 1) * BLOCK)
+    causal = diagonal_mask(FORWARD)
+    for j in range(queries.shape[1] // FORWARD):
+        columns = slice(j * FORWARD, (j + 1) * FORWARD)
         query = queries[:, columns]
         tiles = []
         top = None
         for i in range(j + 1):
-            tile = dot(key_s[i * BLOCK : (i + 1) * BLOCK, :], query, 1, 0) * SCALE
+            tile = dot(key_s[i * FORWARD : (i + 1) * FORWARD, :], query, 1, 0) * SCALE
             if i == j:
                 tile = jnp.where(causal, tile, -1e30)
             tiles.append(tile)
             peak = jnp.max(tile, axis=0, keepdims=True)
             top = peak if top is None else jnp.maximum(top, peak)
         total = jnp.zeros_like(top)
-        summed = jnp.zeros((HEAD_DIM, BLOCK), f32)
+        summed = jnp.zeros((HEAD_DIM, FORWARD), f32)
         for i in range(j + 1):
             tile = jnp.exp2(tiles[i] - top)
             total = total + jnp.sum(tile, axis=0, keepdims=True)
-            summed = summed + dot(values[:, i * BLOCK : (i + 1) * BLOCK], tile.astype(bf16), 1, 0)
+            summed = summed + dot(values[:, i * FORWARD : (i + 1) * FORWARD], tile.astype(bf16), 1, 0)
         out_ref[pl.ds(head, HEAD_DIM), columns] = (summed / total).astype(bf16)
         total_ref[0, :, columns] = top + jnp.log2(total)
 
@@ -330,22 +332,26 @@
     queries, grads, keys = q_ref[...], grad_ref[...], k_ref[...]
     inner = jnp.sum(out_ref[...].astype(f32) * grads.astype(f32), axis=0, keepdims=True)
     totals = total_ref[0]
-    causal = diagonal_mask()
+    causal = diagonal_mask(BACKWARD)
     pieces = []
-    for j in range(queries.shape[1] // BLOCK):
-        columns = slice(j * BLOCK, (j + 1) * BLOCK)
+    for j in range(queries.shape[1] // BACKWARD):
+        columns = slice(j * BACKWARD, (j + 1) * BACKWARD)
         query, grad = queries[:, columns], grads[:, columns]
-        query_grad = jnp.zeros((HEAD_DIM, BLOCK), f32)
+        many = (j + 1) * BACKWARD
+        scores = dot(key_s[:many, :], query, 1, 0)
+        grad_all = dot(val_s[:many, :], grad, 1, 0)
+        low, grads_low = [], []
         for i in range(j + 1):
-            rows = slice(i * BLOCK, (i + 1) * BLOCK)
-            probs = jnp.exp2(dot(key_s[rows, :], query, 1, 0) * SCALE - totals[:, columns])
+            rows = slice(i * BACKWARD, (i + 1) * BACKWARD)
+            probs = jnp.exp2(scores[rows] * SCALE - totals[:, columns])
             if i == j:
                 probs = jnp.where(causal, probs, 0.0)
-            gv_s[rows, :] += dot(probs.astype(bf16), grad, 1, 1)
-            grad_probs = dot(val_s[rows, :], grad, 1, 0)
-            grad_scores = (probs * (grad_probs - inner[:, columns])).astype(bf16)
-            query_grad = query_grad + dot(keys[:, rows], grad_scores, 1, 0)
-            gk_s[rows, :] += dot(grad_scores, query, 1, 1)
+            low.append(probs.astype(bf16))
+            grads_low.append((probs * (grad_all[rows] - inner[:, columns])).astype(bf16))
+        low, grads_low = jnp.concatenate(low, axis=0), jnp.concatenate(grads_low, axis=0)
+        gv_s[:many, :] += dot(low, grad, 1, 1)
+        gk_s[:many, :] += dot(grads_low, query, 1, 1)
+        query_grad = dot(keys[:, :many], grads_low, 1, 0)
         pieces.append(query_grad * FACTOR)
     put(group * GROUP + member, turn(jnp.concatenate(pieces, axis=1), cos, -sin))
 
@@ -412,24 +418,38 @@
     )(jnp.stack([start for _, start in pieces]), *[piece for piece, _ in pieces], weight)
 
 
-def weight_grads_kernel(one_ref, rows_ref, scale_ref, two_ref, other_ref, extra_ref, out_ref):
-    one, two = one_ref.shape[0], two_ref.shape[0]
-    total = dot(one_ref[...], rows_ref[...], 1, 0) * scale_ref[...]
-    out_ref[:, :one] = total.T.astype(bf16)
-    total = dot(two_ref[...], other_ref[...], 1, 0)
-    out_ref[:, one : one + two] = total.T.astype(bf16)
-    out_ref[:, one + two :] = extra_ref[...].T.astype(bf16)
-
-
-def weight_grads(one, rows, scale, two, other, extra):
+def weight_grads_kernel(
+    core_ref, one_ref, rows_ref, scale_ref, two_ref, other_ref, extra_ref, keep_ref, send_ref
+):
+    parts = (
+        dot(one_ref[...], rows_ref[...], 1, 0) * scale_ref[...],
+        dot(two_ref[...], other_ref[...], 1, 0),
+        extra_ref[...],
+    )
+    first = core_ref[0] == 0
+    at = 0
+    for part in parts:
+        part = part.T
+        width = part.shape[1]
+        even = [part[i : i + PART] for i in range(0, part.shape[0], 2 * PART)]
+        odd = [part[i + PART : i + 2 * PART] for i in range(0, part.shape[0], 2 * PART)]
+        even, odd = jnp.concatenate(even, axis=0), jnp.concatenate(odd, axis=0)
+        keep_ref[:, at : at + width] = jnp.where(first, even, odd).astype(bf16)
+        send_ref[:, at : at + width] = jnp.where(first, odd, even).astype(bf16)
+        at += width
+
+
+def weight_grads(core, one, rows, scale, two, other, extra):
     tokens, depth = rows.shape
-    block = 256
+    block = 384
     width = one.shape[0] + two.shape[0] + extra.shape[0]
     whole = lambda shape: pl.BlockSpec(shape, lambda d: (0, 0))
+    out = pl.BlockSpec((block // 2, width), lambda d: (d, 0))
     return pl.pallas_call(
         weight_grads_kernel,
         grid=(depth // block,),
         in_specs=[
+            pl.BlockSpec(memory_space=pltpu.SMEM),
             whole(one.shape),
             pl.BlockSpec((tokens, block), lambda d: (0, d)),
             pl.BlockSpec((1, block), lambda d: (0, d)),
@@ -437,29 +457,32 @@
             pl.BlockSpec((tokens, block), lambda d: (0, d)),
             pl.BlockSpec((extra.shape[0], block), lambda d: (0, d)),
         ],
-        out_specs=pl.BlockSpec((block, width), lambda d: (d, 0)),
-        out_shape=jax.ShapeDtypeStruct((depth, width), bf16),
+        out_specs=[out, out],
+        out_shape=[jax.ShapeDtypeStruct((depth // 2, width), bf16)] * 2,
         compiler_params=pltpu.CompilerParams(vmem_limit_bytes=30 * 2**20),
         cost_estimate=BRIEF,
         name="weight_grads",
-    )(one, rows, scale, two, other, extra)
-
-
-def expert_sums_kernel(place_ref, mine_ref, left_ref, right_ref, up_ref, down_ref):
-    total = mine_ref[...].astype(f32) + left_ref[...].astype(f32) + right_ref[...].astype(f32)
+    )(core, one, rows, scale, two, other, extra)
+
+
+def expert_sums_kernel(place_ref, mine_ref, top_ref, low_ref, far_ref, near_ref, up_ref, down_ref):
+    left = jnp.concatenate([top_ref[...].astype(f32), low_ref[...].astype(f32)], axis=0)
+    right = jnp.concatenate([far_ref[...].astype(f32), near_ref[...].astype(f32)], axis=0)
+    total = mine_ref[...].astype(f32) + left + right
     up_ref[...] = total[:, : 2 * FF]
     down_ref[...] = total[:, 2 * FF :].T
 
 
-def expert_sums(place, grads, left, right):
-    rows, width = left.shape
+def expert_sums(place, grads, left_top, left_low, right_top, right_low):
+    half, width = left_top.shape
+    rows = 2 * half
     whole = lambda shape: pl.BlockSpec(shape, lambda i, at: (0, 0))
     return pl.pallas_call(
         expert_sums_kernel,
         grid_spec=pltpu.PrefetchScalarGridSpec(
             num_scalar_prefetch=1,
             grid=(1,),
-            in_specs=[pl.BlockSpec((rows, width), lambda i, at: (at[0], 0))] + [whole((rows, width))] * 2,
+            in_specs=[pl.BlockSpec((rows, width), lambda i, at: (at[0], 0))] + [whole((half, width))] * 4,
             out_specs=[whole((rows, 2 * FF)), whole((FF, rows))],
         ),
         out_shape=[
@@ -469,7 +492,7 @@
         compiler_params=pltpu.CompilerParams(vmem_limit_bytes=24 * 2**20),
         cost_estimate=BRIEF,
         name="expert_sums",
-    )(place, grads, left, right)
+    )(place, grads, left_top, left_low, right_top, right_low)
 
 
 def attend(projected, inverse, cos, sin):
@@ -534,7 +557,7 @@
     )(turned, turned, turned, out, grad, totals, inverse, cos, sin)
 
 
-def build_kernel(*refs):
+def build_kernel(gated, refs):
     tokens, (expand_ref, pick_ref, core_ref) = refs[:8], refs[8:11]
     outs, token_s = refs[11:19], refs[19]
     step = pl.program_id(0)
@@ -561,25 +584,26 @@
         ).astype(bf16)
         rows = dot(hot, token_s[s, :, :HALF], 1, 0)
         parts = [rows[k * ROWS : (k + 1) * ROWS] for k in range(8)]
-        gates = dot(pick_ref[...], token_s[s, :, HALF:], 1, 1).astype(bf16)
-        for d in range(4):
-            values = dot(gates, hot[d * PAIR : d * PAIR + 128], 1, 1)
-            high, low = values[2 * d : 2 * d + 1], values[2 * d + 1 : 2 * d + 2]
-            spare = jnp.where(below == 4, high, jnp.where(below == 5, low, 0.0))
-            spare = jnp.where(across < ROWS, spare, 0.0)
-            part = parts[2 * d]
-            last = jnp.concatenate([part[64:, :128] + spare, part[64:, 128:]], axis=1)
-            parts[2 * d] = jnp.concatenate([part[:64], last], axis=0)
+        if gated:
+            gates = dot(pick_ref[...], token_s[s, :, HALF:], 1, 1).astype(bf16)
+            for d in range(4):
+                values = dot(gates, hot[d * PAIR : d * PAIR + 128], 1, 1)
+                high, low = values[2 * d : 2 * d + 1], values[2 * d + 1 : 2 * d + 2]
+                spare = jnp.where(below == 4, high, jnp.where(below == 5, low, 0.0))
+                spare = jnp.where(across < ROWS, spare, 0.0)
+                part = parts[2 * d]
+                last = jnp.concatenate([part[64:, :128] + spare, part[64:, 128:]], axis=1)
+                parts[2 * d] = jnp.concatenate([part[:64], last], axis=0)
         pieces.append(parts)
     for k in range(8):
         outs[k][0] = jnp.concatenate([pieces[0][k], pieces[1][k]], axis=0).astype(bf16)
 
 
-def build(core, blocks, expand, pick, cost):
+def build(core, blocks, expand, pick, gated):
     count, width = blocks[0].shape
     whole = lambda shape: pl.BlockSpec(shape, lambda r: (0,) * len(shape))
     outs = pl.pallas_call(
-        build_kernel,
+        lambda *refs: build_kernel(gated, refs),
         grid=(4,),
         in_specs=[whole((count, width))] * 8
         + [whole(expand.shape), whole(pick.shape), pl.BlockSpec(memory_space=pltpu.SMEM)],
@@ -587,7 +611,7 @@
         out_shape=[jax.ShapeDtypeStruct((4, PAIR, HALF), bf16)] * 8,
         scratch_shapes=[pltpu.VMEM((2, count, width), bf16)],
         compiler_params=pltpu.CompilerParams(vmem_limit_bytes=VMEM_LIMIT),
-        cost_estimate=cost,
+        cost_estimate=BRIEF if gated else LONG,
         name="build_rows",
     )(*blocks, expand, pick, core)
     return [[outs[2 * d], outs[2 * d + 1]] for d in range(4)]
@@ -660,7 +684,7 @@
             pltpu.VMEM((2, count, EXTRA), bf16),
         ],
         compiler_params=pltpu.CompilerParams(vmem_limit_bytes=VMEM_LIMIT),
-        cost_estimate=LONG if gated else BRIEF,
+        cost_estimate=LONG,
         name="combine_rows",
     )(*[piece for chunk in chunks for piece in chunk], *blocks, expand, aim, pick, core)
 
@@ -722,24 +746,21 @@
         line = head[at : at + 1] + head[at + 1 : at + 2]
         gates.append(jnp.sum(jnp.where(own, line, 0.0), axis=1, keepdims=True))
     gate = jnp.concatenate(gates, axis=0)
-    inner, total = 0.0, 0.0
-    width = FF // 2
-    for c in range(2):
-        low, high = slice(c * width, (c + 1) * width), slice(FF + c * width, FF + (c + 1) * width)
-        gate_part = dot(rows, up_ref[:, low], 1, 0)
-        up_part = dot(rows, up_ref[:, high], 1, 0)
-        sigmoid = 1.0 / (1.0 + jnp.exp(-gate_part))
-        silu = gate_part * sigmoid
-        hidden = silu * up_part
-        back = back_ref[0, :, low]
-        inner = inner + jnp.sum(hidden * back, axis=1, keepdims=True)
-        hidden_ref[0, :, low] = (gate * hidden).astype(bf16)
-        back = gate * back
-        grad_one = (back * up_part * (sigmoid + silu * (1.0 - sigmoid))).astype(bf16)
-        grad_two = (back * silu).astype(bf16)
-        grad_ref[0, :, low] = grad_one
-        grad_ref[0, :, high] = grad_two
-        total = total + dot(grad_one, up_ref[:, low], 1, 1) + dot(grad_two, up_ref[:, high], 1, 1)
+    low, high = slice(0, FF), slice(FF, 2 * FF)
+    gate_part = dot(rows, up_ref[:, low], 1, 0)
+    up_part = dot(rows, up_ref[:, high], 1, 0)
+    sigmoid = 1.0 / (1.0 + jnp.exp(-gate_part))
+    silu = gate_part * sigmoid
+    hidden = silu * up_part
+    back = back_ref[0]
+    inner = jnp.sum(hidden * back, axis=1, keepdims=True)
+    hidden_ref[0] = (gate * hidden).astype(bf16)
+    back = gate * back
+    grad_one = (back * up_part * (sigmoid + silu * (1.0 - sigmoid))).astype(bf16)
+    grad_two = (back * silu).astype(bf16)
+    grad_ref[0, :, low] = grad_one
+    grad_ref[0, :, high] = grad_two
+    total = dot(grad_one, up_ref[:, low], 1, 1) + dot(grad_two, up_ref[:, high], 1, 1)
     below = lax.broadcasted_iota(jnp.int32, (8, 128), 0)
     spares = []
     for i in range(LINE // ROWS):
@@ -898,11 +919,11 @@
     weight_turned = joined_weight.T
     gained_turned = (norm_gains[0][:, None] * joined_weight.astype(f32)).astype(bf16).T
     cos, sin = rotary_tables(sequence_length, HEAD_DIM)
-    near, cot_near, gained_turned, weight_turned, cos, sin, expand_turned, aim, pick_wide = sync(
-        near, cot_near, gained_turned, weight_turned, cos, sin, expand_turned, aim, pick_wide
+    near, gained_turned, weight_turned, cos, sin, expand_turned, aim, pick_wide = sync(
+        near, gained_turned, weight_turned, cos, sin, expand_turned, aim, pick_wide
     )
     pieces = gather_far(tokens, near, place)
-    cot_chunks = build(core_scalar, spread_far(*cot_near), expand, pick, LONG)
+    cot_chunks = build(core_scalar, spread_far(*cot_near), expand, pick, False)
     pieces, cot_chunks = sync(pieces, cot_chunks)
     cot_first = send_first(cot_chunks)
     projected, sequence, inverse = project(pieces, gained_turned, False)
@@ -914,9 +935,8 @@
     attended, cot_first = sync(attended, cot_first)
     far = scatter_far(output_chunk)
     cot_swapped = send_cross(cot_chunks)
-    far, cot_swapped = sync(far, cot_swapped)
     near = scatter_whole(output_chunk, *far)
-    near, cot_far = sync(near, send_far(cot_first[0]))
+    near, cot_swapped, cot_far = sync(near, cot_swapped, send_far(cot_first[0]))
     cot_got = gather_rows(cot_chunks, cot_first, cot_swapped, cot_far)
     middle = inputs + output_chunk(0) + near[0].astype(f32) + near[1].astype(f32)
     mixed_norm, inv_rms_two = norm_rows(middle, norm_gains[1])
@@ -931,7 +951,7 @@
         mixed_low, wide(jnp.concatenate([gates_high, gates_low, slot], axis=1).astype(bf16)), core
     )
     mixed_blocks = spread_far(*mixed_near)
-    mixed_chunks = build(core_scalar, mixed_blocks, expand, pick, BRIEF)
+    mixed_chunks = build(core_scalar, mixed_blocks, expand, pick, True)
     cot_rows, grad_hidden_one = cotangent_rows(core_scalar, *cot_got, down_matrix)
     mixed_first, grad_hidden_one = sync(send_first(mixed_chunks), grad_hidden_one)
     mixed_got = send_rest(mixed_chunks, *mixed_first)
@@ -961,7 +981,8 @@
         grad_blocks, scatter_far(expert_chunk), hidden_gated
     )
     result_mine, result_other = result_rows(core_scalar, hidden_gated, down_matrix)
-    grad_mixed, grad_gate = sum_near(grad_blocks, sum_far(grad_blocks), core)
+    passing, expert_plain = sync(sum_far(grad_blocks), scatter_plain(expert_chunk))
+    grad_mixed, grad_gate = sum_near(grad_blocks, passing, core)
     grad_mixed, grad_gate, result_mine, result_other = sync(
         grad_mixed, grad_gate, result_mine, result_other
     )
@@ -996,17 +1017,20 @@
     )
     far_rows = [move(middle_rows[0], ACROSS, 1, 0), move(middle_rows[1], ACROSS, -1, 0)]
     swapped = swap_core(result_other[0])
-    expert_near = scatter_whole(expert_chunk, *expert_far)
+    expert_near = scatter_summed(expert_chunk, *expert_far)
     grad_projected, grad_scaled = attend_back(
         turned, attended, grad_attended, log_totals, inverse, cos, sin
     )
-    grad_projected, grad_scaled, far_rows, swapped = sync(
-        grad_projected, grad_scaled, far_rows, swapped
-    )
-    joined_grad = weight_grads(
-        grad_scaled, sequence, norm_gains[0:1], attended, grad_attn_seq, small_rows
-    )
-    grad_projected, joined_grad = sync(grad_projected, joined_grad)
+    grad_projected, grad_scaled, far_rows, swapped, expert_near = sync(
+        grad_projected, grad_scaled, far_rows, swapped, expert_near
+    )
+    joined_keep, joined_send = weight_grads(
+        core_scalar, grad_scaled, sequence, norm_gains[0:1], attended, grad_attn_seq, small_rows
+    )
+    joined_grad = (joined_keep.astype(f32) + swap_core(joined_send).astype(f32)).astype(bf16)
+    grad_projected, joined_grad, far_rows, swapped = sync(
+        grad_projected, joined_grad, far_rows, swapped
+    )
 
     def normed_chunk(grads, k):
         start = lax.rem(place + k, 4) * local_rows
@@ -1014,7 +1038,6 @@
         return dot(piece, weight_turned, 0, 0)
 
     far = scatter_far(lambda k: normed_chunk(grad_projected, k))
-    far, expert_near = sync(far, expert_near)
     near = scatter_whole(lambda k: normed_chunk(grad_projected, k), *far)
     result_chunks = [
         [result_mine[0], swapped],
@@ -1022,7 +1045,14 @@
         far_rows,
         [back_wide, other_wide],
     ]
-    joined_terms = exchange(joined_grad.reshape(dp_size, dp_rows, joined_grad.shape[1]))
+    joined_terms = lax.all_to_all(
+        joined_grad.reshape(dp_size // 2, dp_rows, joined_grad.shape[1]),
+        "dp",
+        split_axis=0,
+        concat_axis=0,
+        tiled=True,
+        axis_index_groups=[[2 * i + c for i in range(16)] for c in range(2)],
+    )
     result_blocks = combine(
         core_scalar, result_chunks, mixed_blocks, expand_turned, aim, pick_wide, False
     )
@@ -1033,7 +1063,12 @@
     joined_all = weight_all[:, : query_width + 2 * keyval_width]
     output_all = weight_all[:, query_width + 2 * keyval_width :]
     expert_up_grad, expert_down_grad = expert_sums(
-        jnp.reshape(place, (1,)), expert_grads, *expert_near
+        jnp.reshape(place, (1,)),
+        expert_grads,
+        expert_near[0],
+        expert_plain[0],
+        expert_plain[1],
+        expert_near[1],
     )
     expert_up_grad, expert_down_grad = expert_up_grad[None], expert_down_grad[None]
     query_weight_grad = joined_all[:, :query_width]

time: 490 us -> 475 us (0.969)
  waiting for transfers between devices: 136 us -> 121 us
  Pallas kernels: 122 us -> 114 us
  local copies, waits for them, and re-layouts: 35.1 us -> 40.7 us
    ppermute x64 -> x65, waiting for transfers between devices: 88.5 us -> 68.1 us  [move(): return lax.ppermute(values, 'dp', pairs)]
    ppermute x20 -> x22, waiting for transfers between devices: 47.8 us -> 53 us  [shift_tensor(): lax.ppermute(values, 'tensor', [(i, (i + step) % 4) for i in range(4)])]
    unnamed x181 -> x219, local copies, waits for them, and re-layouts: 25.5 us -> 29.3 us
    ppermute x64 -> x65, starting transfers between devices: 87.5 us -> 90.8 us  [move(): return lax.ppermute(values, 'dp', pairs)]
    ppermute x20 -> x22, starting transfers between devices: 29.3 us -> 28.4 us  [shift_tensor(): lax.ppermute(values, 'tensor', [(i, (i + step) % 4) for i in range(4)])]
  transfers between devices with their start and end apart: 86 -> 89, of which waited for: 29 -> 29; matrix products, arithmetic and copies ran while one was open for 13% -> 13% of each run, Pallas kernels for 18% -> 16%
where the time goes in v4:
time: 475 us; the launch traced here: 467 us
  starting transfers between devices  128 us (27%)
  waiting for transfers between devices  121 us (25%)
  Pallas kernels  114 us (24%)
  local copies, waits for them, and re-layouts  40.7 us (9%)
  other arithmetic  34.1 us (7%)
  matrix products  26.8 us (6%)
    ppermute x65, starting transfers between devices, move(): return lax.ppermute(values, 'dp', pairs)  90.8 us
    ppermute x65, waiting for transfers between devices, move(): return lax.ppermute(values, 'dp', pairs)  68.1 us
    ppermute x22, waiting for transfers between devices, shift_tensor(): lax.ppermute(values, 'tensor', [(i, (i + step) % 4) for i in range(4)])  53 us
    unnamed x219, local copies, waits for them, and re-layouts  29.3 us
    ppermute x22, starting transfers between devices, shift_tensor(): lax.ppermute(values, 'tensor', [(i, (i + step) % 4) for i in range(4)])  28.4 us
    dot_general x14, matrix products, dot(): lax.dot_general(a, b, (((ca,), (cb,)), ((), ())), preferred_element_type=...  26.8 us
    pallas_call x1, Pallas kernels, expert_rows(): pl.pallas_call(expert_kernel, grid=(4,), in_specs=[CORE_SPEC] + [whole_sp...  25.1 us
    pallas_call x2, Pallas kernels, combine(): pl.pallas_call(lambda *refs: combine_kernel(gated, refs), grid=(4,), in_s...  22.5 us
  transfers between devices with their start and end apart: 89, of which 29 were waited for; matrix products, arithmetic and copies ran while one was open for 13% of the time, Pallas kernels for 16%

profile of v4, /device:TPU:1, one launch (start us, length us, event | category | flops | bytes accessed | tf_op | source)
XLA Modules:
  0.0 467.2 jit_solution(11648602293510887380)
XLA Ops:
  42.2 7.2 %build_rows.2 = (bf16[4,144,768]{2,1,0:T(8,128)(2,1)}, bf16[4,144,768]{2,1,0:T(8,128)(2,1)}, bf16[4,144,768]{2,1,0:T(8,128)(2,1)}, bf16[4,144,768]{2,1,0:T(8,128...) custom-call(bf16[256,896]{1,0:T(8,128)(2,1)} %get-tuple-element.476., ...), custom_call_target="tpu_custom_call" | custom-call | flops 99999997952 | bytes 1 | tf_op jit(solution)/shard_map/build_rows/pallas_call | solution.py:605
  67.4 8.6 %attend.1 = (bf16[384,1024]{1,0:T(8,128)(2,1)S(1)}, f32[6,1,1024]{2,1,0:T(1,128)S(1)}, bf16[640,1024]{1,0:T(8,128)(2,1)S(1)}) custom-call(f32[640,1024]{1,0:T(8,128)S(1)} %get-tuple-element.227.q_ref.k_ref.v_ref, f32[640,1024]{1,0:T(8,128)S(1)} %get-tuple-element.227.q_ref.k_ref.v_ref, f32[640,1024]{1,0:T(8,128)S(1)} %get-tuple-element.227.q_ref.k_ref.v_ref, ...), custom_call_target="tpu_custom_call" | custom-call | flops 1 | bytes 1 | tf_op jit(solution)/shard_map/attend/pallas_call | solution.py:501
  81.6 7.8 %collective-permute-done.17 = bf16[128,1536]{1,0:T(8,128)(2,1)S(1)} collective-permute-done((bf16[128,1536]{1,0:T(8,128)(2,1)S(1)}, bf16[128,1536]{1,0:T(8,128)(2,1)S(1)}, u32[]{:S(2)}, u32[]{:S(2)}) %collective-permute-start.17) | collective-permute-done | bytes 393248 | tf_op jit(solution)/shard_map/ppermute | solution.py:72
  97.5 5.6 %collective-permute-done.22.refs_3_ = bf16[4,144,768]{2,1,0:T(8,128)(2,1)} collective-permute-done((bf16[4,144,768]{2,1,0:T(8,128)(2,1)}, bf16[4,144,768]{2,1,0:T(8,128)(2,1)}, u32[]{:S(2)}, u32[]{:S(2)}) %collective-permute-start.22) | collective-permute-done | bytes 884768 | tf_op jit(solution)/shard_map/ppermute | solution.py:167
  105.7 7.7 %collective-permute-done.18 = bf16[256,1536]{1,0:T(8,128)(2,1)} collective-permute-done((bf16[256,1536]{1,0:T(8,128)(2,1)}, bf16[256,1536]{1,0:T(8,128)(2,1)}, u32[]{:S(2)}, u32[]{:S(2)}) %collective-permute-start.18) | collective-permute-done | bytes 786464 | tf_op jit(solution)/shard_map/ppermute | solution.py:72
  141.7 8.1 %build_rows.3 = (bf16[4,144,768]{2,1,0:T(8,128)(2,1)}, bf16[4,144,768]{2,1,0:T(8,128)(2,1)}, bf16[4,144,768]{2,1,0:T(8,128)(2,1)}, bf16[4,144,768]{2,1,0:T(8,128...) custom-call(bf16[256,896]{1,0:T(8,128)(2,1)} %copy-done.56, ...), custom_call_target="tpu_custom_call" | custom-call | flops 1 | bytes 1 | tf_op jit(solution)/shard_map/build_rows/pallas_call | solution.py:605
  155.2 7.0 %cotangent_rows.1 = (bf16[4,576,1536]{2,1,0:T(8,128)(2,1)S(1)}, f32[4,576,512]{2,1,0:T(8,128)S(1)}) custom-call(s32[1]{0:T(128)} %bitcast.6.refs_10_.refs_0_.refs_19_.core_ref, bf16[4,144,768]{2,1,0:T(8,128)(2,1)S(1)} %copy-done.20, bf16[4,144,768]{2,1,0:T(8,128)(2,1)} %collective-permute-done.13.refs_2_, ...), custom_call_target="tpu_custom_call" | custom-call | flops 1 | bytes 1 | tf_op jit(solution)/shard_map/cotangent_rows/pallas_call | solution.py:795
  167.2 4.3 collective-permute-start.36
  174.2 5.4 %collective-permute-start.38 = (bf16[4,144,768]{2,1,0:T(8,128)(2,1)}, bf16[4,144,768]{2,1,0:T(8,128)(2,1)}, u32[]{:S(2)}, u32[]{:S(2)}) collective-permute-start(bf16[4,144,768]{2,1,0:T(8,128)(2,1)} %collective-permute-done.32), channel_id=1, source_target_pairs={{0,28},{4,96},{8,4},{12,104},{16,12},{20,112},{24,20},{28,120},{32... | collective-permute-start | bytes 2654216 | tf_op jit(solution)/shard_map/ppermute | solution.py:167
  179.7 6.2 %collective-permute-done.37.refs_6_ = bf16[4,144,768]{2,1,0:T(8,128)(2,1)} collective-permute-done((bf16[4,144,768]{2,1,0:T(8,128)(2,1)}, bf16[4,144,768]{2,1,0:T(8,128)(2,1)}, u32[]{:S(2)}, u32[]{:S(2)}) %collective-permute-start.37) | collective-permute-done | bytes 884768 | tf_op jit(solution)/shard_map/ppermute | solution.py:167
  185.9 8.9 %collective-permute-done.35.refs_3_ = bf16[4,144,768]{2,1,0:T(8,128)(2,1)} collective-permute-done((bf16[4,144,768]{2,1,0:T(8,128)(2,1)}, bf16[4,144,768]{2,1,0:T(8,128)(2,1)}, u32[]{:S(2)}, u32[]{:S(2)}) %collective-permute-start.35) | collective-permute-done | bytes 884768 | tf_op jit(solution)/shard_map/ppermute | solution.py:167
  195.3 25.1 %expert_rows.1 = (bf16[4,576,1536]{2,1,0:T(8,128)(2,1)}, bf16[4,576,1024]{2,1,0:T(8,128)(2,1)}, bf16[4,576,512]{2,1,0:T(8,128)(2,1)}, bf16[4,144,768]{2,1,0:T(8,...) custom-call(s32[1]{0:T(128)} %bitcast.6.refs_10_.refs_0_.refs_19_.co, ...), custom_call_target="tpu_custom_call" | custom-call | flops 1 | bytes 1 | tf_op jit(solution)/shard_map/expert_rows/pallas_call | solution.py:815
  227.4 11.3 %bitcast_convert_fusion = bf16[1536,1024]{1,0:T(8,128)(2,1)S(1)} fusion(bf16[4,576,1536]{2,1,0:T(8,128)(2,1)} %get-tuple-element.281, bf16[4,576,1024]{2,1,0:T(8,128)(2,1)} %get-tuple-element.282), kind=kOutput, calls=%fused_computation | convolution fusion | flops 7249330176 | bytes 14942208 | tf_op jit(solution)/shard_map/dot_general | solution.py:39
  256.2 7.0 %collective-permute-done.48.refs_7_ = bf16[4,144,768]{2,1,0:T(8,128)(2,1)} collective-permute-done((bf16[4,144,768]{2,1,0:T(8,128)(2,1)}, bf16[4,144,768]{2,1,0:T(8,128)(2,1)}, u32[]{:S(2)}, u32[]{:S(2)}) %collective-permute-start.48) | collective-permute-done | bytes 884768 | tf_op jit(solution)/shard_map/ppermute | solution.py:167
  271.4 11.7 %combine_rows.2 = (bf16[256,896]{1,0:T(8,128)(2,1)}, bf16[256,896]{1,0:T(8,128)(2,1)}, bf16[256,896]{1,0:T(8,128)(2,1)}, bf16[256,896]{1,0:T(8,128)(2,1)}, bf16[...) custom-call(bf16[4,144,768]{2,1,0:T(8,128)(2,1)} %get-tuple-element.292.ref, ...), custom_call_target="tpu_custom_call" | custom-call | flops 99999997952 | bytes 1 | tf_op jit(solution)/shard_map/combine_rows/pallas_call | solution.py:669
  288.1 5.6 %collective-permute-done.53.low_ref = bf16[192,1536]{1,0:T(8,128)(2,1)S(1)} collective-permute-done((bf16[192,1536]{1,0:T(8,128)(2,1)S(1)}, bf16[192,1536]{1,0:T(8,128)(2,1)S(1)}, u32[]{:S(2)}, u32[]{:S(2)}) %collective-permute-start.53) | collective-permute-done | bytes 589856 | tf_op jit(solution)/shard_map/ppermute | solution.py:72
  302.5 8.8 %result_rows.1 = (bf16[4,144,768]{2,1,0:T(8,128)(2,1)}, bf16[4,144,768]{2,1,0:T(8,128)(2,1)}, bf16[4,144,768]{2,1,0:T(8,128)(2,1)}, bf16[4,144,768]{2,1,0:T(8,12...) custom-call(s32[1]{0:T(128)} %bitcast.6.refs_10_.refs_0_.refs_19_.co, ...), custom_call_target="tpu_custom_call" | custom-call | flops 99999997952 | bytes 1 | tf_op jit(solution)/shard_map/result_rows/pallas_call | solution.py:840
  323.1 15.8 %collective-permute-done.60.refs_1_ = bf16[256,1536]{1,0:T(8,128)(2,1)S(1)} collective-permute-done((bf16[256,1536]{1,0:T(8,128)(2,1)S(1)}, bf16[256,1536]{1,0:T(8,128)(2,1)S(1)}, u32[]{:S(2)}, u32[]{:S(2)}) %collective-permute-start.60) | collective-permute-done | bytes 786464 | tf_op jit(solution)/shard_map/ppermute | solution.py:72
  349.9 7.8 %collective-permute-done.65.refs_3_ = bf16[128,1536]{1,0:T(8,128)(2,1)S(1)} collective-permute-done((bf16[128,1536]{1,0:T(8,128)(2,1)S(1)}, bf16[128,1536]{1,0:T(8,128)(2,1)S(1)}, u32[]{:S(2)}, u32[]{:S(2)}) %collective-permute-start.65) | collective-permute-done | bytes 393248 | tf_op jit(solution)/shard_map/ppermute | solution.py:72
  368.4 12.3 %attend_back.1 = (bf16[640,1024]{1,0:T(8,128)(2,1)S(1)}, bf16[640,1024]{1,0:T(8,128)(2,1)S(1)}) custom-call(bf16[640,1024]{1,0:T(8,128)(2,1)S(1)} %copy-done.39, bf16[640,1024]{1,0:T(8,128)(2,1)S(1)} %copy-done.39, bf16[640,1024]{1,0:T(8,128)(2,1)S(1)} %copy-done.39, bf16[384,1024]{1,0:T(8,128)(2,1)S(1)} %get-tuple-element.236.refs_3_.two_ref, ...), custom_call_target="tpu_custom_call" | custom-call | flops 99999997952 | bytes 1 | tf_op jit(solution)/shard_map/attend_back/pallas_call | solution.py:532
  382.5 6.2 %weight_grads.1 = (bf16[768,1152]{1,0:T(8,128)(2,1)S(1)}, bf16[768,1152]{1,0:T(8,128)(2,1)S(1)}) custom-call(s32[1]{0:T(128)} %bitcast.6.refs_10_.refs_0_.refs_19_.core_ref, bf16[640,1024]{1,0:T(8,128)(2,1)S(1)} %get-tuple-element.365.one_ref, bf16[1024,1536]{1,0:T(8,128)(2,1)S(1)} %copy-done.9, f32[1,1536]{1,0:T(1,128)S(1)} %get-tuple-element.477.scale_ref, ...), custom_call_target="tpu_custom_call" | custom-call | flops 1 | bytes 1 | tf_op jit(solution)/shard_map/weight_grads/pallas_call | solution.py:448
  402.6 4.4 all-to-all-start
  415.9 10.8 %combine_rows.3 = (bf16[256,768]{1,0:T(8,128)(2,1)}, bf16[256,768]{1,0:T(8,128)(2,1)}, bf16[256,768]{1,0:T(8,128)(2,1)}, bf16[256,768]{1,0:T(8,128)(2,1)}, bf16[...) custom-call(bf16[4,144,768]{2,1,0:T(8,128)(2,1)} %get-tuple-element.341.ref, ...), custom_call_target="tpu_custom_call" | custom-call | flops 99999997952 | bytes 1 | tf_op jit(solution)/shard_map/combine_rows/pallas_call | solution.py:669
  458.6 4.5 collective-permute-done.82
  (504 shorter events, 256.3 us)
Async XLA Ops:
  6.5 26.9 %collective-permute-start.10 = (bf16[256,896]{1,0:T(8,128)(2,1)}, bf16[256,896]{1,0:T(8,128)(2,1)}, u32[]{:S(2)}, u32[]{:S(2)}) collective-permute-start(bf16[256,896]{1,0:T(8,128)(2,1)} %get-tuple-element.476.refs_0_), channel_id=1, source_target_pairs={{0,96},{4,28},{8,104},{12,4},{16,112},{20,12},{24,120},{28,20},{32... | collective-permute-start | bytes 1376264 | tf_op jit(solution)/shard_map/ppermute | solution.py:167
  50.1 25.9 %collective-permute-start.11 = (bf16[4,144,768]{2,1,0:T(8,128)(2,1)}, bf16[4,144,768]{2,1,0:T(8,128)(2,1)}, u32[]{:S(2)}, u32[]{:S(2)}) collective-permute-start(bf16[4,144,768]{2,1,0:T(8,128)(2,1)} %get-tuple-element.232), channel_id=1, source_target_pairs={{0,8},{4,36},{8,16},{12,44},{16,24},{20,52},{24,0},{28,60},{32,40}... | collective-permute-start | bytes 2654216 | tf_op jit(solution)/shard_map/ppermute | solution.py:167
  50.1 26.0 %collective-permute-start.12 = (bf16[4,144,768]{2,1,0:T(8,128)(2,1)}, bf16[4,144,768]{2,1,0:T(8,128)(2,1)}, u32[]{:S(2)}, u32[]{:S(2)}) collective-permute-start(bf16[4,144,768]{2,1,0:T(8,128)(2,1)} %get-tuple-element.233), channel_id=1, source_target_pairs={{0,24},{4,100},{8,0},{12,108},{16,8},{20,116},{24,16},{28,124},{32... | collective-permute-start | bytes 2654216 | tf_op jit(solution)/shard_map/ppermute | solution.py:167
  52.8 24.9 %collective-permute-start.13 = (bf16[4,144,768]{2,1,0:T(8,128)(2,1)}, bf16[4,144,768]{2,1,0:T(8,128)(2,1)}, u32[]{:S(2)}, u32[]{:S(2)}) collective-permute-start(bf16[4,144,768]{2,1,0:T(8,128)(2,1)} %get-tuple-element.234), channel_id=1, source_target_pairs={{0,8},{4,36},{8,16},{12,44},{16,24},{20,52},{24,0},{28,60},{32,40}... | collective-permute-start | bytes 2654216 | tf_op jit(solution)/shard_map/ppermute | solution.py:167
  52.8 24.9 %collective-permute-start.14 = (bf16[4,144,768]{2,1,0:T(8,128)(2,1)}, bf16[4,144,768]{2,1,0:T(8,128)(2,1)}, u32[]{:S(2)}, u32[]{:S(2)}) collective-permute-start(bf16[4,144,768]{2,1,0:T(8,128)(2,1)} %get-tuple-element.235), channel_id=1, source_target_pairs={{0,24},{4,100},{8,0},{12,108},{16,8},{20,116},{24,16},{28,124},{32... | collective-permute-start | bytes 2654216 | tf_op jit(solution)/shard_map/ppermute | solution.py:167
  55.4 39.7 %collective-permute-start.19 = (bf16[4,144,768]{2,1,0:T(8,128)(2,1)}, bf16[4,144,768]{2,1,0:T(8,128)(2,1)}, u32[]{:S(2)}, u32[]{:S(2)}) collective-permute-start(bf16[4,144,768]{2,1,0:T(8,128)(2,1)} %get-tuple-element.237), channel_id=1, source_target_pairs={{0,4},{4,0},{8,12},{12,8},{16,20},{20,16},{24,28},{28,24},{32,36},... | collective-permute-start | bytes 2654216 | tf_op jit(solution)/shard_map/ppermute | solution.py:167
  149.8 21.8 %collective-permute-start.31 = (bf16[4,144,768]{2,1,0:T(8,128)(2,1)}, bf16[4,144,768]{2,1,0:T(8,128)(2,1)}, u32[]{:S(2)}, u32[]{:S(2)}) collective-permute-start(bf16[4,144,768]{2,1,0:T(8,128)(2,1)} %get-tuple-element.245), channel_id=1, source_target_pairs={{0,8},{4,36},{8,16},{12,44},{16,24},{20,52},{24,0},{28,60},{32,40}... | collective-permute-start | bytes 2654216 | tf_op jit(solution)/shard_map/ppermute | solution.py:167
  149.9 21.7 %collective-permute-start.32 = (bf16[4,144,768]{2,1,0:T(8,128)(2,1)}, bf16[4,144,768]{2,1,0:T(8,128)(2,1)}, u32[]{:S(2)}, u32[]{:S(2)}) collective-permute-start(bf16[4,144,768]{2,1,0:T(8,128)(2,1)} %get-tuple-element.246), channel_id=1, source_target_pairs={{0,24},{4,100},{8,0},{12,108},{16,8},{20,116},{24,16},{28,124},{32... | collective-permute-start | bytes 2654216 | tf_op jit(solution)/shard_map/ppermute | solution.py:167
  152.5 21.7 %collective-permute-start.33 = (bf16[4,144,768]{2,1,0:T(8,128)(2,1)}, bf16[4,144,768]{2,1,0:T(8,128)(2,1)}, u32[]{:S(2)}, u32[]{:S(2)}) collective-permute-start(bf16[4,144,768]{2,1,0:T(8,128)(2,1)} %get-tuple-element.247), channel_id=1, source_target_pairs={{0,8},{4,36},{8,16},{12,44},{16,24},{20,52},{24,0},{28,60},{32,40}... | collective-permute-start | bytes 2654216 | tf_op jit(solution)/shard_map/ppermute | solution.py:167
  227.1 24.8 %collective-permute-start.40 = (bf16[4,144,768]{2,1,0:T(8,128)(2,1)}, bf16[4,144,768]{2,1,0:T(8,128)(2,1)}, u32[]{:S(2)}, u32[]{:S(2)}) collective-permute-start(bf16[4,144,768]{2,1,0:T(8,128)(2,1)} %get-tuple-element.276), channel_id=1, source_target_pairs={{0,4},{4,0},{8,12},{12,8},{16,20},{20,16},{24,28},{28,24},{32,36},... | collective-permute-start | bytes 2654216 | tf_op jit(solution)/shard_map/ppermute | solution.py:167
  268.5 25.2 %collective-permute-start.53 = (bf16[192,1536]{1,0:T(8,128)(2,1)S(1)}, bf16[192,1536]{1,0:T(8,128)(2,1)S(1)}, u32[]{:S(2)}, u32[]{:S(2)}) collective-permute-start(bf16[192,1536]{1,0:T(8,128)(2,1)S(1)} %get-tuple-element.452), channel_id=1, source_target_pairs={{0,1},{1,2},{2,3},{3,0},{4,5},{5,6},{6,7},{7,4},{8,9},{9,10},{10,1... | collective-permute-start | bytes 1769480 | tf_op jit(solution)/shard_map/ppermute | solution.py:72
  268.5 26.9 %collective-permute-start.54 = (bf16[192,1536]{1,0:T(8,128)(2,1)S(1)}, bf16[192,1536]{1,0:T(8,128)(2,1)S(1)}, u32[]{:S(2)}, u32[]{:S(2)}) collective-permute-start(bf16[192,1536]{1,0:T(8,128)(2,1)S(1)} %get-tuple-element.451), channel_id=1, source_target_pairs={{0,3},{1,0},{2,1},{3,2},{4,7},{5,4},{6,5},{7,6},{8,11},{9,8},{10,9... | collective-permute-start | bytes 1769480 | tf_op jit(solution)/shard_map/ppermute | solution.py:72
  286.7 24.6 %collective-permute-start.56 = (bf16[256,896]{1,0:T(8,128)(2,1)}, bf16[256,896]{1,0:T(8,128)(2,1)S(1)}, u32[]{:S(2)}, u32[]{:S(2)}) collective-permute-start(bf16[256,896]{1,0:T(8,128)(2,1)} %get-tuple-element.318), channel_id=1, source_target_pairs={{0,96},{4,28},{8,104},{12,4},{16,112},{20,12},{24,120},{28,20},{32... | collective-permute-start | bytes 1376264 | tf_op jit(solution)/shard_map/ppermute | solution.py:167
  315.1 27.8 %collective-permute-start.62 = (bf16[4,144,768]{2,1,0:T(8,128)(2,1)S(1)}, bf16[4,144,768]{2,1,0:T(8,128)(2,1)S(1)}, u32[]{:S(2)}, u32[]{:S(2)}) collective-permute-start(bf16[4,144,768]{2,1,0:T(8,128)(2,1)S(1)} %copy-done.99), channel_id=1, source_target_pairs={{0,8},{4,36},{8,16},{12,44},{16,24},{20,52},{24,0},{28,60},{32,40}... | collective-permute-start | bytes 2654216 | tf_op jit(solution)/shard_map/ppermute | solution.py:167
  321.5 22.5 %collective-permute-start.63 = (bf16[4,144,768]{2,1,0:T(8,128)(2,1)}, bf16[4,144,768]{2,1,0:T(8,128)(2,1)}, u32[]{:S(2)}, u32[]{:S(2)}) collective-permute-start(bf16[4,144,768]{2,1,0:T(8,128)(2,1)} %get-tuple-element.345), channel_id=1, source_target_pairs={{0,100},{4,24},{8,108},{12,0},{16,116},{20,8},{24,124},{28,16},{32... | collective-permute-start | bytes 2654216 | tf_op jit(solution)/shard_map/ppermute | solution.py:167
  322.8 21.8 %collective-permute-start.64 = (bf16[4,144,768]{2,1,0:T(8,128)(2,1)}, bf16[4,144,768]{2,1,0:T(8,128)(2,1)}, u32[]{:S(2)}, u32[]{:S(2)}) collective-permute-start(bf16[4,144,768]{2,1,0:T(8,128)(2,1)} %get-tuple-element.346), channel_id=1, source_target_pairs={{0,24},{4,100},{8,0},{12,108},{16,8},{20,116},{24,16},{28,124},{32... | collective-permute-start | bytes 2654216 | tf_op jit(solution)/shard_map/ppermute | solution.py:167
  338.9 22.2 %collective-permute-start.67 = (bf16[4,144,768]{2,1,0:T(8,128)(2,1)}, bf16[4,144,768]{2,1,0:T(8,128)(2,1)}, u32[]{:S(2)}, u32[]{:S(2)}) collective-permute-start(bf16[4,144,768]{2,1,0:T(8,128)(2,1)} %get-tuple-element.350), channel_id=1, source_target_pairs={{0,8},{4,36},{8,16},{12,44},{16,24},{20,52},{24,0},{28,60},{32,40}... | collective-permute-start | bytes 2654216 | tf_op jit(solution)/shard_map/ppermute | solution.py:167
  339.8 24.1 %collective-permute-start.68 = (bf16[4,144,768]{2,1,0:T(8,128)(2,1)}, bf16[4,144,768]{2,1,0:T(8,128)(2,1)}, u32[]{:S(2)}, u32[]{:S(2)}) collective-permute-start(bf16[4,144,768]{2,1,0:T(8,128)(2,1)} %get-tuple-element.351), channel_id=1, source_target_pairs={{0,100},{4,24},{8,108},{12,0},{16,116},{20,8},{24,124},{28,16},{32... | collective-permute-start | bytes 2654216 | tf_op jit(solution)/shard_map/ppermute | solution.py:167
  357.8 22.9 %collective-permute-start.72 = (bf16[4,144,768]{2,1,0:T(8,128)(2,1)S(1)}, bf16[4,144,768]{2,1,0:T(8,128)(2,1)S(1)}, u32[]{:S(2)}, u32[]{:S(2)}) collective-permute-start(bf16[4,144,768]{2,1,0:T(8,128)(2,1)S(1)} %copy-done.92), channel_id=1, source_target_pairs={{0,4},{4,0},{8,12},{12,8},{16,20},{20,16},{24,28},{28,24},{32,36},... | collective-permute-start | bytes 2654216 | tf_op jit(solution)/shard_map/ppermute | solution.py:167
  358.7 22.0 %collective-permute-start.70 = (bf16[4,144,768]{2,1,0:T(8,128)(2,1)S(1)}, bf16[4,144,768]{2,1,0:T(8,128)(2,1)S(1)}, u32[]{:S(2)}, u32[]{:S(2)}) collective-permute-start(bf16[4,144,768]{2,1,0:T(8,128)(2,1)S(1)} %copy-done.96), channel_id=1, source_target_pairs={{0,8},{4,36},{8,16},{12,44},{16,24},{20,52},{24,0},{28,60},{32,40}... | collective-permute-start | bytes 2654216 | tf_op jit(solution)/shard_map/ppermute | solution.py:167
  402.6 35.5 %all-to-all-start = ((bf16[16,48,1152]{2,1,0:T(8,128)(2,1)}), bf16[16,48,1152]{2,1,0:T(8,128)(2,1)}, u32[]{:S(2)}, u32[]{:S(2)}) async-start(bf16[16,48,1152]{2,1,0:T(8,128)(2,1)} %bitcast.62), calls=%async_computation | async-start | bytes 3538944 | tf_op jit(solution)/shard_map/all_to_all | solution.py:1048
  410.3 27.7 %collective-permute-start.81 = (bf16[256,1536]{1,0:T(8,128)(2,1)}, bf16[256,1536]{1,0:T(8,128)(2,1)}, u32[]{:S(2)}, u32[]{:S(2)}) collective-permute-start(bf16[256,1536]{1,0:T(8,128)(2,1)} %pad_maximum_fusion.7), channel_id=1, source_target_pairs={{0,3},{1,0},{2,1},{3,2},{4,7},{5,4},{6,5},{7,6},{8,11},{9,8},{10,9... | collective-permute-start | bytes 2359304 | tf_op jit(solution)/shard_map/ppermute | solution.py:72
  415.6 22.5 %collective-permute-start.79 = (bf16[256,1536]{1,0:T(8,128)(2,1)}, bf16[256,1536]{1,0:T(8,128)(2,1)}, u32[]{:S(2)}, u32[]{:S(2)}) collective-permute-start(bf16[256,1536]{1,0:T(8,128)(2,1)} %pad_maximum_fusion.6), channel_id=1, source_target_pairs={{0,1},{1,2},{2,3},{3,0},{4,5},{5,6},{6,7},{7,4},{8,9},{9,10},{10,1... | collective-permute-start | bytes 2359304 | tf_op jit(solution)/shard_map/ppermute | solution.py:72
  435.0 22.1 %collective-permute-start.83 = (bf16[256,768]{1,0:T(8,128)(2,1)}, bf16[256,768]{1,0:T(8,128)(2,1)}, u32[]{:S(2)}, u32[]{:S(2)}) collective-permute-start(bf16[256,768]{1,0:T(8,128)(2,1)} %get-tuple-element.389), channel_id=1, source_target_pairs={{0,96},{4,28},{8,104},{12,4},{16,112},{20,12},{24,120},{28,20},{32... | collective-permute-start | bytes 1179656 | tf_op jit(solution)/shard_map/ppermute | solution.py:167
  (174 other events, 2109.1 us)

commit v5 on v4

--- a/solution.py
+++ b/solution.py
@@ -728,7 +728,7 @@
     down_ref, rows_ref, hidden_ref, mine_s = refs[9:]
     _, rows = whole_rows(core_ref, mine, other, mine_s)
     rows_ref[0] = rows
-    hidden_ref[0] = dot(rows, down_ref[...], 1, 1)
+    hidden_ref[0] = dot(rows, down_ref[...], 1, 1).astype(bf16)
 
 
 def expert_kernel(*refs):
@@ -752,7 +752,7 @@
     sigmoid = 1.0 / (1.0 + jnp.exp(-gate_part))
     silu = gate_part * sigmoid
     hidden = silu * up_part
-    back = back_ref[0]
+    back = back_ref[0].astype(f32)
     inner = jnp.sum(hidden * back, axis=1, keepdims=True)
     hidden_ref[0] = (gate * hidden).astype(bf16)
     back = gate * back
@@ -802,12 +802,12 @@
         out_specs=(line_spec(LINE, 2 * HALF), line_spec(LINE, FF)),
         out_shape=(
             jax.ShapeDtypeStruct((4, LINE, 2 * HALF), bf16),
-            jax.ShapeDtypeStruct((4, LINE, FF), f32),
+            jax.ShapeDtypeStruct((4, LINE, FF), bf16),
         ),
         scratch_shapes=[pltpu.VMEM((LINE, HALF), bf16)],
         cost_estimate=BRIEF,
         name="cotangent_rows",
-        compiler_params=pltpu.CompilerParams(vmem_limit_bytes=28 * 2**20),
+        compiler_params=pltpu.CompilerParams(vmem_limit_bytes=VMEM_LIMIT),
     )(core, *mine, *other, down)
 
 

time: 475 us -> 475 us (level)
  local copies, waits for them, and re-layouts: 40.7 us -> 33.8 us
    unnamed x219 -> x209, local copies, waits for them, and re-layouts: 29.3 us -> 22.4 us
  transfers between devices with their start and end apart: 89 -> 89, of which waited for: 29 -> 30; matrix products, arithmetic and copies ran while one was open for 13% -> 13% of each run, Pallas kernels for 16% -> 17%
where the time goes in v5:
time: 475 us; the launch traced here: 466 us
  starting transfers between devices  132 us (28%)
  waiting for transfers between devices  120 us (25%)
  Pallas kernels  117 us (25%)
  other arithmetic  34 us (7%)
  local copies, waits for them, and re-layouts  33.8 us (7%)
  matrix products  26.8 us (6%)
    ppermute x65, starting transfers between devices, move(): return lax.ppermute(values, 'dp', pairs)  95.1 us
    ppermute x65, waiting for transfers between devices, move(): return lax.ppermute(values, 'dp', pairs)  70.8 us
    ppermute x22, waiting for transfers between devices, shift_tensor(): lax.ppermute(values, 'tensor', [(i, (i + step) % 4) for i in range(4)])  49.5 us
    ppermute x22, starting transfers between devices, shift_tensor(): lax.ppermute(values, 'tensor', [(i, (i + step) % 4) for i in range(4)])  28.5 us
    dot_general x14, matrix products, dot(): lax.dot_general(a, b, (((ca,), (cb,)), ((), ())), preferred_element_type=...  26.8 us
    pallas_call x1, Pallas kernels, expert_rows(): pl.pallas_call(expert_kernel, grid=(4,), in_specs=[CORE_SPEC] + [whole_sp...  25 us
    pallas_call x2, Pallas kernels, combine(): pl.pallas_call(lambda *refs: combine_kernel(gated, refs), grid=(4,), in_s...  22.5 us
    unnamed x209, local copies, waits for them, and re-layouts  22.4 us
  transfers between devices with their start and end apart: 89, of which 30 were waited for; matrix products, arithmetic and copies ran while one was open for 13% of the time, Pallas kernels for 17%

profile of v5, /device:TPU:1, one launch (start us, length us, event | category | flops | bytes accessed | tf_op | source)
XLA Modules:
  0.0 466.4 jit_solution(7653727436331667950)
XLA Ops:
  42.2 7.2 %build_rows.2 = (bf16[4,144,768]{2,1,0:T(8,128)(2,1)}, bf16[4,144,768]{2,1,0:T(8,128)(2,1)}, bf16[4,144,768]{2,1,0:T(8,128)(2,1)}, bf16[4,144,768]{2,1,0:T(8,128...) custom-call(bf16[256,896]{1,0:T(8,128)(2,1)} %get-tuple-element.476., ...), custom_call_target="tpu_custom_call" | custom-call | flops 99999997952 | bytes 1 | tf_op jit(solution)/shard_map/build_rows/pallas_call | solution.py:605
  67.3 8.6 %attend.1 = (bf16[384,1024]{1,0:T(8,128)(2,1)S(1)}, f32[6,1,1024]{2,1,0:T(1,128)S(1)}, bf16[640,1024]{1,0:T(8,128)(2,1)S(1)}) custom-call(f32[640,1024]{1,0:T(8,128)S(1)} %get-tuple-element.227.q_ref.k_ref.v_ref, f32[640,1024]{1,0:T(8,128)S(1)} %get-tuple-element.227.q_ref.k_ref.v_ref, f32[640,1024]{1,0:T(8,128)S(1)} %get-tuple-element.227.q_ref.k_ref.v_ref, ...), custom_call_target="tpu_custom_call" | custom-call | flops 1 | bytes 1 | tf_op jit(solution)/shard_map/attend/pallas_call | solution.py:501
  81.6 7.9 %collective-permute-done.17 = bf16[128,1536]{1,0:T(8,128)(2,1)S(1)} collective-permute-done((bf16[128,1536]{1,0:T(8,128)(2,1)S(1)}, bf16[128,1536]{1,0:T(8,128)(2,1)S(1)}, u32[]{:S(2)}, u32[]{:S(2)}) %collective-permute-start.17) | collective-permute-done | bytes 393248 | tf_op jit(solution)/shard_map/ppermute | solution.py:72
  96.5 6.7 %collective-permute-done.22.refs_3_ = bf16[4,144,768]{2,1,0:T(8,128)(2,1)} collective-permute-done((bf16[4,144,768]{2,1,0:T(8,128)(2,1)}, bf16[4,144,768]{2,1,0:T(8,128)(2,1)}, u32[]{:S(2)}, u32[]{:S(2)}) %collective-permute-start.22) | collective-permute-done | bytes 884768 | tf_op jit(solution)/shard_map/ppermute | solution.py:167
  105.7 7.6 %collective-permute-done.18 = bf16[256,1536]{1,0:T(8,128)(2,1)} collective-permute-done((bf16[256,1536]{1,0:T(8,128)(2,1)}, bf16[256,1536]{1,0:T(8,128)(2,1)}, u32[]{:S(2)}, u32[]{:S(2)}) %collective-permute-start.18) | collective-permute-done | bytes 786464 | tf_op jit(solution)/shard_map/ppermute | solution.py:72
  141.3 8.1 %build_rows.3 = (bf16[4,144,768]{2,1,0:T(8,128)(2,1)}, bf16[4,144,768]{2,1,0:T(8,128)(2,1)}, bf16[4,144,768]{2,1,0:T(8,128)(2,1)}, bf16[4,144,768]{2,1,0:T(8,128...) custom-call(bf16[256,896]{1,0:T(8,128)(2,1)} %copy-done.50, ...), custom_call_target="tpu_custom_call" | custom-call | flops 1 | bytes 1 | tf_op jit(solution)/shard_map/build_rows/pallas_call | solution.py:605
  154.8 9.7 %cotangent_rows.1 = (bf16[4,576,1536]{2,1,0:T(8,128)(2,1)}, bf16[4,576,512]{2,1,0:T(8,128)(2,1)}) custom-call(s32[1]{0:T(128)} %bitcast.6.refs_10_.refs_0_.refs_19_.core_ref, bf16[4,144,768]{2,1,0:T(8,128)(2,1)} %get-tuple-element.249.refs_1_, bf16[4,144,768]{2,1,0:T(8,128)(2,1)} %collective-permute-done.13.refs_2_, ...), custom_call_target="tpu_custom_call" | custom-call | flops 1 | bytes 1 | tf_op jit(solution)/shard_map/cotangent_rows/pallas_call | solution.py:795
  164.5 4.4 collective-permute-start.36
  172.7 6.6 %collective-permute-start.38 = (bf16[4,144,768]{2,1,0:T(8,128)(2,1)}, bf16[4,144,768]{2,1,0:T(8,128)(2,1)}, u32[]{:S(2)}, u32[]{:S(2)}) collective-permute-start(bf16[4,144,768]{2,1,0:T(8,128)(2,1)} %collective-permute-done.32), channel_id=1, source_target_pairs={{0,28},{4,96},{8,4},{12,104},{16,12},{20,112},{24,20},{28,120},{32... | collective-permute-start | bytes 2654216 | tf_op jit(solution)/shard_map/ppermute | solution.py:167
  179.3 6.3 %collective-permute-done.37.refs_6_ = bf16[4,144,768]{2,1,0:T(8,128)(2,1)} collective-permute-done((bf16[4,144,768]{2,1,0:T(8,128)(2,1)}, bf16[4,144,768]{2,1,0:T(8,128)(2,1)}, u32[]{:S(2)}, u32[]{:S(2)}) %collective-permute-start.37) | collective-permute-done | bytes 884768 | tf_op jit(solution)/shard_map/ppermute | solution.py:167
  185.5 6.5 %collective-permute-done.35.refs_3_ = bf16[4,144,768]{2,1,0:T(8,128)(2,1)} collective-permute-done((bf16[4,144,768]{2,1,0:T(8,128)(2,1)}, bf16[4,144,768]{2,1,0:T(8,128)(2,1)}, u32[]{:S(2)}, u32[]{:S(2)}) %collective-permute-start.35) | collective-permute-done | bytes 884768 | tf_op jit(solution)/shard_map/ppermute | solution.py:167
  195.0 25.0 %expert_rows.1 = (bf16[4,576,1536]{2,1,0:T(8,128)(2,1)}, bf16[4,576,1024]{2,1,0:T(8,128)(2,1)}, bf16[4,576,512]{2,1,0:T(8,128)(2,1)}, bf16[4,144,768]{2,1,0:T(8,...) custom-call(s32[1]{0:T(128)} %bitcast.6.refs_10_.refs_0_.refs_19_.co, ...), custom_call_target="tpu_custom_call" | custom-call | flops 1 | bytes 1 | tf_op jit(solution)/shard_map/expert_rows/pallas_call | solution.py:815
  226.9 11.3 %bitcast_convert_fusion = bf16[1536,1024]{1,0:T(8,128)(2,1)S(1)} fusion(bf16[4,576,1536]{2,1,0:T(8,128)(2,1)} %get-tuple-element.281, bf16[4,576,1024]{2,1,0:T(8,128)(2,1)} %get-tuple-element.282), kind=kOutput, calls=%fused_computation | convolution fusion | flops 7249330176 | bytes 14942208 | tf_op jit(solution)/shard_map/dot_general | solution.py:39
  255.7 6.3 %collective-permute-done.48.refs_7_ = bf16[4,144,768]{2,1,0:T(8,128)(2,1)} collective-permute-done((bf16[4,144,768]{2,1,0:T(8,128)(2,1)}, bf16[4,144,768]{2,1,0:T(8,128)(2,1)}, u32[]{:S(2)}, u32[]{:S(2)}) %collective-permute-start.48) | collective-permute-done | bytes 884768 | tf_op jit(solution)/shard_map/ppermute | solution.py:167
  270.6 11.7 %combine_rows.2 = (bf16[256,896]{1,0:T(8,128)(2,1)}, bf16[256,896]{1,0:T(8,128)(2,1)}, bf16[256,896]{1,0:T(8,128)(2,1)}, bf16[256,896]{1,0:T(8,128)(2,1)}, bf16[...) custom-call(bf16[4,144,768]{2,1,0:T(8,128)(2,1)} %get-tuple-element.292.ref, ...), custom_call_target="tpu_custom_call" | custom-call | flops 99999997952 | bytes 1 | tf_op jit(solution)/shard_map/combine_rows/pallas_call | solution.py:669
  282.5 4.3 collective-permute-start.52
  303.2 8.8 %result_rows.1 = (bf16[4,144,768]{2,1,0:T(8,128)(2,1)}, bf16[4,144,768]{2,1,0:T(8,128)(2,1)}, bf16[4,144,768]{2,1,0:T(8,128)(2,1)}, bf16[4,144,768]{2,1,0:T(8,12...) custom-call(s32[1]{0:T(128)} %bitcast.6.refs_10_.refs_0_.refs_19_.co, ...), custom_call_target="tpu_custom_call" | custom-call | flops 99999997952 | bytes 1 | tf_op jit(solution)/shard_map/result_rows/pallas_call | solution.py:840
  323.0 15.2 %collective-permute-done.60.refs_1_ = bf16[256,1536]{1,0:T(8,128)(2,1)S(1)} collective-permute-done((bf16[256,1536]{1,0:T(8,128)(2,1)S(1)}, bf16[256,1536]{1,0:T(8,128)(2,1)S(1)}, u32[]{:S(2)}, u32[]{:S(2)}) %collective-permute-start.60) | collective-permute-done | bytes 786464 | tf_op jit(solution)/shard_map/ppermute | solution.py:72
  348.9 7.5 %collective-permute-done.65.refs_3_ = bf16[128,1536]{1,0:T(8,128)(2,1)S(1)} collective-permute-done((bf16[128,1536]{1,0:T(8,128)(2,1)S(1)}, bf16[128,1536]{1,0:T(8,128)(2,1)S(1)}, u32[]{:S(2)}, u32[]{:S(2)}) %collective-permute-start.65) | collective-permute-done | bytes 393248 | tf_op jit(solution)/shard_map/ppermute | solution.py:72
  367.3 12.3 %attend_back.1 = (bf16[640,1024]{1,0:T(8,128)(2,1)S(1)}, bf16[640,1024]{1,0:T(8,128)(2,1)S(1)}) custom-call(bf16[640,1024]{1,0:T(8,128)(2,1)S(1)} %copy-done.33, bf16[640,1024]{1,0:T(8,128)(2,1)S(1)} %copy-done.33, bf16[640,1024]{1,0:T(8,128)(2,1)S(1)} %copy-done.33, bf16[384,1024]{1,0:T(8,128)(2,1)S(1)} %get-tuple-element.236.refs_3_.two_ref, ...), custom_call_target="tpu_custom_call" | custom-call | flops 99999997952 | bytes 1 | tf_op jit(solution)/shard_map/attend_back/pallas_call | solution.py:532
  381.4 6.2 %weight_grads.1 = (bf16[768,1152]{1,0:T(8,128)(2,1)S(1)}, bf16[768,1152]{1,0:T(8,128)(2,1)S(1)}) custom-call(s32[1]{0:T(128)} %bitcast.6.refs_10_.refs_0_.refs_19_.core_ref, bf16[640,1024]{1,0:T(8,128)(2,1)S(1)} %get-tuple-element.365.one_ref, bf16[1024,1536]{1,0:T(8,128)(2,1)S(1)} %copy-done.8, f32[1,1536]{1,0:T(1,128)S(1)} %get-tuple-element.477.scale_ref, ...), custom_call_target="tpu_custom_call" | custom-call | flops 1 | bytes 1 | tf_op jit(solution)/shard_map/weight_grads/pallas_call | solution.py:448
  401.5 4.4 all-to-all-start
  414.8 10.8 %combine_rows.3 = (bf16[256,768]{1,0:T(8,128)(2,1)}, bf16[256,768]{1,0:T(8,128)(2,1)}, bf16[256,768]{1,0:T(8,128)(2,1)}, bf16[256,768]{1,0:T(8,128)(2,1)}, bf16[...) custom-call(bf16[4,144,768]{2,1,0:T(8,128)(2,1)} %get-tuple-element.341.ref, ...), custom_call_target="tpu_custom_call" | custom-call | flops 99999997952 | bytes 1 | tf_op jit(solution)/shard_map/combine_rows/pallas_call | solution.py:669
  457.7 4.5 collective-permute-done.82
  (494 shorter events, 256.0 us)
Async XLA Ops:
  4.1 21.4 %collective-permute-start.5 = (bf16[256,896]{1,0:T(8,128)(2,1)}, bf16[256,896]{1,0:T(8,128)(2,1)}, u32[]{:S(2)}, u32[]{:S(2)}) collective-permute-start(bf16[256,896]{1,0:T(8,128)(2,1)} %get-tuple-element.476.refs_0_), channel_id=1, source_target_pairs={{0,32},{4,12},{8,40},{12,20},{16,48},{20,28},{24,56},{28,4},{32,64... | collective-permute-start | bytes 1376264 | tf_op jit(solution)/shard_map/ppermute | solution.py:167
  6.5 26.9 %collective-permute-start.10 = (bf16[256,896]{1,0:T(8,128)(2,1)}, bf16[256,896]{1,0:T(8,128)(2,1)}, u32[]{:S(2)}, u32[]{:S(2)}) collective-permute-start(bf16[256,896]{1,0:T(8,128)(2,1)} %get-tuple-element.476.refs_0_), channel_id=1, source_target_pairs={{0,96},{4,28},{8,104},{12,4},{16,112},{20,12},{24,120},{28,20},{32... | collective-permute-start | bytes 1376264 | tf_op jit(solution)/shard_map/ppermute | solution.py:167
  50.1 25.9 %collective-permute-start.11 = (bf16[4,144,768]{2,1,0:T(8,128)(2,1)}, bf16[4,144,768]{2,1,0:T(8,128)(2,1)}, u32[]{:S(2)}, u32[]{:S(2)}) collective-permute-start(bf16[4,144,768]{2,1,0:T(8,128)(2,1)} %get-tuple-element.232), channel_id=1, source_target_pairs={{0,8},{4,36},{8,16},{12,44},{16,24},{20,52},{24,0},{28,60},{32,40}... | collective-permute-start | bytes 2654216 | tf_op jit(solution)/shard_map/ppermute | solution.py:167
  50.1 26.0 %collective-permute-start.12 = (bf16[4,144,768]{2,1,0:T(8,128)(2,1)}, bf16[4,144,768]{2,1,0:T(8,128)(2,1)}, u32[]{:S(2)}, u32[]{:S(2)}) collective-permute-start(bf16[4,144,768]{2,1,0:T(8,128)(2,1)} %get-tuple-element.233), channel_id=1, source_target_pairs={{0,24},{4,100},{8,0},{12,108},{16,8},{20,116},{24,16},{28,124},{32... | collective-permute-start | bytes 2654216 | tf_op jit(solution)/shard_map/ppermute | solution.py:167
  52.8 24.8 %collective-permute-start.13 = (bf16[4,144,768]{2,1,0:T(8,128)(2,1)}, bf16[4,144,768]{2,1,0:T(8,128)(2,1)}, u32[]{:S(2)}, u32[]{:S(2)}) collective-permute-start(bf16[4,144,768]{2,1,0:T(8,128)(2,1)} %get-tuple-element.234), channel_id=1, source_target_pairs={{0,8},{4,36},{8,16},{12,44},{16,24},{20,52},{24,0},{28,60},{32,40}... | collective-permute-start | bytes 2654216 | tf_op jit(solution)/shard_map/ppermute | solution.py:167
  52.8 24.8 %collective-permute-start.14 = (bf16[4,144,768]{2,1,0:T(8,128)(2,1)}, bf16[4,144,768]{2,1,0:T(8,128)(2,1)}, u32[]{:S(2)}, u32[]{:S(2)}) collective-permute-start(bf16[4,144,768]{2,1,0:T(8,128)(2,1)} %get-tuple-element.235), channel_id=1, source_target_pairs={{0,24},{4,100},{8,0},{12,108},{16,8},{20,116},{24,16},{28,124},{32... | collective-permute-start | bytes 2654216 | tf_op jit(solution)/shard_map/ppermute | solution.py:167
  55.4 39.6 %collective-permute-start.19 = (bf16[4,144,768]{2,1,0:T(8,128)(2,1)}, bf16[4,144,768]{2,1,0:T(8,128)(2,1)}, u32[]{:S(2)}, u32[]{:S(2)}) collective-permute-start(bf16[4,144,768]{2,1,0:T(8,128)(2,1)} %get-tuple-element.237), channel_id=1, source_target_pairs={{0,4},{4,0},{8,12},{12,8},{16,20},{20,16},{24,28},{28,24},{32,36},... | collective-permute-start | bytes 2654216 | tf_op jit(solution)/shard_map/ppermute | solution.py:167
  172.7 22.3 %collective-permute-start.38 = (bf16[4,144,768]{2,1,0:T(8,128)(2,1)}, bf16[4,144,768]{2,1,0:T(8,128)(2,1)}, u32[]{:S(2)}, u32[]{:S(2)}) collective-permute-start(bf16[4,144,768]{2,1,0:T(8,128)(2,1)} %collective-permute-done.32), channel_id=1, source_target_pairs={{0,28},{4,96},{8,4},{12,104},{16,12},{20,112},{24,20},{28,120},{32... | collective-permute-start | bytes 2654216 | tf_op jit(solution)/shard_map/ppermute | solution.py:167
  226.6 24.9 %collective-permute-start.40 = (bf16[4,144,768]{2,1,0:T(8,128)(2,1)}, bf16[4,144,768]{2,1,0:T(8,128)(2,1)}, u32[]{:S(2)}, u32[]{:S(2)}) collective-permute-start(bf16[4,144,768]{2,1,0:T(8,128)(2,1)} %get-tuple-element.276), channel_id=1, source_target_pairs={{0,4},{4,0},{8,12},{12,8},{16,20},{20,16},{24,28},{28,24},{32,36},... | collective-permute-start | bytes 2654216 | tf_op jit(solution)/shard_map/ppermute | solution.py:167
  267.8 24.4 %collective-permute-start.53 = (bf16[192,1536]{1,0:T(8,128)(2,1)S(1)}, bf16[192,1536]{1,0:T(8,128)(2,1)S(1)}, u32[]{:S(2)}, u32[]{:S(2)}) collective-permute-start(bf16[192,1536]{1,0:T(8,128)(2,1)S(1)} %get-tuple-element.452), channel_id=1, source_target_pairs={{0,1},{1,2},{2,3},{3,0},{4,5},{5,6},{6,7},{7,4},{8,9},{9,10},{10,1... | collective-permute-start | bytes 1769480 | tf_op jit(solution)/shard_map/ppermute | solution.py:72
  267.8 26.9 %collective-permute-start.54 = (bf16[192,1536]{1,0:T(8,128)(2,1)S(1)}, bf16[192,1536]{1,0:T(8,128)(2,1)S(1)}, u32[]{:S(2)}, u32[]{:S(2)}) collective-permute-start(bf16[192,1536]{1,0:T(8,128)(2,1)S(1)} %get-tuple-element.451), channel_id=1, source_target_pairs={{0,3},{1,0},{2,1},{3,2},{4,7},{5,4},{6,5},{7,6},{8,11},{9,8},{10,9... | collective-permute-start | bytes 1769480 | tf_op jit(solution)/shard_map/ppermute | solution.py:72
  286.7 25.3 %collective-permute-start.56 = (bf16[256,896]{1,0:T(8,128)(2,1)}, bf16[256,896]{1,0:T(8,128)(2,1)S(1)}, u32[]{:S(2)}, u32[]{:S(2)}) collective-permute-start(bf16[256,896]{1,0:T(8,128)(2,1)} %get-tuple-element.318), channel_id=1, source_target_pairs={{0,96},{4,28},{8,104},{12,4},{16,112},{20,12},{24,120},{28,20},{32... | collective-permute-start | bytes 1376264 | tf_op jit(solution)/shard_map/ppermute | solution.py:167
  315.8 26.3 %collective-permute-start.62 = (bf16[4,144,768]{2,1,0:T(8,128)(2,1)S(1)}, bf16[4,144,768]{2,1,0:T(8,128)(2,1)S(1)}, u32[]{:S(2)}, u32[]{:S(2)}) collective-permute-start(bf16[4,144,768]{2,1,0:T(8,128)(2,1)S(1)} %copy-done.94), channel_id=1, source_target_pairs={{0,8},{4,36},{8,16},{12,44},{16,24},{20,52},{24,0},{28,60},{32,40}... | collective-permute-start | bytes 2654216 | tf_op jit(solution)/shard_map/ppermute | solution.py:167
  317.8 21.4 %collective-permute-start.61 = (bf16[256,1536]{1,0:T(8,128)(2,1)S(1)}, bf16[256,1536]{1,0:T(8,128)(2,1)S(1)}, u32[]{:S(2)}, u32[]{:S(2)}) collective-permute-start(bf16[256,1536]{1,0:T(8,128)(2,1)S(1)} %get-tuple-element.445.refs_0_), channel_id=1, source_target_pairs={{0,3},{1,0},{2,1},{3,2},{4,7},{5,4},{6,5},{7,6},{8,11},{9,8},{10,9... | collective-permute-start | bytes 2359304 | tf_op jit(solution)/shard_map/ppermute | solution.py:72
  320.7 22.5 %collective-permute-start.63 = (bf16[4,144,768]{2,1,0:T(8,128)(2,1)}, bf16[4,144,768]{2,1,0:T(8,128)(2,1)}, u32[]{:S(2)}, u32[]{:S(2)}) collective-permute-start(bf16[4,144,768]{2,1,0:T(8,128)(2,1)} %get-tuple-element.345), channel_id=1, source_target_pairs={{0,100},{4,24},{8,108},{12,0},{16,116},{20,8},{24,124},{28,16},{32... | collective-permute-start | bytes 2654216 | tf_op jit(solution)/shard_map/ppermute | solution.py:167
  322.5 21.0 %collective-permute-start.64 = (bf16[4,144,768]{2,1,0:T(8,128)(2,1)}, bf16[4,144,768]{2,1,0:T(8,128)(2,1)}, u32[]{:S(2)}, u32[]{:S(2)}) collective-permute-start(bf16[4,144,768]{2,1,0:T(8,128)(2,1)} %get-tuple-element.346), channel_id=1, source_target_pairs={{0,24},{4,100},{8,0},{12,108},{16,8},{20,116},{24,16},{28,124},{32... | collective-permute-start | bytes 2654216 | tf_op jit(solution)/shard_map/ppermute | solution.py:167
  338.2 22.5 %collective-permute-start.67 = (bf16[4,144,768]{2,1,0:T(8,128)(2,1)}, bf16[4,144,768]{2,1,0:T(8,128)(2,1)}, u32[]{:S(2)}, u32[]{:S(2)}) collective-permute-start(bf16[4,144,768]{2,1,0:T(8,128)(2,1)} %get-tuple-element.350), channel_id=1, source_target_pairs={{0,8},{4,36},{8,16},{12,44},{16,24},{20,52},{24,0},{28,60},{32,40}... | collective-permute-start | bytes 2654216 | tf_op jit(solution)/shard_map/ppermute | solution.py:167
  339.3 23.6 %collective-permute-start.68 = (bf16[4,144,768]{2,1,0:T(8,128)(2,1)}, bf16[4,144,768]{2,1,0:T(8,128)(2,1)}, u32[]{:S(2)}, u32[]{:S(2)}) collective-permute-start(bf16[4,144,768]{2,1,0:T(8,128)(2,1)} %get-tuple-element.351), channel_id=1, source_target_pairs={{0,100},{4,24},{8,108},{12,0},{16,116},{20,8},{24,124},{28,16},{32... | collective-permute-start | bytes 2654216 | tf_op jit(solution)/shard_map/ppermute | solution.py:167
  356.4 23.3 %collective-permute-start.72 = (bf16[4,144,768]{2,1,0:T(8,128)(2,1)S(1)}, bf16[4,144,768]{2,1,0:T(8,128)(2,1)S(1)}, u32[]{:S(2)}, u32[]{:S(2)}) collective-permute-start(bf16[4,144,768]{2,1,0:T(8,128)(2,1)S(1)} %copy-done.87), channel_id=1, source_target_pairs={{0,4},{4,0},{8,12},{12,8},{16,20},{20,16},{24,28},{28,24},{32,36},... | collective-permute-start | bytes 2654216 | tf_op jit(solution)/shard_map/ppermute | solution.py:167
  357.6 22.0 %collective-permute-start.70 = (bf16[4,144,768]{2,1,0:T(8,128)(2,1)S(1)}, bf16[4,144,768]{2,1,0:T(8,128)(2,1)S(1)}, u32[]{:S(2)}, u32[]{:S(2)}) collective-permute-start(bf16[4,144,768]{2,1,0:T(8,128)(2,1)S(1)} %copy-done.91), channel_id=1, source_target_pairs={{0,8},{4,36},{8,16},{12,44},{16,24},{20,52},{24,0},{28,60},{32,40}... | collective-permute-start | bytes 2654216 | tf_op jit(solution)/shard_map/ppermute | solution.py:167
  401.5 35.7 %all-to-all-start = ((bf16[16,48,1152]{2,1,0:T(8,128)(2,1)}), bf16[16,48,1152]{2,1,0:T(8,128)(2,1)}, u32[]{:S(2)}, u32[]{:S(2)}) async-start(bf16[16,48,1152]{2,1,0:T(8,128)(2,1)} %bitcast.58), calls=%async_computation | async-start | bytes 3538944 | tf_op jit(solution)/shard_map/all_to_all | solution.py:1048
  409.2 28.0 %collective-permute-start.81 = (bf16[256,1536]{1,0:T(8,128)(2,1)}, bf16[256,1536]{1,0:T(8,128)(2,1)}, u32[]{:S(2)}, u32[]{:S(2)}) collective-permute-start(bf16[256,1536]{1,0:T(8,128)(2,1)} %pad_maximum_fusion.7), channel_id=1, source_target_pairs={{0,3},{1,0},{2,1},{3,2},{4,7},{5,4},{6,5},{7,6},{8,11},{9,8},{10,9... | collective-permute-start | bytes 2359304 | tf_op jit(solution)/shard_map/ppermute | solution.py:72
  414.5 22.7 %collective-permute-start.79 = (bf16[256,1536]{1,0:T(8,128)(2,1)}, bf16[256,1536]{1,0:T(8,128)(2,1)}, u32[]{:S(2)}, u32[]{:S(2)}) collective-permute-start(bf16[256,1536]{1,0:T(8,128)(2,1)} %pad_maximum_fusion.6), channel_id=1, source_target_pairs={{0,1},{1,2},{2,3},{3,0},{4,5},{5,6},{6,7},{7,4},{8,9},{9,10},{10,1... | collective-permute-start | bytes 2359304 | tf_op jit(solution)/shard_map/ppermute | solution.py:72
  433.9 22.1 %collective-permute-start.83 = (bf16[256,768]{1,0:T(8,128)(2,1)}, bf16[256,768]{1,0:T(8,128)(2,1)}, u32[]{:S(2)}, u32[]{:S(2)}) collective-permute-start(bf16[256,768]{1,0:T(8,128)(2,1)} %get-tuple-element.389), channel_id=1, source_target_pairs={{0,96},{4,28},{8,104},{12,4},{16,112},{20,12},{24,120},{28,20},{32... | collective-permute-start | bytes 1179656 | tf_op jit(solution)/shard_map/ppermute | solution.py:167
  (169 other events, 2045.3 us)
